TPU v7x, 32 devices: a whole 2x2x4 slice. The times are simulated.
32 devices in a mesh: group: 4 (over z), dev: 8 (over y, x, core).
Axes of the slice: x: 2, y: 2, z: 4, core: 2. Of those that a mesh axis runs over, the one named last changes fastest.
Arguments:
- density: float32 [16, 64, 128], P('dev', 'group'), may hold values from 0.9 to 1.1
- velocity: float32 [3, 16, 64, 128], P(None, 'dev', 'group'), may hold values from -0.2 to 0.2
- basis: bfloat16 [32, 3, 8, 2048], P(None, None, 'dev', 'group'), may hold values from -0.02734375 to 0.02734375
- snap_steps: int32 [4], replicated, may hold values from 0 to 5
Outputs:
- populations: float32 [19, 16, 64, 128], P(None, 'dev', 'group')
- coefficients: float32 [32, 4], replicated
- r_factor: float32 [4, 4], replicated
- new_modes: float32 [4, 3, 8, 2048], P(None, None, 'dev', 'group')
All inputs are finite; a program needn't handle non-finite values.
Results may differ from a plain program's by a relative error of at most 0.0003.
Values sent between devices are 32-bit elements; how exact they have to be, the bound alone decides.
No kernel may reach another device: no remote copies, remote signals or barrier semaphores. Data moves between devices by JAX's collectives and lax.ppermute only.
A program may use at most 64 MiB of HBM per device.

v0:
```python
import functools
import math

import jax
import jax.numpy as jnp
from jax import lax
from jax.experimental import pallas as pl
from jax.experimental.pallas import tpu as pltpu
from jax.sharding import PartitionSpec as P

STEPS = 6
DIRS = 19
DIR_X = [0, 1, -1, 0, 0, 0, 0, 1, -1, 1, -1, 1, -1, 1, -1, 0, 0, 0, 0]
DIR_Y = [0, 0, 0, 1, -1, 0, 0, 1, 1, -1, -1, 0, 0, 0, 0, 1, -1, 1, -1]
DIR_Z = [0, 0, 0, 0, 0, 1, -1, 0, 0, 0, 0, 1, 1, -1, -1, 1, 1, -1, -1]
OPPOSITE = [(1, 2), (3, 4), (5, 6), (7, 10), (8, 9), (11, 14), (12, 13), (15, 18), (16, 17)]
OMEGA = 1.6
UNIT = 10.0
SUB = 8
LANES = 128
HALO = 8
HIGHEST = lax.Precision.HIGHEST
NT = (((1,), (1,)), ((), ()))
VMEM_LIMIT = 48 * 1024 * 1024


def along(direction, parts):
    total = None
    for sign, part in zip(direction, parts):
        if sign == 0:
            continue
        if total is None:
            total = part if sign > 0 else -part
        else:
            total = total + part if sign > 0 else total - part
    return total


def relaxed(rate, dens, flow, speed, pops):
    keep = 1.0 - rate
    twice = [2.0 * f for f in flow]
    squares = [t * s for t, s in zip(twice, speed)]
    base = (rate / 36.0) * dens - (squares[0] + squares[1] + squares[2]) * (1.0 / 6.0)
    base2 = 2.0 * base
    out = [None] * DIRS

    def put(i, value):
        out[i] = value if pops is None else keep * pops[i] + value

    put(0, 12.0 * base)
    for a, b in OPPOSITE:
        direction = (DIR_X[a], DIR_Y[a], DIR_Z[a])
        if a < 7:
            axis = [abs(d) for d in direction].index(1)
            even = base2 + squares[axis]
            odd = twice[axis]
        else:
            odd = along(direction, flow)
            even = base + odd * along(direction, speed)
        put(a, even + odd)
        put(b, even - odd)
    return out


def moments(pops):
    dens = pops[0]
    diff = {}
    for a, b in OPPOSITE:
        dens = dens + (pops[a] + pops[b])
        diff[a] = pops[a] - pops[b]
    mom = []
    for table in (DIR_X, DIR_Y, DIR_Z):
        total = None
        for a, _ in OPPOSITE:
            if table[a] == 0:
                continue
            if total is None:
                total = diff[a] if table[a] > 0 else -diff[a]
            else:
                total = total + diff[a] if table[a] > 0 else total - diff[a]
        mom.append(total)
    return dens, mom


def streamed(src, x, tiles, row):
    turned = {}

    def turn(i, t):
        if (i, t) not in turned:
            tile = src[i, x - DIR_X[i], pl.ds(SUB * t, SUB), :]
            turned[i, t] = pltpu.roll(tile, DIR_Y[i] % SUB, 0)
        return turned[i, t]

    def get(i, t):
        if DIR_Y[i] == 0:
            tile = src[i, x - DIR_X[i], pl.ds(SUB * t, SUB), :]
        elif DIR_Y[i] > 0:
            tile = jnp.where(row == 0, turn(i, max(t - 1, 0)), turn(i, t))
        else:
            tile = jnp.where(row == SUB - 1, turn(i, min(t + 1, tiles - 1)), turn(i, t))
        if DIR_Z[i] != 0:
            tile = pltpu.roll(tile, DIR_Z[i] % LANES, 1)
        return tile

    return get


def edges_kernel(dens, vel, top, bottom):
    rows = dens.shape[1]
    top[0] = dens[:, rows - HALO :, :]
    bottom[0] = dens[:, :HALO, :]
    for c in range(3):
        top[c + 1] = vel[c, :, rows - HALO :, :]
        bottom[c + 1] = vel[c, :, :HALO, :]


def widen_kernel(dens, vel, upper, lower, wide):
    rows = dens.shape[1]
    wide[:, :, :HALO, :] = upper[...]
    wide[:, :, HALO + rows :, :] = lower[...]
    wide[0, :, HALO : HALO + rows, :] = dens[...]
    for c in range(3):
        wide[c + 1, :, HALO : HALO + rows, :] = vel[c]


def lattice_kernel(
    place, snap_steps, b0, b1, b2, b3, b4, b5, b6, basis, pops, snaps, sums, fields, ping, pong, speeds, views, picked, gram
):
    blocks = (b0, b1, b2, b3, b4, b5, b6)
    _, planes, wide, lanes = b0.shape
    reach = STEPS
    span = planes + 2 * reach
    tiles = wide // SUB
    rows = wide - 2 * HALO
    count = snap_steps.shape[0]
    row = lax.broadcasted_iota(jnp.int32, (SUB, lanes), 0)
    for n, block in enumerate(blocks):
        start = place[n]
        for p in range(planes):
            fields[start + p] = block[:, p]

    def put_speed(x, t, speed):
        if HALO <= SUB * t < HALO + rows:
            for c in range(3):
                speeds[x, c, pl.ds(SUB * t - HALO, SUB), :] = speed[c]

    def keep_view(step):
        for c in range(3):
            total = speeds[reach, c]
            for p in range(1, planes):
                total = total + speeds[reach + p, c]
            views[step, c] = total

    def first(x, carry):
        for t in range(tiles):
            at = pl.ds(SUB * t, SUB)
            dens = fields[x, 0, at, :]
            vel = [fields[x, c + 1, at, :] for c in range(3)]
            part = dens * (3.0 / 36.0)
            speed = [1.5 * v for v in vel]
            out = relaxed(1.0, dens, [part * v for v in vel], speed, None)
            for i in range(DIRS):
                ping[i, x, at, :] = out[i]
            put_speed(x, t, speed)
        return carry

    lax.fori_loop(0, span, first, 0)
    keep_view(0)

    src, dst = ping, pong
    for step in range(1, STEPS):

        def later(x, carry, src=src, dst=dst):
            get = streamed(src, x, tiles, row)
            for t in range(tiles):
                pop = [get(i, t) for i in range(DIRS)]
                dens, mom = moments(pop)
                inverse = 1.5 / dens
                speed = [m * inverse for m in mom]
                flow = [m * (OMEGA * 3.0 / 36.0) for m in mom]
                out = relaxed(OMEGA, dens, flow, speed, pop)
                for i in range(DIRS):
                    dst[i, x, pl.ds(SUB * t, SUB), :] = out[i]
                put_speed(x, t, speed)
            return carry

        lax.fori_loop(step, span - step, later, 0)
        keep_view(step)
        src, dst = dst, src

    for p in range(planes):
        get = streamed(src, reach + p, tiles, row)
        for t in range(HALO // SUB, (HALO + rows) // SUB):
            for i in range(DIRS):
                pops[i, p, pl.ds(SUB * t - HALO, SUB), :] = get(i, t)

    picked[...] = jnp.zeros_like(picked)
    for k in range(count):
        at_step = snap_steps[k]
        for c in range(3):
            picked[c, pl.ds(rows * k, rows), :] = views[at_step, c]
    groups = rows // 4
    lefts, rights = [], []
    for c in range(3):
        for t in range(groups):
            part = [picked[c, pl.ds(4 * t + j, SUB, stride=rows), :] for j in range(4)]
            lefts.append(part[0] + part[1])
            rights.append(part[2] + part[3])
    lane = lax.broadcasted_iota(jnp.int32, (lanes, lanes), 0) // 2
    col = lax.broadcasted_iota(jnp.int32, (lanes, lanes), 1)
    to_left = jnp.where(lane == col, 1.0, 0.0).astype(jnp.float32)
    to_right = jnp.where(lane + lanes // 2 == col, 1.0, 0.0).astype(jnp.float32)
    flat = jnp.dot(jnp.concatenate(lefts, axis=0), to_left, precision=HIGHEST, preferred_element_type=jnp.float32)
    flat = flat + jnp.dot(
        jnp.concatenate(rights, axis=0), to_right, precision=HIGHEST, preferred_element_type=jnp.float32
    )
    flat = flat * (UNIT / (4 * planes) / 1.5)
    rank = basis.shape[1]
    width = groups * lanes
    for c in range(3):
        for t in range(groups):
            n = c * groups + t
            snaps[c, :, pl.ds(lanes * t, lanes)] = flat[SUB * n : SUB * (n + 1), :]

    proj = jnp.zeros((SUB, rank), jnp.float32)
    inner = jnp.zeros((SUB, SUB), jnp.float32)
    modes2 = jnp.zeros((rank, rank), jnp.float32)
    for c in range(3):
        snap = snaps[c]
        mode = basis[c].astype(jnp.float32)
        proj += lax.dot_general(snap, mode, NT, precision=HIGHEST, preferred_element_type=jnp.float32)
        inner += lax.dot_general(snap, snap, NT, precision=HIGHEST, preferred_element_type=jnp.float32)
        modes2 += lax.dot_general(basis[c], basis[c], NT, preferred_element_type=jnp.float32)
    sums[...] = jnp.zeros_like(sums)
    gram[...] = jnp.zeros_like(gram)
    sums[0:SUB, 0:rank] = proj
    gram[0:rank, 0:rank] = modes2
    gram[rank : rank + SUB, 0:SUB] = inner
    sums[0:SUB, :] = sums[0:SUB, :] + pltpu.roll(gram[rank : rank + SUB, :], rank, 1)
    packed = gram[0:SUB, :]
    for j in range(1, rank // SUB):
        packed = packed + pltpu.roll(gram[SUB * j : SUB * (j + 1), :], rank * j, 1)
    sums[SUB : 2 * SUB, :] = packed


def finish_kernel(scale, count, rank, *refs):
    parts, (snaps, basis, coef, factor, modes, flag, gram) = refs[:-7], refs[-7:]
    total = tree_sum([part[...] for part in parts])
    lanes = total.shape[1]
    head = total[0:SUB, :]
    proj = head[:, 0:rank]
    inner = pltpu.roll(head, lanes - rank, 1)[:, 0:SUB]
    packed = total[SUB : 2 * SUB, :]
    for j in range(rank // SUB):
        gram[SUB * j : SUB * (j + 1), :] = packed if j == 0 else pltpu.roll(packed, lanes - rank * j, 1)
    modes2 = gram[:, 0:rank]
    dot = functools.partial(lax.dot_general, precision=HIGHEST, preferred_element_type=jnp.float32)
    turned = dot(proj, modes2, (((1,), (0,)), ((), ())))
    crossed = dot(proj, proj, NT)
    bent = dot(turned, proj, NT)
    small = inner - 2.0 * crossed + bent
    r = lax.broadcasted_iota(jnp.int32, (SUB, SUB), 0)
    c = lax.broadcasted_iota(jnp.int32, (SUB, SUB), 1)
    loss = jnp.where((r == c) & (r < count), inner + 2.0 * crossed + bent - 8.0 * small, -1.0)
    flag[0, 0] = jnp.max(jnp.where(loss < 0.0, 0.0, 1.0)).astype(jnp.int32)
    coef[...] = proj[0:count, :]
    resid = []
    for n in range(3):
        mode = basis[n].astype(jnp.float32)
        resid.append(snaps[n] - dot(proj, mode, (((1,), (0,)), ((), ()))))
    small = jnp.where((r < count) & (c < count), small, jnp.where(r == c, 1.0, 0.0))
    below = lax.broadcasted_iota(jnp.int32, (SUB, 1), 0)
    pivots = jnp.ones((SUB, 1), jnp.float32)
    for j in range(count):
        pivot = small[j : j + 1, j : j + 1]
        pivots = jnp.where(below == j, pivot, pivots)
        share = jnp.where(below > j, small[:, j : j + 1] / pivot, 0.0)
        resid = [v - share * v[j : j + 1, :] for v in resid]
        small = small - share * small[j : j + 1, :]
    root = jnp.sqrt(pivots)
    upper = jnp.where(c >= r, small / root, 0.0)
    factor[...] = upper[0:count, 0:count] * (1.0 / scale)
    gain = scale / root
    groups = snaps.shape[2] // lanes
    for n in range(3):
        value = resid[n] * gain
        for t in range(groups):
            modes[pl.ds(groups * n + t, count, stride=3 * groups), :] = value[0:count, lanes * t : lanes * (t + 1)]


def tree_sum(parts):
    parts = list(parts)
    while len(parts) > 1:
        parts = [a + b for a, b in zip(parts[::2], parts[1::2])] + ([parts[-1]] if len(parts) % 2 else [])
    return parts[0]


def moved(block, axis, target):
    return lax.ppermute(block, axis, [(i, target(i)) for i in range(lax.axis_size(axis))])


def partners(block, axis, stride, count):
    digit = lambda i: i // stride % count
    if count & (count - 1) == 0:
        return [block] + [
            moved(block, axis, lambda i, j=j: i + ((digit(i) ^ j) - digit(i)) * stride) for j in range(1, count)
        ]
    got = [block] + [
        moved(block, axis, lambda i, j=j: i + ((digit(i) + j) % count - digit(i)) * stride) for j in range(1, count)
    ]
    mine = lax.axis_index(axis) // stride % count
    return list(jnp.roll(jnp.stack(got)[::-1], mine + 1, axis=0))


def digits(size):
    found, rest = [], size
    for base in (8, 4, 2):
        while rest % base == 0:
            found.append(base)
            rest //= base
    base = 3
    while rest > 1:
        while rest % base == 0:
            found.append(base)
            rest //= base
        base += 2
    return found


def from_residuals(coefficients, snaps, basis, scale):
    modes = basis[:, :, 0, :].astype(jnp.float32)
    count = coefficients.shape[1]
    held = jnp.transpose(snaps[:, :count, :], (1, 0, 2))
    resid = held - jnp.einsum("rk,rab->kab", coefficients, modes, precision=HIGHEST)
    gram = lax.psum(jnp.einsum("kab,lab->kl", resid, resid, precision=HIGHEST), ("group", "dev"))
    lower = jnp.linalg.cholesky(gram)
    solved = []
    for k in range(count):
        value = resid[k]
        for j in range(k):
            value = value - lower[k, j] * solved[j]
        solved.append(value / lower[k, k])
    return lower.T / scale, (jnp.stack(solved) * scale).reshape(-1, LANES)


def per_device(density, velocity, basis, snap_steps):
    planes, rows, lanes = density.shape
    count = snap_steps.shape[0]
    rank = basis.shape[0]
    reach = STEPS
    n_dev, n_group = lax.axis_size("dev"), lax.axis_size("group")
    vmem = pl.BlockSpec(memory_space=pltpu.VMEM)
    smem = pl.BlockSpec(memory_space=pltpu.SMEM)
    f32 = jnp.float32
    params = pltpu.CompilerParams(vmem_limit_bytes=VMEM_LIMIT)

    edge = jax.ShapeDtypeStruct((4, planes, HALO, lanes), f32)
    top, bottom = pl.pallas_call(
        edges_kernel, out_shape=(edge, edge), in_specs=[vmem] * 2, out_specs=(vmem, vmem), compiler_params=params
    )(density, velocity)
    upper = moved(top, "group", lambda i: (i + 1) % n_group)
    lower = moved(bottom, "group", lambda i: (i - 1) % n_group)
    wide_rows = rows + 2 * HALO
    own = pl.pallas_call(
        widen_kernel,
        out_shape=jax.ShapeDtypeStruct((4, planes, wide_rows, lanes), f32),
        in_specs=[vmem] * 4,
        out_specs=vmem,
        compiler_params=params,
    )(density, velocity, upper, lower)

    ahead = moved(own, "dev", lambda i: (i - 2) % n_dev)
    behind = moved(own, "dev", lambda i: (i + 2) % n_dev)
    far = moved(own, "dev", lambda i: (i + 3 if i % 2 else i - 3) % n_dev)
    other = moved(own, "dev", lambda i: i ^ 1)
    other_ahead = moved(ahead, "dev", lambda i: i ^ 1)
    other_behind = moved(behind, "dev", lambda i: i ^ 1)
    odd = lax.axis_index("dev") % 2
    offsets = jnp.where(
        odd == 1, jnp.array([0, 2, -2, 3, -1, 1, -3], jnp.int32), jnp.array([0, 2, -2, -3, 1, 3, -1], jnp.int32)
    )
    place = reach + planes * offsets
    modes = jnp.transpose(basis[:, :, 0, :], (1, 0, 2))
    span = planes + 2 * reach
    width = basis.shape[3]
    pops, snaps, sums = pl.pallas_call(
        lattice_kernel,
        out_shape=(
            jax.ShapeDtypeStruct((DIRS, planes, rows, lanes), f32),
            jax.ShapeDtypeStruct((3, SUB, width), f32),
            jax.ShapeDtypeStruct((2 * SUB, lanes), f32),
        ),
        in_specs=[smem, smem] + [vmem] * 8,
        out_specs=(vmem, vmem, vmem),
        scratch_shapes=[
            pltpu.VMEM((span, 4, wide_rows, lanes), f32),
            pltpu.VMEM((DIRS, span, wide_rows, lanes), f32),
            pltpu.VMEM((DIRS, span, wide_rows, lanes), f32),
            pltpu.VMEM((span, 3, rows, lanes), f32),
            pltpu.VMEM((STEPS, 3, rows, lanes), f32),
            pltpu.VMEM((3, SUB * rows, lanes), f32),
            pltpu.VMEM((rank + SUB, lanes), f32),
        ],
        compiler_params=params,
    )(place, snap_steps, own, ahead, behind, far, other, other_ahead, other_behind, modes)

    rounds = []
    for axis, size in (("dev", n_dev), ("group", n_group)):
        stride = 1
        for base in digits(size):
            rounds.append((axis, stride, base))
            stride *= base
    parts = [sums]
    for axis, stride, base in rounds:
        parts = partners(tree_sum(parts), axis, stride, base)
    scale = math.sqrt(3 * width * n_dev * n_group)
    coef, factor, new_modes, flag = pl.pallas_call(
        functools.partial(finish_kernel, scale, count, rank),
        out_shape=(
            jax.ShapeDtypeStruct((count, rank), f32),
            jax.ShapeDtypeStruct((count, count), f32),
            jax.ShapeDtypeStruct((count * 3 * width // lanes, lanes), f32),
            jax.ShapeDtypeStruct((1, 1), jnp.int32),
        ),
        in_specs=[vmem] * (len(parts) + 2),
        out_specs=(vmem, vmem, vmem, smem),
        scratch_shapes=[pltpu.VMEM((rank, lanes), f32)],
        compiler_params=params,
    )(*parts, snaps, modes)
    coefficients = coef.T
    factor, new_modes = lax.cond(
        flag[0, 0] != 0,
        lambda: from_residuals(coefficients, snaps, basis, scale),
        lambda: (factor, new_modes),
    )
    return (pops, coefficients, factor, new_modes.reshape(count, 3, 1, width))


def solution(mesh):
    placed = (
        P("dev", "group", None),
        P(None, "dev", "group", None),
        P(None, None, "dev", "group"),
        P(),
    )
    return jax.shard_map(
        per_device,
        mesh=mesh,
        in_specs=placed,
        out_specs=(P(None, "dev", "group", None), P(), P(), P(None, None, "dev", "group")),
        check_vma=False,
    )
```

profile of v0, /device:TPU:0, one launch (start us, length us, event | category | flops | bytes accessed | tf_op | source)
XLA Modules:
  0.0 49.1 jit_solution(12238086356931992981)
XLA Ops:
  0.6 0.8 %copy-done = f32[3,2,16,128]{3,2,1,0:T(8,128)S(1)} copy-done((f32[3,2,16,128]{3,2,1,0:T(8,128)S(1)}, f32[3,2,16,128]{3,2,1,0:T(8,128)}, u32[]{:S(2)}) %copy-start) | copy-done | bytes 49176
  1.4 0.7 %copy-done.1 = f32[2,16,128]{2,1,0:T(8,128)S(1)} copy-done((f32[2,16,128]{2,1,0:T(8,128)S(1)}, f32[2,16,128]{2,1,0:T(8,128)}, u32[]{:S(2)}) %copy-start.1) | copy-done | bytes 16408
  2.2 3.0 %collective-permute-start = (f32[4,2,8,128]{3,2,1,0:T(8,128)S(1)}, f32[4,2,8,128]{3,2,1,0:T(8,128)S(1)}, u32[]{:S(2)}, u32[]{:S(2)}) collective-permute-start(f32[4,2,8,128]{3,2,1,0:T(8,128)S(1)} %get-tuple-element.33), channel_id=1, source_target_pairs={{0,8},{8,16},{16,24},{24,0},{1,9},{9,17},{17,25},{25,1},{2,10},{10... | collective-permute-start | bytes 98312 | tf_op jit(solution)/shard_map/ppermute | solution.py:299
  5.2 2.1 %collective-permute-start.1 = (f32[4,2,8,128]{3,2,1,0:T(8,128)S(1)}, f32[4,2,8,128]{3,2,1,0:T(8,128)S(1)}, u32[]{:S(2)}, u32[]{:S(2)}) collective-permute-start(f32[4,2,8,128]{3,2,1,0:T(8,128)S(1)} %get-tuple-element.34), channel_id=1, source_target_pairs={{0,24},{8,0},{16,8},{24,16},{1,25},{9,1},{17,9},{25,17},{2,26},{10... | collective-permute-start | bytes 98312 | tf_op jit(solution)/shard_map/ppermute | solution.py:299
  7.3 1.9 %collective-permute-done.upper = f32[4,2,8,128]{3,2,1,0:T(8,128)S(1)} collective-permute-done((f32[4,2,8,128]{3,2,1,0:T(8,128)S(1)}, f32[4,2,8,128]{3,2,1,0:T(8,128)S(1)}, u32[]{:S(2)}, u32[]{:S(2)}) %collective-permute-start) | collective-permute-done | bytes 32800 | tf_op jit(solution)/shard_map/ppermute | solution.py:299
  9.1 0.3 collective-permute-done.1.lower
  9.5 1.5 %collective-permute-start.3 = (f32[4,2,32,128]{3,2,1,0:T(8,128)S(1)}, f32[4,2,32,128]{3,2,1,0:T(8,128)S(1)}, u32[]{:S(2)}, u32[]{:S(2)}) collective-permute-start(f32[4,2,32,128]{3,2,1,0:T(8,128)S(1)} %shard_map.94.b0), channel_id=1, source_target_pairs={{0,2},{1,3},{2,4},{3,5},{4,6},{5,7},{6,0},{7,1},{8,10},{9,11},{10,... | collective-permute-start | bytes 393224 | tf_op jit(solution)/shard_map/ppermute | solution.py:299
  11.0 1.4 %collective-permute-start.2 = (f32[4,2,32,128]{3,2,1,0:T(8,128)S(1)}, f32[4,2,32,128]{3,2,1,0:T(8,128)S(1)}, u32[]{:S(2)}, u32[]{:S(2)}) collective-permute-start(f32[4,2,32,128]{3,2,1,0:T(8,128)S(1)} %shard_map.94.b0), channel_id=1, source_target_pairs={{0,6},{1,7},{2,0},{3,1},{4,2},{5,3},{6,4},{7,5},{8,14},{9,15},{10,... | collective-permute-start | bytes 393224 | tf_op jit(solution)/shard_map/ppermute | solution.py:299
  12.4 1.6 %collective-permute-start.4 = (f32[4,2,32,128]{3,2,1,0:T(8,128)S(1)}, f32[4,2,32,128]{3,2,1,0:T(8,128)S(1)}, u32[]{:S(2)}, u32[]{:S(2)}) collective-permute-start(f32[4,2,32,128]{3,2,1,0:T(8,128)S(1)} %shard_map.94.b0), channel_id=1, source_target_pairs={{0,5},{1,4},{2,7},{3,6},{4,1},{5,0},{6,3},{7,2},{8,13},{9,12},{10,... | collective-permute-start | bytes 393224 | tf_op jit(solution)/shard_map/ppermute | solution.py:299
  14.1 1.8 %collective-permute-done.3.b2 = f32[4,2,32,128]{3,2,1,0:T(8,128)S(1)} collective-permute-done((f32[4,2,32,128]{3,2,1,0:T(8,128)S(1)}, f32[4,2,32,128]{3,2,1,0:T(8,128)S(1)}, u32[]{:S(2)}, u32[]{:S(2)}) %collective-permute-start.3) | collective-permute-done | bytes 131104 | tf_op jit(solution)/shard_map/ppermute | solution.py:299
  15.9 1.4 %collective-permute-done.2.b1 = f32[4,2,32,128]{3,2,1,0:T(8,128)S(1)} collective-permute-done((f32[4,2,32,128]{3,2,1,0:T(8,128)S(1)}, f32[4,2,32,128]{3,2,1,0:T(8,128)S(1)}, u32[]{:S(2)}, u32[]{:S(2)}) %collective-permute-start.2) | collective-permute-done | bytes 131104 | tf_op jit(solution)/shard_map/ppermute | solution.py:299
  17.3 0.0 copy-start.2
  17.3 1.0 %collective-permute-done.4.b3 = f32[4,2,32,128]{3,2,1,0:T(8,128)S(1)} collective-permute-done((f32[4,2,32,128]{3,2,1,0:T(8,128)S(1)}, f32[4,2,32,128]{3,2,1,0:T(8,128)S(1)}, u32[]{:S(2)}, u32[]{:S(2)}) %collective-permute-start.4) | collective-permute-done | bytes 131104 | tf_op jit(solution)/shard_map/ppermute | solution.py:299
  18.4 0.3 collective-permute-done.6.b5
  18.7 10.3 %shard_map.95 = (f32[19,2,16,128]{3,2,1,0:T(8,128)}, f32[3,8,512]{2,1,0:T(8,128)S(1)}, f32[16,128]{1,0:T(8,128)S(1)}) custom-call(s32[7]{0:T(128)S(1)} %fusion.9.place, s32[4]{0:T(128)S(1)} %copy-done.2, f32[4,2,32,128]{3,2,1,0:T(8,128)S(1)} %shard_map.94.b0, f32[4,2,32,128]{3,2,1,0:T(8,128)S(1)} %collective-permute-done.2.b1, ...), custom_call_target="tpu_custom_call" | custom-call | tf_op jit(solution)/shard_map/pallas_call | solution.py:386
  28.9 2.0 %collective-permute-start.14 = (f32[16,128]{1,0:T(8,128)S(1)}, f32[16,128]{1,0:T(8,128)S(1)}, u32[]{:S(2)}, u32[]{:S(2)}) collective-permute-start(f32[16,128]{1,0:T(8,128)S(1)} %get-tuple-element.36), channel_id=1, source_target_pairs={{0,7},{1,6},{2,5},{3,4},{4,3},{5,2},{6,1},{7,0},{8,15},{9,14},{10,... | collective-permute-start | bytes 24584 | tf_op jit(solution)/shard_map/ppermute | solution.py:299
  30.9 0.7 %collective-permute-start.13 = (f32[16,128]{1,0:T(8,128)S(1)}, f32[16,128]{1,0:T(8,128)S(1)}, u32[]{:S(2)}, u32[]{:S(2)}) collective-permute-start(f32[16,128]{1,0:T(8,128)S(1)} %get-tuple-element.36), channel_id=1, source_target_pairs={{0,6},{1,7},{2,4},{3,5},{4,2},{5,3},{6,0},{7,1},{8,14},{9,15},{10,... | collective-permute-start | bytes 24584 | tf_op jit(solution)/shard_map/ppermute | solution.py:299
  31.6 1.0 %collective-permute-start.12 = (f32[16,128]{1,0:T(8,128)S(1)}, f32[16,128]{1,0:T(8,128)S(1)}, u32[]{:S(2)}, u32[]{:S(2)}) collective-permute-start(f32[16,128]{1,0:T(8,128)S(1)} %get-tuple-element.36), channel_id=1, source_target_pairs={{0,5},{1,4},{2,7},{3,6},{4,1},{5,0},{6,3},{7,2},{8,13},{9,12},{10,... | collective-permute-start | bytes 24584 | tf_op jit(solution)/shard_map/ppermute | solution.py:299
  32.6 0.7 %collective-permute-start.11 = (f32[16,128]{1,0:T(8,128)S(1)}, f32[16,128]{1,0:T(8,128)S(1)}, u32[]{:S(2)}, u32[]{:S(2)}) collective-permute-start(f32[16,128]{1,0:T(8,128)S(1)} %get-tuple-element.36), channel_id=1, source_target_pairs={{0,4},{1,5},{2,6},{3,7},{4,0},{5,1},{6,2},{7,3},{8,12},{9,13},{10,... | collective-permute-start | bytes 24584 | tf_op jit(solution)/shard_map/ppermute | solution.py:299
  33.3 1.4 %collective-permute-start.10 = (f32[16,128]{1,0:T(8,128)S(1)}, f32[16,128]{1,0:T(8,128)S(1)}, u32[]{:S(2)}, u32[]{:S(2)}) collective-permute-start(f32[16,128]{1,0:T(8,128)S(1)} %get-tuple-element.36), channel_id=1, source_target_pairs={{0,3},{1,2},{2,1},{3,0},{4,7},{5,6},{6,5},{7,4},{8,11},{9,10},{10,... | collective-permute-start | bytes 24584 | tf_op jit(solution)/shard_map/ppermute | solution.py:299
  34.7 0.4 collective-permute-start.9
  35.1 0.4 collective-permute-done.13
  35.5 0.8 %collective-permute-done.11 = f32[16,128]{1,0:T(8,128)S(1)} collective-permute-done((f32[16,128]{1,0:T(8,128)S(1)}, f32[16,128]{1,0:T(8,128)S(1)}, u32[]{:S(2)}, u32[]{:S(2)}) %collective-permute-start.11) | collective-permute-done | bytes 8224 | tf_op jit(solution)/shard_map/ppermute | solution.py:299
  36.2 0.2 collective-permute-done.10
  36.4 1.9 %collective-permute-done.9 = f32[16,128]{1,0:T(8,128)S(1)} collective-permute-done((f32[16,128]{1,0:T(8,128)S(1)}, f32[16,128]{1,0:T(8,128)S(1)}, u32[]{:S(2)}, u32[]{:S(2)}) %collective-permute-start.9) | collective-permute-done | bytes 8224 | tf_op jit(solution)/shard_map/ppermute | solution.py:299
  38.4 3.7 %collective-permute-start.17 = (f32[16,128]{1,0:T(8,128)S(1)}, f32[16,128]{1,0:T(8,128)S(1)}, u32[]{:S(2)}, u32[]{:S(2)}) collective-permute-start(f32[16,128]{1,0:T(8,128)S(1)} %add_add_fusion.refs_0_), channel_id=1, source_target_pairs={{0,24},{8,16},{16,8},{24,0},{1,25},{9,17},{17,9},{25,1},{2,26},{10... | collective-permute-start | bytes 24584 | tf_op jit(solution)/shard_map/ppermute | solution.py:299
  42.0 0.8 %collective-permute-start.15 = (f32[16,128]{1,0:T(8,128)S(1)}, f32[16,128]{1,0:T(8,128)S(1)}, u32[]{:S(2)}, u32[]{:S(2)}) collective-permute-start(f32[16,128]{1,0:T(8,128)S(1)} %add_add_fusion.refs_0_), channel_id=1, source_target_pairs={{0,8},{8,0},{16,24},{24,16},{1,9},{9,1},{17,25},{25,17},{2,10},{10... | collective-permute-start | bytes 24584 | tf_op jit(solution)/shard_map/ppermute | solution.py:299
  42.8 1.1 %collective-permute-done.17.refs_3_ = f32[16,128]{1,0:T(8,128)S(1)} collective-permute-done((f32[16,128]{1,0:T(8,128)S(1)}, f32[16,128]{1,0:T(8,128)S(1)}, u32[]{:S(2)}, u32[]{:S(2)}) %collective-permute-start.17) | collective-permute-done | bytes 8224 | tf_op jit(solution)/shard_map/ppermute | solution.py:299
  43.9 2.7 %collective-permute-done.16.refs_2_ = f32[16,128]{1,0:T(8,128)S(1)} collective-permute-done((f32[16,128]{1,0:T(8,128)S(1)}, f32[16,128]{1,0:T(8,128)S(1)}, u32[]{:S(2)}, u32[]{:S(2)}) %collective-permute-start.16) | collective-permute-done | bytes 8224 | tf_op jit(solution)/shard_map/ppermute | solution.py:299
  46.6 1.2 %shard_map.96 = (f32[4,32]{1,0:T(4,128)S(1)}, f32[4,4]{1,0:T(4,128)S(1)}, f32[48,128]{1,0:T(8,128)S(1)}, s32[1,1]{1,0:T(1,128)}) custom-call(f32[16,128]{1,0:T(8,128)S(1)} %add_add_fusion.refs_0_, f32[16,128]{1,0:T(8,128)S(1)} %collective-permute-done.15.refs_1_, f32[16,128]{1,0:T(8,128)S(1)} %collective-permute-done.16.refs_2_, ...), custom_call_target="tpu_custom_call" | custom-call | tf_op jit(solution)/shard_map/pallas_call | solution.py:417
  47.8 0.0 copy-start.4
  48.5 0.6 %copy-done.7 = f32[4,3,1,512]{3,2,1,0:T(1,128)} copy-done((f32[4,3,1,512]{3,2,1,0:T(1,128)}, f32[4,3,1,512]{3,2,1,0:T(1,128)S(1)}, u32[]{:S(2)}) %copy-start.7) | copy-done | bytes 24600
  (29 shorter events, 0.1 us)
Async XLA Ops:
  0.6 0.8 %copy-start = (f32[3,2,16,128]{3,2,1,0:T(8,128)S(1)}, f32[3,2,16,128]{3,2,1,0:T(8,128)}, u32[]{:S(2)}) copy-start(f32[3,2,16,128]{3,2,1,0:T(8,128)} %vel.3) | copy-start | bytes 147460
  1.4 0.7 %copy-start.1 = (f32[2,16,128]{2,1,0:T(8,128)S(1)}, f32[2,16,128]{2,1,0:T(8,128)}, u32[]{:S(2)}) copy-start(f32[2,16,128]{2,1,0:T(8,128)} %dens.3) | copy-start | bytes 49156
  2.2 7.0 %collective-permute-start = (f32[4,2,8,128]{3,2,1,0:T(8,128)S(1)}, f32[4,2,8,128]{3,2,1,0:T(8,128)S(1)}, u32[]{:S(2)}, u32[]{:S(2)}) collective-permute-start(f32[4,2,8,128]{3,2,1,0:T(8,128)S(1)} %get-tuple-element.33), channel_id=1, source_target_pairs={{0,8},{8,16},{16,24},{24,0},{1,9},{9,17},{17,25},{25,1},{2,10},{10... | collective-permute-start | bytes 98312 | tf_op jit(solution)/shard_map/ppermute | solution.py:299
  5.2 13.5 %copy-start.3 = (bf16[32,3,1,512]{3,0,2,1:T(8,128)(2,1)S(1)}, bf16[32,3,1,512]{3,0,2,1:T(8,128)(2,1)}, u32[]{:S(2)}) copy-start(bf16[32,3,1,512]{3,0,2,1:T(8,128)(2,1)} %param.10) | copy-start | bytes 294916
  5.2 4.3 %collective-permute-start.1 = (f32[4,2,8,128]{3,2,1,0:T(8,128)S(1)}, f32[4,2,8,128]{3,2,1,0:T(8,128)S(1)}, u32[]{:S(2)}, u32[]{:S(2)}) collective-permute-start(f32[4,2,8,128]{3,2,1,0:T(8,128)S(1)} %get-tuple-element.34), channel_id=1, source_target_pairs={{0,24},{8,0},{16,8},{24,16},{1,25},{9,1},{17,9},{25,17},{2,26},{10... | collective-permute-start | bytes 98312 | tf_op jit(solution)/shard_map/ppermute | solution.py:299
  9.5 6.4 %collective-permute-start.3 = (f32[4,2,32,128]{3,2,1,0:T(8,128)S(1)}, f32[4,2,32,128]{3,2,1,0:T(8,128)S(1)}, u32[]{:S(2)}, u32[]{:S(2)}) collective-permute-start(f32[4,2,32,128]{3,2,1,0:T(8,128)S(1)} %shard_map.94.b0), channel_id=1, source_target_pairs={{0,2},{1,3},{2,4},{3,5},{4,6},{5,7},{6,0},{7,1},{8,10},{9,11},{10,... | collective-permute-start | bytes 393224 | tf_op jit(solution)/shard_map/ppermute | solution.py:299
  11.0 6.3 %collective-permute-start.2 = (f32[4,2,32,128]{3,2,1,0:T(8,128)S(1)}, f32[4,2,32,128]{3,2,1,0:T(8,128)S(1)}, u32[]{:S(2)}, u32[]{:S(2)}) collective-permute-start(f32[4,2,32,128]{3,2,1,0:T(8,128)S(1)} %shard_map.94.b0), channel_id=1, source_target_pairs={{0,6},{1,7},{2,0},{3,1},{4,2},{5,3},{6,4},{7,5},{8,14},{9,15},{10,... | collective-permute-start | bytes 393224 | tf_op jit(solution)/shard_map/ppermute | solution.py:299
  12.4 4.9 %copy-start.5 = (s32[7]{0:T(128)S(1)}, s32[7]{0:T(128)}, u32[]{:S(2)}) copy-start(s32[7]{0:T(128)} %constant.71.clone) | copy-start | bytes 88
  12.4 4.9 %copy-start.6 = (s32[7]{0:T(128)S(1)}, s32[7]{0:T(128)}, u32[]{:S(2)}) copy-start(s32[7]{0:T(128)} %constant.70.clone) | copy-start | bytes 88
  12.4 4.9 %collective-permute-start.5 = (f32[4,2,32,128]{3,2,1,0:T(8,128)S(1)}, f32[4,2,32,128]{3,2,1,0:T(8,128)S(1)}, u32[]{:S(2)}, u32[]{:S(2)}) collective-permute-start(f32[4,2,32,128]{3,2,1,0:T(8,128)S(1)} %shard_map.94.b0), channel_id=1, source_target_pairs={{0,1},{1,0},{2,3},{3,2},{4,5},{5,4},{6,7},{7,6},{8,9},{9,8},{10,11... | collective-permute-start | bytes 393224 | tf_op jit(solution)/shard_map/ppermute | solution.py:299
  12.4 5.9 %collective-permute-start.4 = (f32[4,2,32,128]{3,2,1,0:T(8,128)S(1)}, f32[4,2,32,128]{3,2,1,0:T(8,128)S(1)}, u32[]{:S(2)}, u32[]{:S(2)}) collective-permute-start(f32[4,2,32,128]{3,2,1,0:T(8,128)S(1)} %shard_map.94.b0), channel_id=1, source_target_pairs={{0,5},{1,4},{2,7},{3,6},{4,1},{5,0},{6,3},{7,2},{8,13},{9,12},{10,... | collective-permute-start | bytes 393224 | tf_op jit(solution)/shard_map/ppermute | solution.py:299
  15.9 2.5 %collective-permute-start.7 = (f32[4,2,32,128]{3,2,1,0:T(8,128)S(1)}, f32[4,2,32,128]{3,2,1,0:T(8,128)S(1)}, u32[]{:S(2)}, u32[]{:S(2)}) collective-permute-start(f32[4,2,32,128]{3,2,1,0:T(8,128)S(1)} %collective-permute-done.3.b2), channel_id=1, source_target_pairs={{0,1},{1,0},{2,3},{3,2},{4,5},{5,4},{6,7},{7,6},{8,9},{9,8},{10,11... | collective-permute-start | bytes 393224 | tf_op jit(solution)/shard_map/ppermute | solution.py:299
  17.3 1.3 %collective-permute-start.6 = (f32[4,2,32,128]{3,2,1,0:T(8,128)S(1)}, f32[4,2,32,128]{3,2,1,0:T(8,128)S(1)}, u32[]{:S(2)}, u32[]{:S(2)}) collective-permute-start(f32[4,2,32,128]{3,2,1,0:T(8,128)S(1)} %collective-permute-done.2.b1), channel_id=1, source_target_pairs={{0,1},{1,0},{2,3},{3,2},{4,5},{5,4},{6,7},{7,6},{8,9},{9,8},{10,11... | collective-permute-start | bytes 393224 | tf_op jit(solution)/shard_map/ppermute | solution.py:299
  17.3 1.3 %copy-start.2 = (s32[4]{0:T(128)S(1)}, s32[4]{0:T(128)}, u32[]{:S(2)}) copy-start(s32[4]{0:T(128)} %snap_steps.1) | copy-start | bytes 52
  28.9 5.8 %collective-permute-start.14 = (f32[16,128]{1,0:T(8,128)S(1)}, f32[16,128]{1,0:T(8,128)S(1)}, u32[]{:S(2)}, u32[]{:S(2)}) collective-permute-start(f32[16,128]{1,0:T(8,128)S(1)} %get-tuple-element.36), channel_id=1, source_target_pairs={{0,7},{1,6},{2,5},{3,4},{4,3},{5,2},{6,1},{7,0},{8,15},{9,14},{10,... | collective-permute-start | bytes 24584 | tf_op jit(solution)/shard_map/ppermute | solution.py:299
  30.9 4.5 %collective-permute-start.13 = (f32[16,128]{1,0:T(8,128)S(1)}, f32[16,128]{1,0:T(8,128)S(1)}, u32[]{:S(2)}, u32[]{:S(2)}) collective-permute-start(f32[16,128]{1,0:T(8,128)S(1)} %get-tuple-element.36), channel_id=1, source_target_pairs={{0,6},{1,7},{2,4},{3,5},{4,2},{5,3},{6,0},{7,1},{8,14},{9,15},{10,... | collective-permute-start | bytes 24584 | tf_op jit(solution)/shard_map/ppermute | solution.py:299
  31.6 3.9 %collective-permute-start.12 = (f32[16,128]{1,0:T(8,128)S(1)}, f32[16,128]{1,0:T(8,128)S(1)}, u32[]{:S(2)}, u32[]{:S(2)}) collective-permute-start(f32[16,128]{1,0:T(8,128)S(1)} %get-tuple-element.36), channel_id=1, source_target_pairs={{0,5},{1,4},{2,7},{3,6},{4,1},{5,0},{6,3},{7,2},{8,13},{9,12},{10,... | collective-permute-start | bytes 24584 | tf_op jit(solution)/shard_map/ppermute | solution.py:299
  32.6 3.7 %collective-permute-start.11 = (f32[16,128]{1,0:T(8,128)S(1)}, f32[16,128]{1,0:T(8,128)S(1)}, u32[]{:S(2)}, u32[]{:S(2)}) collective-permute-start(f32[16,128]{1,0:T(8,128)S(1)} %get-tuple-element.36), channel_id=1, source_target_pairs={{0,4},{1,5},{2,6},{3,7},{4,0},{5,1},{6,2},{7,3},{8,12},{9,13},{10,... | collective-permute-start | bytes 24584 | tf_op jit(solution)/shard_map/ppermute | solution.py:299
  33.3 3.1 %collective-permute-start.10 = (f32[16,128]{1,0:T(8,128)S(1)}, f32[16,128]{1,0:T(8,128)S(1)}, u32[]{:S(2)}, u32[]{:S(2)}) collective-permute-start(f32[16,128]{1,0:T(8,128)S(1)} %get-tuple-element.36), channel_id=1, source_target_pairs={{0,3},{1,2},{2,1},{3,0},{4,7},{5,6},{6,5},{7,4},{8,11},{9,10},{10,... | collective-permute-start | bytes 24584 | tf_op jit(solution)/shard_map/ppermute | solution.py:299
  34.7 3.7 %collective-permute-start.9 = (f32[16,128]{1,0:T(8,128)S(1)}, f32[16,128]{1,0:T(8,128)S(1)}, u32[]{:S(2)}, u32[]{:S(2)}) collective-permute-start(f32[16,128]{1,0:T(8,128)S(1)} %get-tuple-element.36), channel_id=1, source_target_pairs={{0,2},{1,3},{2,0},{3,1},{4,6},{5,7},{6,4},{7,5},{8,10},{9,11},{10,... | collective-permute-start | bytes 24584 | tf_op jit(solution)/shard_map/ppermute | solution.py:299
  35.5 2.9 %collective-permute-start.8 = (f32[16,128]{1,0:T(8,128)S(1)}, f32[16,128]{1,0:T(8,128)S(1)}, u32[]{:S(2)}, u32[]{:S(2)}) collective-permute-start(f32[16,128]{1,0:T(8,128)S(1)} %get-tuple-element.36), channel_id=1, source_target_pairs={{0,1},{1,0},{2,3},{3,2},{4,5},{5,4},{6,7},{7,6},{8,9},{9,8},{10,11... | collective-permute-start | bytes 24584 | tf_op jit(solution)/shard_map/ppermute | solution.py:299
  38.4 5.5 %collective-permute-start.17 = (f32[16,128]{1,0:T(8,128)S(1)}, f32[16,128]{1,0:T(8,128)S(1)}, u32[]{:S(2)}, u32[]{:S(2)}) collective-permute-start(f32[16,128]{1,0:T(8,128)S(1)} %add_add_fusion.refs_0_), channel_id=1, source_target_pairs={{0,24},{8,16},{16,8},{24,0},{1,25},{9,17},{17,9},{25,1},{2,26},{10... | collective-permute-start | bytes 24584 | tf_op jit(solution)/shard_map/ppermute | solution.py:299
  42.0 4.5 %collective-permute-start.16 = (f32[16,128]{1,0:T(8,128)S(1)}, f32[16,128]{1,0:T(8,128)S(1)}, u32[]{:S(2)}, u32[]{:S(2)}) collective-permute-start(f32[16,128]{1,0:T(8,128)S(1)} %add_add_fusion.refs_0_), channel_id=1, source_target_pairs={{0,16},{8,24},{16,0},{24,8},{1,17},{9,25},{17,1},{25,9},{2,18},{10... | collective-permute-start | bytes 24584 | tf_op jit(solution)/shard_map/ppermute | solution.py:299
  42.0 4.5 %collective-permute-start.15 = (f32[16,128]{1,0:T(8,128)S(1)}, f32[16,128]{1,0:T(8,128)S(1)}, u32[]{:S(2)}, u32[]{:S(2)}) collective-permute-start(f32[16,128]{1,0:T(8,128)S(1)} %add_add_fusion.refs_0_), channel_id=1, source_target_pairs={{0,8},{8,0},{16,24},{24,16},{1,9},{9,1},{17,25},{25,17},{2,10},{10... | collective-permute-start | bytes 24584 | tf_op jit(solution)/shard_map/ppermute | solution.py:299
  47.8 0.7 %copy-start.4 = (f32[4,32]{1,0:T(4,128)}, f32[4,32]{1,0:T(4,128)S(1)}, u32[]{:S(2)}) copy-start(f32[4,32]{1,0:T(4,128)S(1)} %get-tuple-element.38) | copy-start | bytes 1540
  48.5 0.6 %copy-start.7 = (f32[4,3,1,512]{3,2,1,0:T(1,128)}, f32[4,3,1,512]{3,2,1,0:T(1,128)S(1)}, u32[]{:S(2)}) copy-start(f32[4,3,1,512]{3,2,1,0:T(1,128)S(1)} %get-tuple-element.65) | copy-start | bytes 73732
  48.5 0.6 %copy-start.8 = (f32[4,4]{1,0:T(4,128)}, f32[4,4]{1,0:T(4,128)S(1)}, u32[]{:S(2)}) copy-start(f32[4,4]{1,0:T(4,128)S(1)} %get-tuple-element.64) | copy-start | bytes 196
where the time goes:
time: 49.3 us; the launch traced here: 49.1 us
  starting transfers between devices  20.4 us (41%)
  waiting for transfers between devices  13.7 us (28%)
  Pallas kernels  11.5 us (23%)
  local copies, waits for them, and re-layouts  2.13 us (4%)
  between operations  1.39 us (3%)
    ppermute x18, starting transfers between devices, moved(): lax.ppermute(block, axis, [(i, target(i)) for i in range(lax.axis_size(ax...  20.4 us
    ppermute x18, waiting for transfers between devices, moved(): lax.ppermute(block, axis, [(i, target(i)) for i in range(lax.axis_size(ax...  13.7 us
    pallas_call x1, Pallas kernels, per_device(): pl.pallas_call(lattice_kernel, out_shape=(jax.ShapeDtypeStruct((DIRS, pla...  10.3 us
    unnamed x18, local copies, waits for them, and re-layouts  2.13 us
    pallas_call x1, Pallas kernels, per_device(): pl.pallas_call(functools.partial(finish_kernel, scale, count, rank), out_...  1.2 us
  transfers between devices with their start and end apart: 18, of which 12 were waited for; matrix products, arithmetic and copies ran while one was open for 0% of the time, Pallas kernels for 0%

commit v1 on v0

--- a/solution.py
+++ b/solution.py
@@ -123,21 +123,22 @@
         wide[c + 1, :, HALO : HALO + rows, :] = vel[c]
 
 
-def lattice_kernel(
-    place, snap_steps, b0, b1, b2, b3, b4, b5, b6, basis, pops, snaps, sums, fields, ping, pong, speeds, views, picked, gram
-):
-    blocks = (b0, b1, b2, b3, b4, b5, b6)
-    _, planes, wide, lanes = b0.shape
+def lattice_kernel(place, snap_steps, *refs):
+    blocks, refs = refs[:-11], refs[-11:]
+    basis, pops, snaps, sums, fields, ping, pong, speeds, views, picked, gram = refs
+    planes, wide, lanes = blocks[0].shape[-3:]
     reach = STEPS
     span = planes + 2 * reach
     tiles = wide // SUB
     rows = wide - 2 * HALO
     count = snap_steps.shape[0]
     row = lax.broadcasted_iota(jnp.int32, (SUB, lanes), 0)
-    for n, block in enumerate(blocks):
-        start = place[n]
+    for n in range(1 + 2 * (reach // planes)):
         for p in range(planes):
-            fields[start + p] = block[:, p]
+            if len(blocks) == 1:
+                fields[planes * n + p] = blocks[0][place[n], :, p]
+            else:
+                fields[place[n] + p] = blocks[n][:, p]
 
     def put_speed(x, t, speed):
         if HALO <= SUB * t < HALO + rows:
@@ -245,7 +246,10 @@
 
 def finish_kernel(scale, count, rank, *refs):
     parts, (snaps, basis, coef, factor, modes, flag, gram) = refs[:-7], refs[-7:]
-    total = tree_sum([part[...] for part in parts])
+    if len(parts) == 1:
+        total = tree_sum([parts[0][n] for n in range(parts[0].shape[0])])
+    else:
+        total = tree_sum([part[...] for part in parts])
     lanes = total.shape[1]
     head = total[0:SUB, :]
     proj = head[:, 0:rank]
@@ -327,6 +331,19 @@
     return found
 
 
+def summed(sums, n_dev, n_group):
+    rounds = []
+    for axis, size in (("dev", n_dev), ("group", n_group)):
+        stride = 1
+        for base in digits(size):
+            rounds.append((axis, stride, base))
+            stride *= base
+    parts = [sums]
+    for axis, stride, base in rounds:
+        parts = partners(tree_sum(parts), axis, stride, base)
+    return parts
+
+
 def from_residuals(coefficients, snaps, basis, scale):
     modes = basis[:, :, 0, :].astype(jnp.float32)
     count = coefficients.shape[1]
@@ -343,6 +360,20 @@
     return lower.T / scale, (jnp.stack(solved) * scale).reshape(-1, LANES)
 
 
+def ring_blocks(own, n_dev, planes, reach):
+    ahead = moved(own, "dev", lambda i: (i - 2) % n_dev)
+    behind = moved(own, "dev", lambda i: (i + 2) % n_dev)
+    far = moved(own, "dev", lambda i: (i + 3 if i % 2 else i - 3) % n_dev)
+    other = moved(own, "dev", lambda i: i ^ 1)
+    other_ahead = moved(ahead, "dev", lambda i: i ^ 1)
+    other_behind = moved(behind, "dev", lambda i: i ^ 1)
+    odd = lax.axis_index("dev") % 2
+    offsets = jnp.where(
+        odd == 1, jnp.array([0, 2, -2, 3, -1, 1, -3], jnp.int32), jnp.array([0, 2, -2, -3, 1, 3, -1], jnp.int32)
+    )
+    return [own, ahead, behind, far, other, other_ahead, other_behind], reach + planes * offsets
+
+
 def per_device(density, velocity, basis, snap_steps):
     planes, rows, lanes = density.shape
     count = snap_steps.shape[0]
@@ -369,17 +400,12 @@
         compiler_params=params,
     )(density, velocity, upper, lower)
 
-    ahead = moved(own, "dev", lambda i: (i - 2) % n_dev)
-    behind = moved(own, "dev", lambda i: (i + 2) % n_dev)
-    far = moved(own, "dev", lambda i: (i + 3 if i % 2 else i - 3) % n_dev)
-    other = moved(own, "dev", lambda i: i ^ 1)
-    other_ahead = moved(ahead, "dev", lambda i: i ^ 1)
-    other_behind = moved(behind, "dev", lambda i: i ^ 1)
-    odd = lax.axis_index("dev") % 2
-    offsets = jnp.where(
-        odd == 1, jnp.array([0, 2, -2, 3, -1, 1, -3], jnp.int32), jnp.array([0, 2, -2, -3, 1, 3, -1], jnp.int32)
-    )
-    place = reach + planes * offsets
+    near = reach // planes
+    if n_dev == 2 * near + 2:
+        blocks = [lax.all_gather(own, "dev")]
+        place = (lax.axis_index("dev") + jnp.arange(-near, near + 1, dtype=jnp.int32)) % n_dev
+    else:
+        blocks, place = ring_blocks(own, n_dev, planes, reach)
     modes = jnp.transpose(basis[:, :, 0, :], (1, 0, 2))
     span = planes + 2 * reach
     width = basis.shape[3]
@@ -390,7 +416,7 @@
             jax.ShapeDtypeStruct((3, SUB, width), f32),
             jax.ShapeDtypeStruct((2 * SUB, lanes), f32),
         ),
-        in_specs=[smem, smem] + [vmem] * 8,
+        in_specs=[smem, smem] + [vmem] * (len(blocks) + 1),
         out_specs=(vmem, vmem, vmem),
         scratch_shapes=[
             pltpu.VMEM((span, 4, wide_rows, lanes), f32),
@@ -402,17 +428,12 @@
             pltpu.VMEM((rank + SUB, lanes), f32),
         ],
         compiler_params=params,
-    )(place, snap_steps, own, ahead, behind, far, other, other_ahead, other_behind, modes)
-
-    rounds = []
-    for axis, size in (("dev", n_dev), ("group", n_group)):
-        stride = 1
-        for base in digits(size):
-            rounds.append((axis, stride, base))
-            stride *= base
-    parts = [sums]
-    for axis, stride, base in rounds:
-        parts = partners(tree_sum(parts), axis, stride, base)
+    )(place, snap_steps, *blocks, modes)
+
+    if n_dev * n_group <= 32:
+        parts = [lax.all_gather(sums, ("group", "dev"))]
+    else:
+        parts = summed(sums, n_dev, n_group)
     scale = math.sqrt(3 * width * n_dev * n_group)
     coef, factor, new_modes, flag = pl.pallas_call(
         functools.partial(finish_kernel, scale, count, rank),

time: 49.3 us -> 105 us (2.13)
  blocking collectives: 0 us -> 41.3 us
  starting transfers between devices: 20.4 us -> 5.14 us
  waiting for transfers between devices: 13.7 us -> 27.2 us
  between operations: 1.39 us -> 14.7 us
  local copies, waits for them, and re-layouts: 2.13 us -> 3.99 us
    all_gather x0 -> x1, blocking collectives: none -> 41.3 us  [per_device(): parts = [lax.all_gather(sums, ('group', 'dev'))]]
    all_gather x0 -> x1, waiting for transfers between devices: none -> 25 us  [per_device(): blocks = [lax.all_gather(own, 'dev')]]
    ppermute x18 -> x2, starting transfers between devices: 20.4 us -> 5.11 us  [moved(): lax.ppermute(block, axis, [(i, target(i)) for i in range(lax.axis_size(ax...]
    ppermute x18 -> x2, waiting for transfers between devices: 13.7 us -> 2.18 us  [moved(): lax.ppermute(block, axis, [(i, target(i)) for i in range(lax.axis_size(ax...]
    unnamed x18 -> x16, local copies, waits for them, and re-layouts: 2.13 us -> 3.99 us
  transfers between devices with their start and end apart: 18 -> 3, of which waited for: 12 -> 3; matrix products, arithmetic and copies ran while one was open for 0% -> 0% of each run, Pallas kernels for 0% -> 0%
where the time goes in v1:
time: 105 us
  blocking collectives  41.3 us (39%)
  waiting for transfers between devices  27.2 us (26%)
  between operations  14.7 us (14%)
  Pallas kernels  12.2 us (12%)
  starting transfers between devices  5.14 us (5%)
  local copies, waits for them, and re-layouts  3.99 us (4%)
    all_gather x1, blocking collectives, per_device(): parts = [lax.all_gather(sums, ('group', 'dev'))]  41.3 us
    all_gather x1, waiting for transfers between devices, per_device(): blocks = [lax.all_gather(own, 'dev')]  25 us
    pallas_call x1, Pallas kernels, per_device(): pl.pallas_call(lattice_kernel, out_shape=(jax.ShapeDtypeStruct((DIRS, pla...  10.3 us
    ppermute x2, starting transfers between devices, moved(): lax.ppermute(block, axis, [(i, target(i)) for i in range(lax.axis_size(ax...  5.11 us
    unnamed x16, local copies, waits for them, and re-layouts  3.99 us
    ppermute x2, waiting for transfers between devices, moved(): lax.ppermute(block, axis, [(i, target(i)) for i in range(lax.axis_size(ax...  2.18 us
  transfers between devices with their start and end apart: 3, of which 3 were waited for; matrix products, arithmetic and copies ran while one was open for 0% of the time, Pallas kernels for 0%

profile of v1, /device:TPU:0, one launch (start us, length us, event | category | flops | bytes accessed | tf_op | source)
XLA Modules:
  0.0 104.5 jit_solution(5755695174083835189)
XLA Ops:
  7.2 0.0 all-gather.4.cloned.1.call-start
  7.2 0.0 copy-start.1
  7.2 0.8 copy-done.1
  8.0 0.0 copy-start.2
  8.0 0.7 copy-done.2
  8.7 3.0 %collective-permute-start = (f32[4,2,8,128]{3,2,1,0:T(8,128)S(1)}, f32[4,2,8,128]{3,2,1,0:T(8,128)S(1)}, u32[]{:S(2)}, u32[]{:S(2)}) collective-permute-start(f32[4,2,8,128]{3,2,1,0:T(8,128)S(1)} %get-tuple-element.33), channel_id=1, source_target_pairs={{0,8},{8,16},{16,24},{24,0},{1,9},{9,17},{17,25},{25,1},{2,10},{10... | collective-permute-start | bytes 98312 | tf_op jit(solution)/shard_map/ppermute | solution.py:303
  11.8 2.1 %collective-permute-start.1 = (f32[4,2,8,128]{3,2,1,0:T(8,128)S(1)}, f32[4,2,8,128]{3,2,1,0:T(8,128)S(1)}, u32[]{:S(2)}, u32[]{:S(2)}) collective-permute-start(f32[4,2,8,128]{3,2,1,0:T(8,128)S(1)} %get-tuple-element.34), channel_id=1, source_target_pairs={{0,24},{8,0},{16,8},{24,16},{1,25},{9,1},{17,9},{25,17},{2,26},{10... | collective-permute-start | bytes 98312 | tf_op jit(solution)/shard_map/ppermute | solution.py:303
  13.8 1.9 %collective-permute-done.upper = f32[4,2,8,128]{3,2,1,0:T(8,128)S(1)} collective-permute-done((f32[4,2,8,128]{3,2,1,0:T(8,128)S(1)}, f32[4,2,8,128]{3,2,1,0:T(8,128)S(1)}, u32[]{:S(2)}, u32[]{:S(2)}) %collective-permute-start) | collective-permute-done | bytes 32800 | tf_op jit(solution)/shard_map/ppermute | solution.py:303
  15.8 0.2 collective-permute-done.1.lower
  16.0 0.7 shard_map.76
  16.7 0.0 copy-start.4
  16.7 0.0 all-gather.4.cloned.1.call-update
  16.7 25.0 %all-gather.4.cloned.1.call-done = f32[32,2,32,128]{3,2,1,0:T(8,128)} async-done(((f32[4,2,32,128]{3,2,1,0:T(8,128)}), f32[32,2,32,128]{3,2,1,0:T(8,128)}) %all-gather.4.cloned.1.call-update) | async-done | bytes 1048592 | tf_op jit(solution)/shard_map/all_gather | solution.py:405
  41.7 0.0 copy-start.3
  41.7 0.0 copy-done.4
  41.7 0.7 copy-done.3
  42.4 0.0 copy-start
  42.4 1.2 %copy-done = f32[32,2,32,128]{3,2,1,0:T(8,128)S(1)} copy-done((f32[32,2,32,128]{3,2,1,0:T(8,128)S(1)}, f32[32,2,32,128]{3,2,1,0:T(8,128)}, u32[]{:S(2)}) %copy-start) | copy-done | bytes 1048600
  43.6 10.3 %shard_map.77 = (f32[19,2,16,128]{3,2,1,0:T(8,128)}, f32[3,8,512]{2,1,0:T(8,128)S(1)}, f32[16,128]{1,0:T(8,128)S(1)}) custom-call(s32[7]{0:T(128)S(1)} %and_select_fusion.place, s32[4]{0:T(128)S(1)} %copy-done.3, f32[8,4,2,32,128]{4,3,2,1,0:T(8,128)S(1)} %bitcast.42, bf16[3,32,512]{2,1,0:T(8,128)(2,1)S(1)} %bitcast.44), custom_call_target="tpu_custom_call" | custom-call | tf_op jit(solution)/shard_map/pallas_call | solution.py:412
  53.9 41.3 %all-gather.1 = f32[512,128]{1,0:T(8,128)S(1)} all-gather(f32[16,128]{1,0:T(8,128)S(1)} %get-tuple-element.36), channel_id=3, replica_groups=mesh['group'=4,'dev'=8] {'group','dev'}, dimensions={0}, use_global_device_ids=true | all-gather | bytes 270336 | tf_op jit(solution)/shard_map/all_gather | solution.py:434
  95.1 1.2 %shard_map.78 = (f32[4,32]{1,0:T(4,128)S(1)}, f32[4,4]{1,0:T(4,128)S(1)}, f32[48,128]{1,0:T(8,128)S(1)}, s32[1,1]{1,0:T(1,128)}) custom-call(f32[32,16,128]{2,1,0:T(8,128)S(1)} %bitcast.43, f32[3,8,512]{2,1,0:T(8,128)S(1)} %get-tuple-element.37.refs_1_, bf16[3,32,512]{2,1,0:T(8,128)(2,1)S(1)} %bitcast.45), custom_call_target="tpu_custom_call" | custom-call | tf_op jit(solution)/shard_map/pallas_call | solution.py:438
  96.4 0.0 copy-start.5
  97.0 0.0 copy-done.5
  97.0 0.0 copy-start.6
  97.1 0.0 copy-start.7
  97.1 0.6 copy-done.6
  97.7 0.0 copy-done.7
  (3 shorter events, 0.0 us)
Async XLA Ops:
  7.2 34.5 %all-gather.4.cloned.1.call-start = ((), (), s32[]{:S(2)}) async-start(), calls=%async_computation | async-start | bytes 1179648 | tf_op jit(solution)/shard_map/all_gather | solution.py:405
  7.2 0.8 copy-start.1
  8.0 0.7 copy-start.2
  8.7 7.0 %collective-permute-start = (f32[4,2,8,128]{3,2,1,0:T(8,128)S(1)}, f32[4,2,8,128]{3,2,1,0:T(8,128)S(1)}, u32[]{:S(2)}, u32[]{:S(2)}) collective-permute-start(f32[4,2,8,128]{3,2,1,0:T(8,128)S(1)} %get-tuple-element.33), channel_id=1, source_target_pairs={{0,8},{8,16},{16,24},{24,0},{1,9},{9,17},{17,25},{25,1},{2,10},{10... | collective-permute-start | bytes 98312 | tf_op jit(solution)/shard_map/ppermute | solution.py:303
  11.8 4.3 %collective-permute-start.1 = (f32[4,2,8,128]{3,2,1,0:T(8,128)S(1)}, f32[4,2,8,128]{3,2,1,0:T(8,128)S(1)}, u32[]{:S(2)}, u32[]{:S(2)}) collective-permute-start(f32[4,2,8,128]{3,2,1,0:T(8,128)S(1)} %get-tuple-element.34), channel_id=1, source_target_pairs={{0,24},{8,0},{16,8},{24,16},{1,25},{9,1},{17,9},{25,17},{2,26},{10... | collective-permute-start | bytes 98312 | tf_op jit(solution)/shard_map/ppermute | solution.py:303
  16.7 25.0 %copy-start.4 = (bf16[32,3,1,512]{3,0,2,1:T(8,128)(2,1)S(1)}, bf16[32,3,1,512]{3,0,2,1:T(8,128)(2,1)}, u32[]{:S(2)}) copy-start(bf16[32,3,1,512]{3,0,2,1:T(8,128)(2,1)} %param.8) | copy-start | bytes 294916
  41.7 0.7 copy-start.3
  42.4 1.2 %copy-start = (f32[32,2,32,128]{3,2,1,0:T(8,128)S(1)}, f32[32,2,32,128]{3,2,1,0:T(8,128)}, u32[]{:S(2)}) copy-start(f32[32,2,32,128]{3,2,1,0:T(8,128)} %all-gather.4.cloned.1.call-done) | copy-start | bytes 3145732
  96.4 0.7 copy-start.5
  97.0 0.6 copy-start.6
  97.1 0.6 copy-start.7
Sparse Core Ops, SparseCore 0:
  16.8 24.8 all-gather.3

commit v2 on v1

--- a/solution.py
+++ b/solution.py
@@ -402,7 +402,7 @@
 
     near = reach // planes
     if n_dev == 2 * near + 2:
-        blocks = [lax.all_gather(own, "dev")]
+        blocks = [lax.all_to_all(jnp.broadcast_to(own, (n_dev, *own.shape)), "dev", 0, 0)]
         place = (lax.axis_index("dev") + jnp.arange(-near, near + 1, dtype=jnp.int32)) % n_dev
     else:
         blocks, place = ring_blocks(own, n_dev, planes, reach)
@@ -431,7 +431,7 @@
     )(place, snap_steps, *blocks, modes)
 
     if n_dev * n_group <= 32:
-        parts = [lax.all_gather(sums, ("group", "dev"))]
+        parts = [lax.all_to_all(jnp.broadcast_to(sums, (n_dev * n_group, *sums.shape)), ("group", "dev"), 0, 0)]
     else:
         parts = summed(sums, n_dev, n_group)
     scale = math.sqrt(3 * width * n_dev * n_group)

time: 105 us -> 57.5 us (0.55)
  blocking collectives: 41.3 us -> 14.5 us
  between operations: 14.7 us -> 1.36 us
  waiting for transfers between devices: 27.2 us -> 17.6 us
  starting transfers between devices: 5.14 us -> 8.96 us
    all_gather x1 -> x0, blocking collectives: 41.3 us -> none  [per_device(): parts = [lax.all_gather(sums, ('group', 'dev'))]]
    all_gather x1 -> x0, waiting for transfers between devices: 25 us -> none  [per_device(): blocks = [lax.all_gather(own, 'dev')]]
    all_to_all x0 -> x1, waiting for transfers between devices: none -> 15.4 us  [per_device(): lax.all_to_all(jnp.broadcast_to(own, (n_dev, *own.shape)), 'dev', 0, 0)]
    all_to_all x0 -> x1, blocking collectives: none -> 14.5 us  [per_device(): lax.all_to_all(jnp.broadcast_to(sums, (n_dev * n_group, *sums.shape)), ('...]
    all_to_all x0 -> x1, starting transfers between devices: none -> 3.85 us  [per_device(): lax.all_to_all(jnp.broadcast_to(own, (n_dev, *own.shape)), 'dev', 0, 0)]
    unnamed x16 -> x14, local copies, waits for them, and re-layouts: 3.99 us -> 2.12 us
    broadcast_in_dim x0 -> x2, local copies, waits for them, and re-layouts: none -> 1.12 us  [the longest x1 1.1 us: per_device(): jnp.broadcast_to(own, (n_dev, *own.shape))]
where the time goes in v2:
time: 57.5 us; the launch traced here: 57.1 us
  waiting for transfers between devices  17.6 us (31%)
  blocking collectives  14.5 us (25%)
  Pallas kernels  11.5 us (20%)
  starting transfers between devices  8.96 us (16%)
  local copies, waits for them, and re-layouts  3.24 us (6%)
  between operations  1.36 us (2%)
    all_to_all x1, waiting for transfers between devices, per_device(): lax.all_to_all(jnp.broadcast_to(own, (n_dev, *own.shape)), 'dev', 0, 0)  15.4 us
    all_to_all x1, blocking collectives, per_device(): lax.all_to_all(jnp.broadcast_to(sums, (n_dev * n_group, *sums.shape)), ('...  14.5 us
    pallas_call x1, Pallas kernels, per_device(): pl.pallas_call(lattice_kernel, out_shape=(jax.ShapeDtypeStruct((DIRS, pla...  10.3 us
    ppermute x2, starting transfers between devices, moved(): lax.ppermute(block, axis, [(i, target(i)) for i in range(lax.axis_size(ax...  5.11 us
    all_to_all x1, starting transfers between devices, per_device(): lax.all_to_all(jnp.broadcast_to(own, (n_dev, *own.shape)), 'dev', 0, 0)  3.85 us
    ppermute x2, waiting for transfers between devices, moved(): lax.ppermute(block, axis, [(i, target(i)) for i in range(lax.axis_size(ax...  2.18 us
    unnamed x14, local copies, waits for them, and re-layouts  2.12 us
    pallas_call x1, Pallas kernels, per_device(): pl.pallas_call(functools.partial(finish_kernel, scale, count, rank), out_...  1.2 us
  transfers between devices with their start and end apart: 3, of which 3 were waited for; matrix products, arithmetic and copies ran while one was open for 0% of the time, Pallas kernels for 0%

profile of v2, /device:TPU:0, one launch (start us, length us, event | category | flops | bytes accessed | tf_op | source)
XLA Modules:
  0.0 57.1 jit_solution(10201218698233648198)
XLA Ops:
  0.6 0.0 copy-start
  0.6 0.8 %copy-done = f32[3,2,16,128]{3,2,1,0:T(8,128)S(1)} copy-done((f32[3,2,16,128]{3,2,1,0:T(8,128)S(1)}, f32[3,2,16,128]{3,2,1,0:T(8,128)}, u32[]{:S(2)}) %copy-start) | copy-done | bytes 49176
  1.4 0.0 copy-start.1
  1.4 0.7 %copy-done.1 = f32[2,16,128]{2,1,0:T(8,128)S(1)} copy-done((f32[2,16,128]{2,1,0:T(8,128)S(1)}, f32[2,16,128]{2,1,0:T(8,128)}, u32[]{:S(2)}) %copy-start.1) | copy-done | bytes 16408
  2.2 3.0 %collective-permute-start = (f32[4,2,8,128]{3,2,1,0:T(8,128)S(1)}, f32[4,2,8,128]{3,2,1,0:T(8,128)S(1)}, u32[]{:S(2)}, u32[]{:S(2)}) collective-permute-start(f32[4,2,8,128]{3,2,1,0:T(8,128)S(1)} %get-tuple-element.33), channel_id=1, source_target_pairs={{0,8},{8,16},{16,24},{24,0},{1,9},{9,17},{17,25},{25,1},{2,10},{10... | collective-permute-start | bytes 98312 | tf_op jit(solution)/shard_map/ppermute | solution.py:303
  5.2 2.1 %collective-permute-start.1 = (f32[4,2,8,128]{3,2,1,0:T(8,128)S(1)}, f32[4,2,8,128]{3,2,1,0:T(8,128)S(1)}, u32[]{:S(2)}, u32[]{:S(2)}) collective-permute-start(f32[4,2,8,128]{3,2,1,0:T(8,128)S(1)} %get-tuple-element.34), channel_id=1, source_target_pairs={{0,24},{8,0},{16,8},{24,16},{1,25},{9,1},{17,9},{25,17},{2,26},{10... | collective-permute-start | bytes 98312 | tf_op jit(solution)/shard_map/ppermute | solution.py:303
  7.3 1.9 %collective-permute-done.upper = f32[4,2,8,128]{3,2,1,0:T(8,128)S(1)} collective-permute-done((f32[4,2,8,128]{3,2,1,0:T(8,128)S(1)}, f32[4,2,8,128]{3,2,1,0:T(8,128)S(1)}, u32[]{:S(2)}, u32[]{:S(2)}) %collective-permute-start) | collective-permute-done | bytes 32800 | tf_op jit(solution)/shard_map/ppermute | solution.py:303
  9.2 0.2 collective-permute-done.1.lower
  9.5 1.1 %broadcast_in_dim.6 = f32[8,4,2,32,128]{4,3,2,1,0:T(8,128)} broadcast(f32[4,2,32,128]{3,2,1,0:T(8,128)S(1)} %shard_map.76), dimensions={1,2,3,4} | broadcast | bytes 1179648 | tf_op jit(solution)/shard_map/broadcast_in_dim | solution.py:405
  10.6 0.0 copy-start.3
  10.6 3.9 %all-to-all-start = ((f32[8,4,2,32,128]{4,3,2,1,0:T(8,128)}), f32[8,4,2,32,128]{4,3,2,1,0:T(8,128)S(1)}, u32[]{:S(2)}, u32[]{:S(2)}) async-start(f32[8,4,2,32,128]{4,3,2,1,0:T(8,128)} %broadcast_in_dim.6), calls=%async_computation | async-start | bytes 2097152 | tf_op jit(solution)/shard_map/all_to_all | solution.py:405
  14.4 0.0 copy-start.2
  14.4 15.4 %all-to-all-done.refs_0_ = f32[8,4,2,32,128]{4,3,2,1,0:T(8,128)S(1)} async-done(((f32[8,4,2,32,128]{4,3,2,1,0:T(8,128)}), f32[8,4,2,32,128]{4,3,2,1,0:T(8,128)S(1)}, u32[]{:S(2)}, u32[]{:S(2)}) %all-to-all-start) | async-done | bytes 1048608 | tf_op jit(solution)/shard_map/all_to_all | solution.py:405
  29.8 0.0 copy-done.3
  29.8 0.0 copy-done.2
  29.8 10.3 %shard_map.77 = (f32[19,2,16,128]{3,2,1,0:T(8,128)}, f32[3,8,512]{2,1,0:T(8,128)S(1)}, f32[16,128]{1,0:T(8,128)S(1)}) custom-call(s32[7]{0:T(128)S(1)} %and_select_fusion.place, s32[4]{0:T(128)S(1)} %copy-done.2, f32[8,4,2,32,128]{4,3,2,1,0:T(8,128)S(1)} %all-to-all-done.refs_0_, bf16[3,32,512]{2,1,0:T(8,128)(2,1)S(1)} %bitcast.40), custom_call_target="tpu_custom_call" | custom-call | tf_op jit(solution)/shard_map/pallas_call | solution.py:412
  40.1 14.5 %all_to_all.10.refs_0_ = f32[32,16,128]{2,1,0:T(8,128)S(1)} all-to-all(f32[32,16,128]{2,1,0:T(8,128)S(1)} %broadcast_in_dim.7), channel_id=1, replica_groups=mesh['group'=4,'dev'=8] {'group','dev'}, dimensions={0} | all-to-all | bytes 524288 | tf_op jit(solution)/shard_map/all_to_all | solution.py:434
  54.6 1.2 %shard_map.78 = (f32[4,32]{1,0:T(4,128)S(1)}, f32[4,4]{1,0:T(4,128)S(1)}, f32[48,128]{1,0:T(8,128)S(1)}, s32[1,1]{1,0:T(1,128)}) custom-call(f32[32,16,128]{2,1,0:T(8,128)S(1)} %all_to_all.10.refs_0_, f32[3,8,512]{2,1,0:T(8,128)S(1)} %get-tuple-element.37.refs_1_, bf16[3,32,512]{2,1,0:T(8,128)(2,1)S(1)} %bitcast.41), custom_call_target="tpu_custom_call" | custom-call | tf_op jit(solution)/shard_map/pallas_call | solution.py:438
  55.8 0.0 copy-start.4
  56.5 0.0 copy-done.4
  56.5 0.0 copy-start.5
  56.5 0.0 copy-start.6
  56.6 0.6 %copy-done.5 = f32[4,3,1,512]{3,2,1,0:T(1,128)} copy-done((f32[4,3,1,512]{3,2,1,0:T(1,128)}, f32[4,3,1,512]{3,2,1,0:T(1,128)S(1)}, u32[]{:S(2)}) %copy-start.5) | copy-done | bytes 24600
  57.1 0.0 copy-done.6
  (5 shorter events, 0.1 us)
Async XLA Ops:
  0.6 0.8 %copy-start = (f32[3,2,16,128]{3,2,1,0:T(8,128)S(1)}, f32[3,2,16,128]{3,2,1,0:T(8,128)}, u32[]{:S(2)}) copy-start(f32[3,2,16,128]{3,2,1,0:T(8,128)} %vel.3) | copy-start | bytes 147460
  1.4 0.7 %copy-start.1 = (f32[2,16,128]{2,1,0:T(8,128)S(1)}, f32[2,16,128]{2,1,0:T(8,128)}, u32[]{:S(2)}) copy-start(f32[2,16,128]{2,1,0:T(8,128)} %dens.3) | copy-start | bytes 49156
  2.2 7.0 %collective-permute-start = (f32[4,2,8,128]{3,2,1,0:T(8,128)S(1)}, f32[4,2,8,128]{3,2,1,0:T(8,128)S(1)}, u32[]{:S(2)}, u32[]{:S(2)}) collective-permute-start(f32[4,2,8,128]{3,2,1,0:T(8,128)S(1)} %get-tuple-element.33), channel_id=1, source_target_pairs={{0,8},{8,16},{16,24},{24,0},{1,9},{9,17},{17,25},{25,1},{2,10},{10... | collective-permute-start | bytes 98312 | tf_op jit(solution)/shard_map/ppermute | solution.py:303
  5.2 4.3 %collective-permute-start.1 = (f32[4,2,8,128]{3,2,1,0:T(8,128)S(1)}, f32[4,2,8,128]{3,2,1,0:T(8,128)S(1)}, u32[]{:S(2)}, u32[]{:S(2)}) collective-permute-start(f32[4,2,8,128]{3,2,1,0:T(8,128)S(1)} %get-tuple-element.34), channel_id=1, source_target_pairs={{0,24},{8,0},{16,8},{24,16},{1,25},{9,1},{17,9},{25,17},{2,26},{10... | collective-permute-start | bytes 98312 | tf_op jit(solution)/shard_map/ppermute | solution.py:303
  10.6 19.3 %copy-start.3 = (bf16[32,3,1,512]{3,0,2,1:T(8,128)(2,1)S(1)}, bf16[32,3,1,512]{3,0,2,1:T(8,128)(2,1)}, u32[]{:S(2)}) copy-start(bf16[32,3,1,512]{3,0,2,1:T(8,128)(2,1)} %param.8) | copy-start | bytes 294916
  10.6 19.3 %all-to-all-start = ((f32[8,4,2,32,128]{4,3,2,1,0:T(8,128)}), f32[8,4,2,32,128]{4,3,2,1,0:T(8,128)S(1)}, u32[]{:S(2)}, u32[]{:S(2)}) async-start(f32[8,4,2,32,128]{4,3,2,1,0:T(8,128)} %broadcast_in_dim.6), calls=%async_computation | async-start | bytes 2097152 | tf_op jit(solution)/shard_map/all_to_all | solution.py:405
  14.4 15.4 %copy-start.2 = (s32[4]{0:T(128)S(1)}, s32[4]{0:T(128)}, u32[]{:S(2)}) copy-start(s32[4]{0:T(128)} %snap_steps.1) | copy-start | bytes 52
  55.8 0.7 %copy-start.4 = (f32[4,32]{1,0:T(4,128)}, f32[4,32]{1,0:T(4,128)S(1)}, u32[]{:S(2)}) copy-start(f32[4,32]{1,0:T(4,128)S(1)} %get-tuple-element.38) | copy-start | bytes 1540
  56.5 0.6 %copy-start.5 = (f32[4,3,1,512]{3,2,1,0:T(1,128)}, f32[4,3,1,512]{3,2,1,0:T(1,128)S(1)}, u32[]{:S(2)}) copy-start(f32[4,3,1,512]{3,2,1,0:T(1,128)S(1)} %get-tuple-element.65) | copy-start | bytes 73732
  56.5 0.6 %copy-start.6 = (f32[4,4]{1,0:T(4,128)}, f32[4,4]{1,0:T(4,128)S(1)}, u32[]{:S(2)}) copy-start(f32[4,4]{1,0:T(4,128)S(1)} %get-tuple-element.64) | copy-start | bytes 196

commit v3 on v2

--- a/solution.py
+++ b/solution.py
@@ -26,7 +26,7 @@
 
 def along(direction, parts):
     total = None
-    for sign, part in zip(direction, parts):
+    for sign, part in sorted(zip(direction, parts), key=lambda pair: -pair[0]):
         if sign == 0:
             continue
         if total is None:
@@ -82,22 +82,12 @@
     return dens, mom
 
 
-def streamed(src, x, tiles, row):
-    turned = {}
-
-    def turn(i, t):
-        if (i, t) not in turned:
-            tile = src[i, x - DIR_X[i], pl.ds(SUB * t, SUB), :]
-            turned[i, t] = pltpu.roll(tile, DIR_Y[i] % SUB, 0)
-        return turned[i, t]
-
+def streamed(src, x, tiles):
     def get(i, t):
-        if DIR_Y[i] == 0:
-            tile = src[i, x - DIR_X[i], pl.ds(SUB * t, SUB), :]
-        elif DIR_Y[i] > 0:
-            tile = jnp.where(row == 0, turn(i, max(t - 1, 0)), turn(i, t))
-        else:
-            tile = jnp.where(row == SUB - 1, turn(i, min(t + 1, tiles - 1)), turn(i, t))
+        at = t - DIR_Y[i]
+        tile = src[i, x - DIR_X[i], at % tiles]
+        if at < 0 or at >= tiles:
+            tile = pltpu.roll(tile, DIR_Y[i] % SUB, 0)
         if DIR_Z[i] != 0:
             tile = pltpu.roll(tile, DIR_Z[i] % LANES, 1)
         return tile
@@ -105,74 +95,91 @@
     return get
 
 
-def edges_kernel(dens, vel, top, bottom):
+def edges_kernel(dens, vel, top, bottom, sems):
     rows = dens.shape[1]
-    top[0] = dens[:, rows - HALO :, :]
-    bottom[0] = dens[:, :HALO, :]
+    last, first = pl.ds(rows - HALO, HALO), pl.ds(0, HALO)
+    copies = [
+        pltpu.make_async_copy(dens.at[:, last, :], top.at[0], sems.at[0]),
+        pltpu.make_async_copy(vel.at[:, :, last, :], top.at[pl.ds(1, 3)], sems.at[1]),
+        pltpu.make_async_copy(dens.at[:, first, :], bottom.at[0], sems.at[2]),
+        pltpu.make_async_copy(vel.at[:, :, first, :], bottom.at[pl.ds(1, 3)], sems.at[3]),
+    ]
+    for copy in copies:
+        copy.start()
+    for copy in copies:
+        copy.wait()
+
+
+def widen_kernel(dens, vel, upper, lower, wide, whole):
+    planes, rows, _ = dens.shape
+    whole[:, :, :HALO, :] = upper[...]
+    whole[:, :, HALO + rows :, :] = lower[...]
+    whole[0, :, HALO : HALO + rows, :] = dens[...]
+    tiles = wide.shape[2]
     for c in range(3):
-        top[c + 1] = vel[c, :, rows - HALO :, :]
-        bottom[c + 1] = vel[c, :, :HALO, :]
-
-
-def widen_kernel(dens, vel, upper, lower, wide):
-    rows = dens.shape[1]
-    wide[:, :, :HALO, :] = upper[...]
-    wide[:, :, HALO + rows :, :] = lower[...]
-    wide[0, :, HALO : HALO + rows, :] = dens[...]
-    for c in range(3):
-        wide[c + 1, :, HALO : HALO + rows, :] = vel[c]
+        whole[c + 1, :, HALO : HALO + rows, :] = vel[c]
+    for f in range(4):
+        for p in range(planes):
+            for t in range(tiles):
+                wide[f, p, t] = whole[f, p, pl.ds(t, SUB, stride=tiles), :]
+
+
+def split3(value):
+    a = value.astype(jnp.bfloat16).astype(jnp.float32)
+    rest = value - a
+    b = rest.astype(jnp.bfloat16).astype(jnp.float32)
+    return a, b, rest - b
 
 
 def lattice_kernel(place, snap_steps, *refs):
-    blocks, refs = refs[:-11], refs[-11:]
-    basis, pops, snaps, sums, fields, ping, pong, speeds, views, picked, gram = refs
-    planes, wide, lanes = blocks[0].shape[-3:]
+    blocks, refs = refs[:-12], refs[-12:]
+    basis, pops, snaps, sums, ping, pong, speeds, views, coarse, rowwise, gram, whole = refs
+    planes, tiles, _, lanes = blocks[0].shape[1:]
     reach = STEPS
     span = planes + 2 * reach
-    tiles = wide // SUB
-    rows = wide - 2 * HALO
+    rows = pops.shape[2]
+    inner = HALO // tiles
     count = snap_steps.shape[0]
-    row = lax.broadcasted_iota(jnp.int32, (SUB, lanes), 0)
-    for n in range(1 + 2 * (reach // planes)):
-        for p in range(planes):
-            if len(blocks) == 1:
-                fields[planes * n + p] = blocks[0][place[n], :, p]
-            else:
-                fields[place[n] + p] = blocks[n][:, p]
-
-    def put_speed(x, t, speed):
-        if HALO <= SUB * t < HALO + rows:
-            for c in range(3):
-                speeds[x, c, pl.ds(SUB * t - HALO, SUB), :] = speed[c]
+
+    def put_speed(x, held):
+        for c in range(3):
+            for half in range(2):
+                speeds[x, c, half] = held[2 * half][c] + held[2 * half + 1][c]
 
     def keep_view(step):
         for c in range(3):
-            total = speeds[reach, c]
-            for p in range(1, planes):
-                total = total + speeds[reach + p, c]
-            views[step, c] = total
-
-    def first(x, carry):
-        for t in range(tiles):
-            at = pl.ds(SUB * t, SUB)
-            dens = fields[x, 0, at, :]
-            vel = [fields[x, c + 1, at, :] for c in range(3)]
-            part = dens * (3.0 / 36.0)
-            speed = [1.5 * v for v in vel]
-            out = relaxed(1.0, dens, [part * v for v in vel], speed, None)
-            for i in range(DIRS):
-                ping[i, x, at, :] = out[i]
-            put_speed(x, t, speed)
-        return carry
-
-    lax.fori_loop(0, span, first, 0)
+            for half in range(2):
+                total = speeds[reach, c, half]
+                for p in range(1, planes):
+                    total = total + speeds[reach + p, c, half]
+                views[step, c, half] = total
+
+    for n, block in enumerate(blocks):
+        start = place[n]
+
+        def first(p, carry, block=block, start=start):
+            held = []
+            for t in range(tiles):
+                dens = block[0, p, t]
+                vel = [block[c + 1, p, t] for c in range(3)]
+                part = dens * (3.0 / 36.0)
+                speed = [1.5 * v for v in vel]
+                out = relaxed(1.0, dens, [part * v for v in vel], speed, None)
+                for i in range(DIRS):
+                    ping[i, start + p, t] = out[i]
+                held.append(speed)
+            put_speed(start + p, held)
+            return carry
+
+        lax.fori_loop(0, planes, first, 0)
     keep_view(0)
 
     src, dst = ping, pong
     for step in range(1, STEPS):
 
         def later(x, carry, src=src, dst=dst):
-            get = streamed(src, x, tiles, row)
+            get = streamed(src, x, tiles)
+            held = []
             for t in range(tiles):
                 pop = [get(i, t) for i in range(DIRS)]
                 dens, mom = moments(pop)
@@ -181,8 +188,9 @@
                 flow = [m * (OMEGA * 3.0 / 36.0) for m in mom]
                 out = relaxed(OMEGA, dens, flow, speed, pop)
                 for i in range(DIRS):
-                    dst[i, x, pl.ds(SUB * t, SUB), :] = out[i]
-                put_speed(x, t, speed)
+                    dst[i, x, t] = out[i]
+                held.append(speed)
+            put_speed(x, held)
             return carry
 
         lax.fori_loop(step, span - step, later, 0)
@@ -190,78 +198,97 @@
         src, dst = dst, src
 
     for p in range(planes):
-        get = streamed(src, reach + p, tiles, row)
-        for t in range(HALO // SUB, (HALO + rows) // SUB):
-            for i in range(DIRS):
-                pops[i, p, pl.ds(SUB * t - HALO, SUB), :] = get(i, t)
-
-    picked[...] = jnp.zeros_like(picked)
-    for k in range(count):
-        at_step = snap_steps[k]
-        for c in range(3):
-            picked[c, pl.ds(rows * k, rows), :] = views[at_step, c]
-    groups = rows // 4
-    lefts, rights = [], []
-    for c in range(3):
-        for t in range(groups):
-            part = [picked[c, pl.ds(4 * t + j, SUB, stride=rows), :] for j in range(4)]
-            lefts.append(part[0] + part[1])
-            rights.append(part[2] + part[3])
+        get = streamed(src, reach + p, tiles)
+        for i in range(DIRS):
+            for t in range(tiles):
+                whole[p, i, pl.ds(t, SUB, stride=tiles), :] = get(i, t)
+            pops[i, p] = whole[p, i, HALO : HALO + rows, :]
+
+    halves = [[views[snap_steps[k], c, half] for k in range(count) for c in range(3)] for half in range(2)]
     lane = lax.broadcasted_iota(jnp.int32, (lanes, lanes), 0) // 2
     col = lax.broadcasted_iota(jnp.int32, (lanes, lanes), 1)
-    to_left = jnp.where(lane == col, 1.0, 0.0).astype(jnp.float32)
-    to_right = jnp.where(lane + lanes // 2 == col, 1.0, 0.0).astype(jnp.float32)
-    flat = jnp.dot(jnp.concatenate(lefts, axis=0), to_left, precision=HIGHEST, preferred_element_type=jnp.float32)
-    flat = flat + jnp.dot(
-        jnp.concatenate(rights, axis=0), to_right, precision=HIGHEST, preferred_element_type=jnp.float32
-    )
-    flat = flat * (UNIT / (4 * planes) / 1.5)
+    flat = None
+    for half in range(2):
+        gather = jnp.where(lane + half * (lanes // 2) == col, 1.0, 0.0).astype(jnp.bfloat16)
+        stack = jnp.concatenate(halves[half], axis=0)
+        for part in split3(stack):
+            term = jnp.dot(part.astype(jnp.bfloat16), gather, preferred_element_type=jnp.float32)
+            flat = term if flat is None else flat + term
+    height = 3 * SUB * count
+    coarse[height:, :] = jnp.zeros_like(coarse[height:, :])
+    coarse[0:height, :] = flat * (UNIT / (4 * planes) / 1.5)
     rank = basis.shape[1]
-    width = groups * lanes
+    groups = rows // tiles
+    total = None
     for c in range(3):
-        for t in range(groups):
-            n = c * groups + t
-            snaps[c, :, pl.ds(lanes * t, lanes)] = flat[SUB * n : SUB * (n + 1), :]
-
-    proj = jnp.zeros((SUB, rank), jnp.float32)
-    inner = jnp.zeros((SUB, SUB), jnp.float32)
-    modes2 = jnp.zeros((rank, rank), jnp.float32)
-    for c in range(3):
-        snap = snaps[c]
-        mode = basis[c].astype(jnp.float32)
-        proj += lax.dot_general(snap, mode, NT, precision=HIGHEST, preferred_element_type=jnp.float32)
-        inner += lax.dot_general(snap, snap, NT, precision=HIGHEST, preferred_element_type=jnp.float32)
-        modes2 += lax.dot_general(basis[c], basis[c], NT, preferred_element_type=jnp.float32)
-    sums[...] = jnp.zeros_like(sums)
+        parts = [coarse[pl.ds(SUB * c + inner + t, SUB, stride=3 * SUB), :] for t in range(groups)]
+        snap = jnp.concatenate(parts, axis=1)
+        snaps[c] = snap
+        a, b, d = split3(snap)
+        rowwise[0:rank, :] = basis[c]
+        rowwise[rank : rank + 2 * SUB, :] = jnp.concatenate([a, b], axis=0).astype(jnp.bfloat16)
+        rowwise[rank + 2 * SUB :, :] = jnp.concatenate([d, jnp.zeros_like(d)], axis=0).astype(jnp.bfloat16)
+        term = lax.dot_general(rowwise[...], rowwise[...], NT, preferred_element_type=jnp.float32)
+        total = term if total is None else total + term
     gram[...] = jnp.zeros_like(gram)
-    sums[0:SUB, 0:rank] = proj
-    gram[0:rank, 0:rank] = modes2
-    gram[rank : rank + SUB, 0:SUB] = inner
-    sums[0:SUB, :] = sums[0:SUB, :] + pltpu.roll(gram[rank : rank + SUB, :], rank, 1)
-    packed = gram[0:SUB, :]
-    for j in range(1, rank // SUB):
-        packed = packed + pltpu.roll(gram[SUB * j : SUB * (j + 1), :], rank * j, 1)
-    sums[SUB : 2 * SUB, :] = packed
+    gram[:, 0 : total.shape[1]] = total
+    half = rank // 2
+    lane = lax.broadcasted_iota(jnp.int32, (SUB, lanes), 1)
+    row = lax.broadcasted_iota(jnp.int32, (SUB, lanes), 0)
+    packed = None
+    for j in range(rank // SUB):
+        part = gram[SUB * j : SUB * (j + 1), :]
+        if SUB * j < half:
+            part = jnp.where(lane < half, 0.5 * part, jnp.where(lane < rank, part, 0.0))
+        else:
+            part = jnp.where((lane >= half) & (lane < rank), 0.5 * part, 0.0)
+        shift = pack_shift(j, rank)
+        packed = part if packed is None else packed + (pltpu.roll(part, shift, 1) if shift else part)
+    crossed = gram[rank : rank + SUB, :] + gram[rank + SUB : rank + 2 * SUB, :]
+    crossed = crossed + gram[rank + 2 * SUB : rank + 3 * SUB, :]
+    selves = crossed + pltpu.roll(crossed, lanes - SUB, 1) + pltpu.roll(crossed, lanes - 2 * SUB, 1)
+    first_lane = lanes - rank
+    crossed = pltpu.roll(crossed, first_lane, 1)
+    selves = pltpu.roll(pltpu.roll(selves, first_lane - rank, 1), count, 0)
+    tail = jnp.where(row < count, crossed, jnp.where(lane < first_lane + count, selves, 0.0))
+    packed = jnp.where(lane < first_lane, packed, tail)
+    if len(sums.shape) == 2:
+        sums[...] = packed
+    else:
+        for n in range(sums.shape[0]):
+            sums[n] = packed
+
+
+def pack_shift(j, rank):
+    half = rank // 2
+    if SUB * j < half:
+        return rank * j
+    return half // SUB * rank + half * (j - half // SUB) - half
 
 
 def finish_kernel(scale, count, rank, *refs):
     parts, (snaps, basis, coef, factor, modes, flag, gram) = refs[:-7], refs[-7:]
-    if len(parts) == 1:
-        total = tree_sum([parts[0][n] for n in range(parts[0].shape[0])])
+    if len(parts) == 1 and len(parts[0].shape) == 3:
+        packed = tree_sum([parts[0][n] for n in range(parts[0].shape[0])])
     else:
-        total = tree_sum([part[...] for part in parts])
-    lanes = total.shape[1]
-    head = total[0:SUB, :]
-    proj = head[:, 0:rank]
-    inner = pltpu.roll(head, lanes - rank, 1)[:, 0:SUB]
-    packed = total[SUB : 2 * SUB, :]
+        packed = tree_sum([part[...] for part in parts])
+    lanes = packed.shape[1]
+    half = rank // 2
+    lane = lax.broadcasted_iota(jnp.int32, (SUB, lanes), 1)
+    row = lax.broadcasted_iota(jnp.int32, (SUB, lanes), 0)
     for j in range(rank // SUB):
-        gram[SUB * j : SUB * (j + 1), :] = packed if j == 0 else pltpu.roll(packed, lanes - rank * j, 1)
-    modes2 = gram[:, 0:rank]
+        shift = pack_shift(j, rank)
+        part = pltpu.roll(packed, lanes - shift, 1) if shift else packed
+        if SUB * j >= half:
+            part = jnp.where(lane < half, 0.0, part)
+        gram[SUB * j : SUB * (j + 1), :] = part
+    tail = pltpu.roll(packed, rank, 1)
+    proj = jnp.where(row < count, tail, 0.0)[:, 0:rank]
+    inner = pltpu.roll(tail, SUB - count, 0)[:, 0:SUB]
     dot = functools.partial(lax.dot_general, precision=HIGHEST, preferred_element_type=jnp.float32)
-    turned = dot(proj, modes2, (((1,), (0,)), ((), ())))
+    turned = dot(proj, gram[:, 0:rank], (((1,), (0,)), ((), ())))
     crossed = dot(proj, proj, NT)
-    bent = dot(turned, proj, NT)
+    bent = dot(turned, proj, NT) + dot(proj, turned, NT)
     small = inner - 2.0 * crossed + bent
     r = lax.broadcasted_iota(jnp.int32, (SUB, SUB), 0)
     c = lax.broadcasted_iota(jnp.int32, (SUB, SUB), 1)
@@ -269,9 +296,12 @@
     flag[0, 0] = jnp.max(jnp.where(loss < 0.0, 0.0, 1.0)).astype(jnp.int32)
     coef[...] = proj[0:count, :]
     resid = []
+    thirds = [part.astype(jnp.bfloat16) for part in split3(proj)]
     for n in range(3):
-        mode = basis[n].astype(jnp.float32)
-        resid.append(snaps[n] - dot(proj, mode, (((1,), (0,)), ((), ()))))
+        value = snaps[n]
+        for third in thirds:
+            value = value - jnp.dot(third, basis[n], preferred_element_type=jnp.float32)
+        resid.append(value)
     small = jnp.where((r < count) & (c < count), small, jnp.where(r == c, 1.0, 0.0))
     below = lax.broadcasted_iota(jnp.int32, (SUB, 1), 0)
     pivots = jnp.ones((SUB, 1), jnp.float32)
@@ -386,55 +416,60 @@
     params = pltpu.CompilerParams(vmem_limit_bytes=VMEM_LIMIT)
 
     edge = jax.ShapeDtypeStruct((4, planes, HALO, lanes), f32)
+    hbm = pl.BlockSpec(memory_space=pltpu.HBM)
     top, bottom = pl.pallas_call(
-        edges_kernel, out_shape=(edge, edge), in_specs=[vmem] * 2, out_specs=(vmem, vmem), compiler_params=params
+        edges_kernel,
+        out_shape=(edge, edge),
+        in_specs=[hbm, hbm],
+        out_specs=(hbm, hbm),
+        scratch_shapes=[pltpu.SemaphoreType.DMA((4,))],
+        compiler_params=pltpu.CompilerParams(vmem_limit_bytes=62 * 1024 * 1024),
     )(density, velocity)
     upper = moved(top, "group", lambda i: (i + 1) % n_group)
     lower = moved(bottom, "group", lambda i: (i - 1) % n_group)
     wide_rows = rows + 2 * HALO
+    tiles = wide_rows // SUB
     own = pl.pallas_call(
         widen_kernel,
-        out_shape=jax.ShapeDtypeStruct((4, planes, wide_rows, lanes), f32),
+        out_shape=jax.ShapeDtypeStruct((4, planes, tiles, SUB, lanes), f32),
         in_specs=[vmem] * 4,
         out_specs=vmem,
+        scratch_shapes=[pltpu.VMEM((4, planes, wide_rows, lanes), f32)],
         compiler_params=params,
     )(density, velocity, upper, lower)
-
-    near = reach // planes
-    if n_dev == 2 * near + 2:
-        blocks = [lax.all_to_all(jnp.broadcast_to(own, (n_dev, *own.shape)), "dev", 0, 0)]
-        place = (lax.axis_index("dev") + jnp.arange(-near, near + 1, dtype=jnp.int32)) % n_dev
-    else:
-        blocks, place = ring_blocks(own, n_dev, planes, reach)
+    blocks, place = ring_blocks(own, n_dev, planes, reach)
     modes = jnp.transpose(basis[:, :, 0, :], (1, 0, 2))
     span = planes + 2 * reach
     width = basis.shape[3]
+    members = n_dev * n_group
+    at_once = members <= 32
     pops, snaps, sums = pl.pallas_call(
         lattice_kernel,
         out_shape=(
             jax.ShapeDtypeStruct((DIRS, planes, rows, lanes), f32),
             jax.ShapeDtypeStruct((3, SUB, width), f32),
-            jax.ShapeDtypeStruct((2 * SUB, lanes), f32),
+            jax.ShapeDtypeStruct((members, SUB, lanes) if at_once else (SUB, lanes), f32),
         ),
         in_specs=[smem, smem] + [vmem] * (len(blocks) + 1),
         out_specs=(vmem, vmem, vmem),
         scratch_shapes=[
-            pltpu.VMEM((span, 4, wide_rows, lanes), f32),
-            pltpu.VMEM((DIRS, span, wide_rows, lanes), f32),
-            pltpu.VMEM((DIRS, span, wide_rows, lanes), f32),
-            pltpu.VMEM((span, 3, rows, lanes), f32),
-            pltpu.VMEM((STEPS, 3, rows, lanes), f32),
-            pltpu.VMEM((3, SUB * rows, lanes), f32),
-            pltpu.VMEM((rank + SUB, lanes), f32),
+            pltpu.VMEM((DIRS, span, tiles, SUB, lanes), f32),
+            pltpu.VMEM((DIRS, span, tiles, SUB, lanes), f32),
+            pltpu.VMEM((span, 3, 2, SUB, lanes), f32),
+            pltpu.VMEM((STEPS, 3, 2, SUB, lanes), f32),
+            pltpu.VMEM((3 * SUB * SUB, lanes), f32),
+            pltpu.VMEM((rank + 4 * SUB, width), jnp.bfloat16),
+            pltpu.VMEM((rank + 4 * SUB, lanes), f32),
+            pltpu.VMEM((planes, DIRS, wide_rows, lanes), f32),
         ],
         compiler_params=params,
     )(place, snap_steps, *blocks, modes)
 
-    if n_dev * n_group <= 32:
-        parts = [lax.all_to_all(jnp.broadcast_to(sums, (n_dev * n_group, *sums.shape)), ("group", "dev"), 0, 0)]
+    if at_once:
+        parts = [lax.all_to_all(sums, ("group", "dev"), 0, 0)]
     else:
         parts = summed(sums, n_dev, n_group)
-    scale = math.sqrt(3 * width * n_dev * n_group)
+    scale = math.sqrt(3 * width * members)
     coef, factor, new_modes, flag = pl.pallas_call(
         functools.partial(finish_kernel, scale, count, rank),
         out_shape=(

time: 57.5 us -> 46.9 us (0.82)
  waiting for transfers between devices: 17.6 us -> 6.9 us
  Pallas kernels: 11.5 us -> 14.2 us
  local copies, waits for them, and re-layouts: 3.24 us -> 0.63 us
  starting transfers between devices: 8.96 us -> 9.79 us
  blocking collectives: 14.5 us -> 13.8 us
    all_to_all x1 -> x0, waiting for transfers between devices: 15.4 us -> none  [per_device(): lax.all_to_all(jnp.broadcast_to(own, (n_dev, *own.shape)), 'dev', 0, 0)]
    ppermute x2 -> x8, waiting for transfers between devices: 2.18 us -> 6.9 us  [moved(): lax.ppermute(block, axis, [(i, target(i)) for i in range(lax.axis_size(ax...]
    ppermute x2 -> x8, starting transfers between devices: 5.11 us -> 9.79 us  [moved(): lax.ppermute(block, axis, [(i, target(i)) for i in range(lax.axis_size(ax...]
    all_to_all x1 -> x0, starting transfers between devices: 3.85 us -> none  [per_device(): lax.all_to_all(jnp.broadcast_to(own, (n_dev, *own.shape)), 'dev', 0, 0)]
    pallas_call x2, Pallas kernels: 0.01 us -> 3.21 us  [the longest x1 3.19 us: per_device(): pl.pallas_call(edges_kernel, out_shape=(edge, edge), in_specs=[hbm, hbm],...]
    unnamed x14 -> x18, local copies, waits for them, and re-layouts: 2.12 us -> 0.63 us
    broadcast_in_dim x2 -> x0, local copies, waits for them, and re-layouts: 1.12 us -> none  [the longest x1 1.1 us: per_device(): jnp.broadcast_to(own, (n_dev, *own.shape))]
    all_to_all x1, blocking collectives: 14.5 us -> 13.8 us  [per_device(): parts = [lax.all_to_all(sums, ('group', 'dev'), 0, 0)]]
  transfers between devices with their start and end apart: 3 -> 8, of which waited for: 3 -> 6; matrix products, arithmetic and copies ran while one was open for 0% -> 0% of each run, Pallas kernels for 0% -> 0%
where the time goes in v3:
time: 46.9 us; the launch traced here: 46.7 us
  Pallas kernels  14.2 us (30%)
  blocking collectives  13.8 us (29%)
  starting transfers between devices  9.79 us (21%)
  waiting for transfers between devices  6.9 us (15%)
  between operations  1.4 us (3%)
  local copies, waits for them, and re-layouts  0.63 us (1%)
    all_to_all x1, blocking collectives, per_device(): parts = [lax.all_to_all(sums, ('group', 'dev'), 0, 0)]  13.8 us
    pallas_call x1, Pallas kernels, per_device(): pl.pallas_call(lattice_kernel, out_shape=(jax.ShapeDtypeStruct((DIRS, pla...  9.81 us
    ppermute x8, starting transfers between devices, moved(): lax.ppermute(block, axis, [(i, target(i)) for i in range(lax.axis_size(ax...  9.79 us
    ppermute x8, waiting for transfers between devices, moved(): lax.ppermute(block, axis, [(i, target(i)) for i in range(lax.axis_size(ax...  6.9 us
    pallas_call x1, Pallas kernels, per_device(): pl.pallas_call(edges_kernel, out_shape=(edge, edge), in_specs=[hbm, hbm],...  3.19 us
    pallas_call x1, Pallas kernels, per_device(): pl.pallas_call(functools.partial(finish_kernel, scale, count, rank), out_...  1.22 us
  transfers between devices with their start and end apart: 8, of which 6 were waited for; matrix products, arithmetic and copies ran while one was open for 0% of the time, Pallas kernels for 0%

profile of v3, /device:TPU:0, one launch (start us, length us, event | category | flops | bytes accessed | tf_op | source)
XLA Modules:
  0.0 46.7 jit_solution(7229671220521284711)
XLA Ops:
  0.6 0.0 copy-start
  0.6 0.0 copy-start.1
  0.7 3.2 %shard_map.93 = (f32[4,2,8,128]{3,2,1,0:T(8,128)}, f32[4,2,8,128]{3,2,1,0:T(8,128)}) custom-call(f32[2,16,128]{2,1,0:T(8,128)} %dens.3, f32[3,2,16,128]{3,2,1,0:T(8,128)} %vel.3), custom_call_target="tpu_custom_call" | custom-call | tf_op jit(solution)/shard_map/pallas_call | solution.py:420
  3.8 3.1 %collective-permute-start = (f32[4,2,8,128]{3,2,1,0:T(8,128)}, f32[4,2,8,128]{3,2,1,0:T(8,128)S(1)}, u32[]{:S(2)}, u32[]{:S(2)}) collective-permute-start(f32[4,2,8,128]{3,2,1,0:T(8,128)} %get-tuple-element.33), channel_id=1, source_target_pairs={{0,8},{8,16},{16,24},{24,0},{1,9},{9,17},{17,25},{25,1},{2,10},{10... | collective-permute-start | bytes 98312 | tf_op jit(solution)/shard_map/ppermute | solution.py:333
  6.9 2.1 %collective-permute-start.1 = (f32[4,2,8,128]{3,2,1,0:T(8,128)}, f32[4,2,8,128]{3,2,1,0:T(8,128)S(1)}, u32[]{:S(2)}, u32[]{:S(2)}) collective-permute-start(f32[4,2,8,128]{3,2,1,0:T(8,128)} %get-tuple-element.34), channel_id=1, source_target_pairs={{0,24},{8,0},{16,8},{24,16},{1,25},{9,1},{17,9},{25,17},{2,26},{10... | collective-permute-start | bytes 98312 | tf_op jit(solution)/shard_map/ppermute | solution.py:333
  9.0 2.1 %collective-permute-done.upper = f32[4,2,8,128]{3,2,1,0:T(8,128)S(1)} collective-permute-done((f32[4,2,8,128]{3,2,1,0:T(8,128)}, f32[4,2,8,128]{3,2,1,0:T(8,128)S(1)}, u32[]{:S(2)}, u32[]{:S(2)}) %collective-permute-start) | collective-permute-done | bytes 32800 | tf_op jit(solution)/shard_map/ppermute | solution.py:333
  11.2 0.2 collective-permute-done.1.lower
  11.4 0.0 copy-done
  11.4 0.0 copy-done.1
  11.4 1.5 %collective-permute-start.3 = (f32[4,2,4,8,128]{4,3,2,1,0:T(8,128)S(1)}, f32[4,2,4,8,128]{4,3,2,1,0:T(8,128)S(1)}, u32[]{:S(2)}, u32[]{:S(2)}) collective-permute-start(f32[4,2,4,8,128]{4,3,2,1,0:T(8,128)S(1)} %shard_map.94.refs_0_), channel_id=1, source_target_pairs={{0,2},{1,3},{2,4},{3,5},{4,6},{5,7},{6,0},{7,1},{8,10},{9,11},{10,... | collective-permute-start | bytes 393224 | tf_op jit(solution)/shard_map/ppermute | solution.py:333
  13.0 1.4 %collective-permute-start.2 = (f32[4,2,4,8,128]{4,3,2,1,0:T(8,128)S(1)}, f32[4,2,4,8,128]{4,3,2,1,0:T(8,128)S(1)}, u32[]{:S(2)}, u32[]{:S(2)}) collective-permute-start(f32[4,2,4,8,128]{4,3,2,1,0:T(8,128)S(1)} %shard_map.94.refs_0_), channel_id=1, source_target_pairs={{0,6},{1,7},{2,0},{3,1},{4,2},{5,3},{6,4},{7,5},{8,14},{9,15},{10,... | collective-permute-start | bytes 393224 | tf_op jit(solution)/shard_map/ppermute | solution.py:333
  14.4 0.0 collective-permute-start.5
  14.4 1.6 %collective-permute-start.4 = (f32[4,2,4,8,128]{4,3,2,1,0:T(8,128)S(1)}, f32[4,2,4,8,128]{4,3,2,1,0:T(8,128)S(1)}, u32[]{:S(2)}, u32[]{:S(2)}) collective-permute-start(f32[4,2,4,8,128]{4,3,2,1,0:T(8,128)S(1)} %shard_map.94.refs_0_), channel_id=1, source_target_pairs={{0,5},{1,4},{2,7},{3,6},{4,1},{5,0},{6,3},{7,2},{8,13},{9,12},{10,... | collective-permute-start | bytes 393224 | tf_op jit(solution)/shard_map/ppermute | solution.py:333
  16.0 1.8 %collective-permute-done.3.refs_2_ = f32[4,2,4,8,128]{4,3,2,1,0:T(8,128)S(1)} collective-permute-done((f32[4,2,4,8,128]{4,3,2,1,0:T(8,128)S(1)}, f32[4,2,4,8,128]{4,3,2,1,0:T(8,128)S(1)}, u32[]{:S(2)}, u32[]{:S(2)}) %collective-permute-start.3) | collective-permute-done | bytes 131104 | tf_op jit(solution)/shard_map/ppermute | solution.py:333
  17.9 0.0 collective-permute-start.7
  17.9 1.4 %collective-permute-done.2.refs_1_ = f32[4,2,4,8,128]{4,3,2,1,0:T(8,128)S(1)} collective-permute-done((f32[4,2,4,8,128]{4,3,2,1,0:T(8,128)S(1)}, f32[4,2,4,8,128]{4,3,2,1,0:T(8,128)S(1)}, u32[]{:S(2)}, u32[]{:S(2)}) %collective-permute-start.2) | collective-permute-done | bytes 131104 | tf_op jit(solution)/shard_map/ppermute | solution.py:333
  19.3 0.0 collective-permute-start.6
  19.3 0.0 copy-done.6
  19.3 0.0 copy-start.2
  19.3 0.0 collective-permute-done.5.refs_4_
  19.3 1.0 %collective-permute-done.4.refs_3_ = f32[4,2,4,8,128]{4,3,2,1,0:T(8,128)S(1)} collective-permute-done((f32[4,2,4,8,128]{4,3,2,1,0:T(8,128)S(1)}, f32[4,2,4,8,128]{4,3,2,1,0:T(8,128)S(1)}, u32[]{:S(2)}, u32[]{:S(2)}) %collective-permute-start.4) | collective-permute-done | bytes 131104 | tf_op jit(solution)/shard_map/ppermute | solution.py:333
  20.3 0.0 collective-permute-done.7.refs_6_
  20.3 0.3 collective-permute-done.6.refs_5_
  20.6 0.0 copy-done.3
  20.6 9.8 %shard_map.95 = (f32[19,2,16,128]{3,2,1,0:T(8,128)}, f32[3,8,512]{2,1,0:T(8,128)S(1)}, f32[32,8,128]{2,1,0:T(8,128)S(1)}) custom-call(s32[7]{0:T(128)S(1)} %fusion.9.place, s32[4]{0:T(128)S(1)} %copy-done.2, f32[4,2,4,8,128]{4,3,2,1,0:T(8,128)S(1)} %shard_map.94.refs_0_, f32[4,2,4,8,128]{4,3,2,1,0:T(8,128)S(1)} %collective-permute-done.2.refs_1_, ...), custom_call_target="tpu_custom_call" | custom-call | tf_op jit(solution)/shard_map/pallas_call | solution.py:446
  30.4 13.8 %all_to_all.5.refs_0_ = f32[32,8,128]{2,1,0:T(8,128)S(1)} all-to-all(f32[32,8,128]{2,1,0:T(8,128)S(1)} %get-tuple-element.36), channel_id=1, replica_groups=mesh['group'=4,'dev'=8] {'group','dev'}, dimensions={0} | all-to-all | bytes 262144 | tf_op jit(solution)/shard_map/all_to_all | solution.py:469
  44.2 1.2 %shard_map.96 = (f32[4,32]{1,0:T(4,128)S(1)}, f32[4,4]{1,0:T(4,128)S(1)}, f32[48,128]{1,0:T(8,128)S(1)}, s32[1,1]{1,0:T(1,128)}) custom-call(f32[32,8,128]{2,1,0:T(8,128)S(1)} %all_to_all.5.refs_0_, f32[3,8,512]{2,1,0:T(8,128)S(1)} %get-tuple-element.37.refs_1_, bf16[3,32,512]{2,1,0:T(8,128)(2,1)S(1)} %bitcast.41), custom_call_target="tpu_custom_call" | custom-call | tf_op jit(solution)/shard_map/pallas_call | solution.py:473
  45.4 0.0 copy-start.4
  46.1 0.0 copy-done.4
  46.1 0.0 copy-start.7
  46.1 0.0 copy-start.8
  46.1 0.6 %copy-done.7 = f32[4,3,1,512]{3,2,1,0:T(1,128)} copy-done((f32[4,3,1,512]{3,2,1,0:T(1,128)}, f32[4,3,1,512]{3,2,1,0:T(1,128)S(1)}, u32[]{:S(2)}) %copy-start.7) | copy-done | bytes 24600
  (9 shorter events, 0.0 us)
Async XLA Ops:
  0.6 10.8 %copy-start = (f32[3,2,16,128]{3,2,1,0:T(8,128)S(1)}, f32[3,2,16,128]{3,2,1,0:T(8,128)}, u32[]{:S(2)}) copy-start(f32[3,2,16,128]{3,2,1,0:T(8,128)} %vel.3) | copy-start | bytes 147460
  0.6 10.8 %copy-start.1 = (f32[2,16,128]{2,1,0:T(8,128)S(1)}, f32[2,16,128]{2,1,0:T(8,128)}, u32[]{:S(2)}) copy-start(f32[2,16,128]{2,1,0:T(8,128)} %dens.3) | copy-start | bytes 49156
  3.8 7.3 %collective-permute-start = (f32[4,2,8,128]{3,2,1,0:T(8,128)}, f32[4,2,8,128]{3,2,1,0:T(8,128)S(1)}, u32[]{:S(2)}, u32[]{:S(2)}) collective-permute-start(f32[4,2,8,128]{3,2,1,0:T(8,128)} %get-tuple-element.33), channel_id=1, source_target_pairs={{0,8},{8,16},{16,24},{24,0},{1,9},{9,17},{17,25},{25,1},{2,10},{10... | collective-permute-start | bytes 98312 | tf_op jit(solution)/shard_map/ppermute | solution.py:333
  6.9 13.7 %copy-start.3 = (bf16[32,3,1,512]{3,0,2,1:T(8,128)(2,1)S(1)}, bf16[32,3,1,512]{3,0,2,1:T(8,128)(2,1)}, u32[]{:S(2)}) copy-start(bf16[32,3,1,512]{3,0,2,1:T(8,128)(2,1)} %param.10) | copy-start | bytes 294916
  6.9 4.5 %collective-permute-start.1 = (f32[4,2,8,128]{3,2,1,0:T(8,128)}, f32[4,2,8,128]{3,2,1,0:T(8,128)S(1)}, u32[]{:S(2)}, u32[]{:S(2)}) collective-permute-start(f32[4,2,8,128]{3,2,1,0:T(8,128)} %get-tuple-element.34), channel_id=1, source_target_pairs={{0,24},{8,0},{16,8},{24,16},{1,25},{9,1},{17,9},{25,17},{2,26},{10... | collective-permute-start | bytes 98312 | tf_op jit(solution)/shard_map/ppermute | solution.py:333
  11.4 6.4 %collective-permute-start.3 = (f32[4,2,4,8,128]{4,3,2,1,0:T(8,128)S(1)}, f32[4,2,4,8,128]{4,3,2,1,0:T(8,128)S(1)}, u32[]{:S(2)}, u32[]{:S(2)}) collective-permute-start(f32[4,2,4,8,128]{4,3,2,1,0:T(8,128)S(1)} %shard_map.94.refs_0_), channel_id=1, source_target_pairs={{0,2},{1,3},{2,4},{3,5},{4,6},{5,7},{6,0},{7,1},{8,10},{9,11},{10,... | collective-permute-start | bytes 393224 | tf_op jit(solution)/shard_map/ppermute | solution.py:333
  13.0 6.3 %collective-permute-start.2 = (f32[4,2,4,8,128]{4,3,2,1,0:T(8,128)S(1)}, f32[4,2,4,8,128]{4,3,2,1,0:T(8,128)S(1)}, u32[]{:S(2)}, u32[]{:S(2)}) collective-permute-start(f32[4,2,4,8,128]{4,3,2,1,0:T(8,128)S(1)} %shard_map.94.refs_0_), channel_id=1, source_target_pairs={{0,6},{1,7},{2,0},{3,1},{4,2},{5,3},{6,4},{7,5},{8,14},{9,15},{10,... | collective-permute-start | bytes 393224 | tf_op jit(solution)/shard_map/ppermute | solution.py:333
  14.4 4.9 %copy-start.5 = (s32[7]{0:T(128)S(1)}, s32[7]{0:T(128)}, u32[]{:S(2)}) copy-start(s32[7]{0:T(128)} %constant.71.clone) | copy-start | bytes 88
  14.4 4.9 %copy-start.6 = (s32[7]{0:T(128)S(1)}, s32[7]{0:T(128)}, u32[]{:S(2)}) copy-start(s32[7]{0:T(128)} %constant.70.clone) | copy-start | bytes 88
  14.4 4.9 %collective-permute-start.5 = (f32[4,2,4,8,128]{4,3,2,1,0:T(8,128)S(1)}, f32[4,2,4,8,128]{4,3,2,1,0:T(8,128)S(1)}, u32[]{:S(2)}, u32[]{:S(2)}) collective-permute-start(f32[4,2,4,8,128]{4,3,2,1,0:T(8,128)S(1)} %shard_map.94.refs_0_), channel_id=1, source_target_pairs={{0,1},{1,0},{2,3},{3,2},{4,5},{5,4},{6,7},{7,6},{8,9},{9,8},{10,11... | collective-permute-start | bytes 393224 | tf_op jit(solution)/shard_map/ppermute | solution.py:333
  14.4 5.9 %collective-permute-start.4 = (f32[4,2,4,8,128]{4,3,2,1,0:T(8,128)S(1)}, f32[4,2,4,8,128]{4,3,2,1,0:T(8,128)S(1)}, u32[]{:S(2)}, u32[]{:S(2)}) collective-permute-start(f32[4,2,4,8,128]{4,3,2,1,0:T(8,128)S(1)} %shard_map.94.refs_0_), channel_id=1, source_target_pairs={{0,5},{1,4},{2,7},{3,6},{4,1},{5,0},{6,3},{7,2},{8,13},{9,12},{10,... | collective-permute-start | bytes 393224 | tf_op jit(solution)/shard_map/ppermute | solution.py:333
  17.9 2.5 %collective-permute-start.7 = (f32[4,2,4,8,128]{4,3,2,1,0:T(8,128)S(1)}, f32[4,2,4,8,128]{4,3,2,1,0:T(8,128)S(1)}, u32[]{:S(2)}, u32[]{:S(2)}) collective-permute-start(f32[4,2,4,8,128]{4,3,2,1,0:T(8,128)S(1)} %collective-permute-done.3.refs_2_), channel_id=1, source_target_pairs={{0,1},{1,0},{2,3},{3,2},{4,5},{5,4},{6,7},{7,6},{8,9},{9,8},{10,11... | collective-permute-start | bytes 393224 | tf_op jit(solution)/shard_map/ppermute | solution.py:333
  19.3 1.3 %collective-permute-start.6 = (f32[4,2,4,8,128]{4,3,2,1,0:T(8,128)S(1)}, f32[4,2,4,8,128]{4,3,2,1,0:T(8,128)S(1)}, u32[]{:S(2)}, u32[]{:S(2)}) collective-permute-start(f32[4,2,4,8,128]{4,3,2,1,0:T(8,128)S(1)} %collective-permute-done.2.refs_1_), channel_id=1, source_target_pairs={{0,1},{1,0},{2,3},{3,2},{4,5},{5,4},{6,7},{7,6},{8,9},{9,8},{10,11... | collective-permute-start | bytes 393224 | tf_op jit(solution)/shard_map/ppermute | solution.py:333
  19.3 1.3 %copy-start.2 = (s32[4]{0:T(128)S(1)}, s32[4]{0:T(128)}, u32[]{:S(2)}) copy-start(s32[4]{0:T(128)} %snap_steps.1) | copy-start | bytes 52
  45.4 0.7 %copy-start.4 = (f32[4,32]{1,0:T(4,128)}, f32[4,32]{1,0:T(4,128)S(1)}, u32[]{:S(2)}) copy-start(f32[4,32]{1,0:T(4,128)S(1)} %get-tuple-element.38) | copy-start | bytes 1540
  46.1 0.6 %copy-start.7 = (f32[4,3,1,512]{3,2,1,0:T(1,128)}, f32[4,3,1,512]{3,2,1,0:T(1,128)S(1)}, u32[]{:S(2)}) copy-start(f32[4,3,1,512]{3,2,1,0:T(1,128)S(1)} %get-tuple-element.65) | copy-start | bytes 73732
  46.1 0.6 %copy-start.8 = (f32[4,4]{1,0:T(4,128)}, f32[4,4]{1,0:T(4,128)S(1)}, u32[]{:S(2)}) copy-start(f32[4,4]{1,0:T(4,128)S(1)} %get-tuple-element.64) | copy-start | bytes 196

commit v4 on v3

--- a/solution.py
+++ b/solution.py
@@ -19,6 +19,7 @@
 SUB = 8
 LANES = 128
 HALO = 8
+AT_ONCE = 2
 HIGHEST = lax.Precision.HIGHEST
 NT = (((1,), (1,)), ((), ()))
 VMEM_LIMIT = 48 * 1024 * 1024
@@ -63,11 +64,8 @@
 
 
 def moments(pops):
-    dens = pops[0]
-    diff = {}
-    for a, b in OPPOSITE:
-        dens = dens + (pops[a] + pops[b])
-        diff[a] = pops[a] - pops[b]
+    dens = tree_sum([pops[0]] + [pops[a] + pops[b] for a, b in OPPOSITE])
+    diff = {a: pops[a] - pops[b] for a, b in OPPOSITE}
     mom = []
     for table in (DIR_X, DIR_Y, DIR_Z):
         total = None
@@ -82,6 +80,12 @@
     return dens, mom
 
 
+def reciprocal(value):
+    near = pl.reciprocal(value, approx=True)
+    near = near * (2.0 - value * near)
+    return near * (2.0 - value * near)
+
+
 def streamed(src, x, tiles):
     def get(i, t):
         at = t - DIR_Y[i]
@@ -95,30 +99,17 @@
     return get
 
 
-def edges_kernel(dens, vel, top, bottom, sems):
-    rows = dens.shape[1]
-    last, first = pl.ds(rows - HALO, HALO), pl.ds(0, HALO)
-    copies = [
-        pltpu.make_async_copy(dens.at[:, last, :], top.at[0], sems.at[0]),
-        pltpu.make_async_copy(vel.at[:, :, last, :], top.at[pl.ds(1, 3)], sems.at[1]),
-        pltpu.make_async_copy(dens.at[:, first, :], bottom.at[0], sems.at[2]),
-        pltpu.make_async_copy(vel.at[:, :, first, :], bottom.at[pl.ds(1, 3)], sems.at[3]),
-    ]
-    for copy in copies:
-        copy.start()
-    for copy in copies:
-        copy.wait()
-
-
-def widen_kernel(dens, vel, upper, lower, wide, whole):
-    planes, rows, _ = dens.shape
-    whole[:, :, :HALO, :] = upper[...]
-    whole[:, :, HALO + rows :, :] = lower[...]
-    whole[0, :, HALO : HALO + rows, :] = dens[...]
+def widen_kernel(held, up_dens, up_vel, low_dens, low_vel, wide, whole):
+    fields, planes, rows, _ = held.shape
+    below = HALO + rows
+    whole[0, :, :HALO, :] = up_dens[:, rows - HALO :, :]
+    whole[0, :, below:, :] = low_dens[:, :HALO, :]
+    for c in range(3):
+        whole[c + 1, :, :HALO, :] = up_vel[c, :, rows - HALO :, :]
+        whole[c + 1, :, below:, :] = low_vel[c, :, :HALO, :]
+    whole[:, :, HALO:below, :] = held[...]
     tiles = wide.shape[2]
-    for c in range(3):
-        whole[c + 1, :, HALO : HALO + rows, :] = vel[c]
-    for f in range(4):
+    for f in range(fields):
         for p in range(planes):
             for t in range(tiles):
                 wide[f, p, t] = whole[f, p, pl.ds(t, SUB, stride=tiles), :]
@@ -132,8 +123,8 @@
 
 
 def lattice_kernel(place, snap_steps, *refs):
-    blocks, refs = refs[:-12], refs[-12:]
-    basis, pops, snaps, sums, ping, pong, speeds, views, coarse, rowwise, gram, whole = refs
+    blocks, refs = refs[:-13], refs[-13:]
+    basis, pops, snaps, sums, ping, pong, speeds, views, coarse, rowwise, gram, whole, sems = refs
     planes, tiles, _, lanes = blocks[0].shape[1:]
     reach = STEPS
     span = planes + 2 * reach
@@ -155,9 +146,8 @@
                 views[step, c, half] = total
 
     for n, block in enumerate(blocks):
-        start = place[n]
-
-        def first(p, carry, block=block, start=start):
+        for p in range(planes):
+            x = place[n] + p
             held = []
             for t in range(tiles):
                 dens = block[0, p, t]
@@ -166,43 +156,45 @@
                 speed = [1.5 * v for v in vel]
                 out = relaxed(1.0, dens, [part * v for v in vel], speed, None)
                 for i in range(DIRS):
-                    ping[i, start + p, t] = out[i]
+                    ping[i, x, t] = out[i]
                 held.append(speed)
-            put_speed(start + p, held)
-            return carry
-
-        lax.fori_loop(0, planes, first, 0)
+            put_speed(x, held)
     keep_view(0)
 
     src, dst = ping, pong
     for step in range(1, STEPS):
-
-        def later(x, carry, src=src, dst=dst):
-            get = streamed(src, x, tiles)
-            held = []
-            for t in range(tiles):
-                pop = [get(i, t) for i in range(DIRS)]
-                dens, mom = moments(pop)
-                inverse = 1.5 / dens
-                speed = [m * inverse for m in mom]
-                flow = [m * (OMEGA * 3.0 / 36.0) for m in mom]
-                out = relaxed(OMEGA, dens, flow, speed, pop)
-                for i in range(DIRS):
-                    dst[i, x, t] = out[i]
-                held.append(speed)
-            put_speed(x, held)
+        size = span - 2 * step
+        together = math.gcd(size, AT_ONCE)
+
+        def later(n, carry, src=src, dst=dst, step=step, together=together):
+            for x in [step + together * n + m for m in range(together)]:
+                get = streamed(src, x, tiles)
+                held = []
+                for t in range(tiles):
+                    pop = [get(i, t) for i in range(DIRS)]
+                    dens, mom = moments(pop)
+                    inverse = 1.5 * reciprocal(dens)
+                    speed = [m * inverse for m in mom]
+                    flow = [m * (OMEGA * 3.0 / 36.0) for m in mom]
+                    out = relaxed(OMEGA, dens, flow, speed, pop)
+                    for i in range(DIRS):
+                        dst[i, x, t] = out[i]
+                    held.append(speed)
+                put_speed(x, held)
             return carry
 
-        lax.fori_loop(step, span - step, later, 0)
+        lax.fori_loop(0, size // together, later, 0)
         keep_view(step)
         src, dst = dst, src
 
+    copies = []
     for p in range(planes):
         get = streamed(src, reach + p, tiles)
         for i in range(DIRS):
             for t in range(tiles):
                 whole[p, i, pl.ds(t, SUB, stride=tiles), :] = get(i, t)
-            pops[i, p] = whole[p, i, HALO : HALO + rows, :]
+        copies.append(pltpu.make_async_copy(whole.at[p, :, pl.ds(HALO, rows), :], pops.at[:, p], sems.at[p]))
+        copies[-1].start()
 
     halves = [[views[snap_steps[k], c, half] for k in range(count) for c in range(3)] for half in range(2)]
     lane = lax.broadcasted_iota(jnp.int32, (lanes, lanes), 0) // 2
@@ -257,6 +249,8 @@
     else:
         for n in range(sums.shape[0]):
             sums[n] = packed
+    for copy in copies:
+        copy.wait()
 
 
 def pack_shift(j, rank):
@@ -415,28 +409,21 @@
     f32 = jnp.float32
     params = pltpu.CompilerParams(vmem_limit_bytes=VMEM_LIMIT)
 
-    edge = jax.ShapeDtypeStruct((4, planes, HALO, lanes), f32)
-    hbm = pl.BlockSpec(memory_space=pltpu.HBM)
-    top, bottom = pl.pallas_call(
-        edges_kernel,
-        out_shape=(edge, edge),
-        in_specs=[hbm, hbm],
-        out_specs=(hbm, hbm),
-        scratch_shapes=[pltpu.SemaphoreType.DMA((4,))],
-        compiler_params=pltpu.CompilerParams(vmem_limit_bytes=62 * 1024 * 1024),
-    )(density, velocity)
-    upper = moved(top, "group", lambda i: (i + 1) % n_group)
-    lower = moved(bottom, "group", lambda i: (i - 1) % n_group)
+    up = lambda i: (i + 1) % n_group
+    down = lambda i: (i - 1) % n_group
+    held = jnp.concatenate([density[None], velocity])
+    upper = [moved(array, "group", up) for array in (density, velocity)]
+    lower = [moved(array, "group", down) for array in (density, velocity)]
     wide_rows = rows + 2 * HALO
     tiles = wide_rows // SUB
     own = pl.pallas_call(
         widen_kernel,
         out_shape=jax.ShapeDtypeStruct((4, planes, tiles, SUB, lanes), f32),
-        in_specs=[vmem] * 4,
+        in_specs=[vmem] * 5,
         out_specs=vmem,
         scratch_shapes=[pltpu.VMEM((4, planes, wide_rows, lanes), f32)],
         compiler_params=params,
-    )(density, velocity, upper, lower)
+    )(held, *upper, *lower)
     blocks, place = ring_blocks(own, n_dev, planes, reach)
     modes = jnp.transpose(basis[:, :, 0, :], (1, 0, 2))
     span = planes + 2 * reach
@@ -451,7 +438,7 @@
             jax.ShapeDtypeStruct((members, SUB, lanes) if at_once else (SUB, lanes), f32),
         ),
         in_specs=[smem, smem] + [vmem] * (len(blocks) + 1),
-        out_specs=(vmem, vmem, vmem),
+        out_specs=(pl.BlockSpec(memory_space=pltpu.HBM), vmem, vmem),
         scratch_shapes=[
             pltpu.VMEM((DIRS, span, tiles, SUB, lanes), f32),
             pltpu.VMEM((DIRS, span, tiles, SUB, lanes), f32),
@@ -461,6 +448,7 @@
             pltpu.VMEM((rank + 4 * SUB, width), jnp.bfloat16),
             pltpu.VMEM((rank + 4 * SUB, lanes), f32),
             pltpu.VMEM((planes, DIRS, wide_rows, lanes), f32),
+            pltpu.SemaphoreType.DMA((planes,)),
         ],
         compiler_params=params,
     )(place, snap_steps, *blocks, modes)

time: 46.9 us -> 46.4 us (0.989)
  Pallas kernels: 14.2 us -> 9.17 us
  starting transfers between devices: 9.79 us -> 13.5 us
  blocking collectives: 13.8 us -> 11.3 us
  waiting for transfers between devices: 6.9 us -> 9.28 us
  other arithmetic: 0.01 us -> 0.88 us
    ppermute x8 -> x10, starting transfers between devices: 9.79 us -> 13.5 us  [moved(): lax.ppermute(block, axis, [(i, target(i)) for i in range(lax.axis_size(ax...]
    pallas_call x1 -> x0, Pallas kernels: 3.19 us -> none  [per_device(): pl.pallas_call(edges_kernel, out_shape=(edge, edge), in_specs=[hbm, hbm],...]
    all_to_all x1, blocking collectives: 13.8 us -> 11.3 us  [per_device(): parts = [lax.all_to_all(sums, ('group', 'dev'), 0, 0)]]
    ppermute x8 -> x10, waiting for transfers between devices: 6.9 us -> 9.28 us  [moved(): lax.ppermute(block, axis, [(i, target(i)) for i in range(lax.axis_size(ax...]
    pallas_call x1, Pallas kernels: 9.81 us -> 7.93 us  [per_device(): pl.pallas_call(lattice_kernel, out_shape=(jax.ShapeDtypeStruct((DIRS, pla...]
    concatenate x0 -> x1, other arithmetic: none -> 0.87 us  [per_device(): held = jnp.concatenate([density[None], velocity])]
  transfers between devices with their start and end apart: 8 -> 10, of which waited for: 6 -> 7; matrix products, arithmetic and copies ran while one was open for 0% -> 2% of each run, Pallas kernels for 0% -> 0%
where the time goes in v4:
time: 46.4 us; the launch traced here: 46.2 us
  starting transfers between devices  13.5 us (29%)
  blocking collectives  11.3 us (24%)
  waiting for transfers between devices  9.28 us (20%)
  Pallas kernels  9.17 us (20%)
  between operations  1.38 us (3%)
  other arithmetic  0.88 us (2%)
  local copies, waits for them, and re-layouts  0.62 us (1%)
    ppermute x10, starting transfers between devices, moved(): lax.ppermute(block, axis, [(i, target(i)) for i in range(lax.axis_size(ax...  13.5 us
    all_to_all x1, blocking collectives, per_device(): parts = [lax.all_to_all(sums, ('group', 'dev'), 0, 0)]  11.3 us
    ppermute x10, waiting for transfers between devices, moved(): lax.ppermute(block, axis, [(i, target(i)) for i in range(lax.axis_size(ax...  9.28 us
    pallas_call x1, Pallas kernels, per_device(): pl.pallas_call(lattice_kernel, out_shape=(jax.ShapeDtypeStruct((DIRS, pla...  7.93 us
    pallas_call x1, Pallas kernels, per_device(): pl.pallas_call(functools.partial(finish_kernel, scale, count, rank), out_...  1.22 us
  transfers between devices with their start and end apart: 10, of which 7 were waited for; matrix products, arithmetic and copies ran while one was open for 2% of the time, Pallas kernels for 0%

profile of v4, /device:TPU:0, one launch (start us, length us, event | category | flops | bytes accessed | tf_op | source)
XLA Modules:
  0.0 46.2 jit_solution(490493366285275433)
XLA Ops:
  0.6 5.1 %collective-permute-start.2 = (f32[2,16,128]{2,1,0:T(8,128)}, f32[2,16,128]{2,1,0:T(8,128)S(1)}, u32[]{:S(2)}, u32[]{:S(2)}) collective-permute-start(f32[2,16,128]{2,1,0:T(8,128)} %param.8), channel_id=1, source_target_pairs={{0,24},{8,0},{16,8},{24,16},{1,25},{9,1},{17,9},{25,17},{2,26},{10... | collective-permute-start | bytes 49160 | tf_op jit(solution)/shard_map/ppermute | solution.py:327
  5.7 0.0 collective-permute-start
  5.7 3.8 %collective-permute-start.3 = (f32[3,2,16,128]{3,2,1,0:T(8,128)}, f32[3,2,16,128]{3,2,1,0:T(8,128)S(1)}, u32[]{:S(2)}, u32[]{:S(2)}) collective-permute-start(f32[3,2,16,128]{3,2,1,0:T(8,128)} %param.9), channel_id=1, source_target_pairs={{0,24},{8,0},{16,8},{24,16},{1,25},{9,1},{17,9},{25,17},{2,26},{10... | collective-permute-start | bytes 147464 | tf_op jit(solution)/shard_map/ppermute | solution.py:327
  9.6 0.0 collective-permute-start.1
  9.6 0.9 %pad_maximum_fusion.held = f32[4,2,16,128]{3,2,1,0:T(8,128)S(1)} fusion(f32[3,2,16,128]{3,2,1,0:T(8,128)} %param.9, f32[1,2,16,128]{3,2,1,0:T(8,128)} %bitcast.46), kind=kLoop, calls=%fused_computation.23 | loop fusion | flops 16384 | bytes 131072 | tf_op jit(solution)/shard_map/concatenate | solution.py:414
  10.4 0.0 collective-permute-done.2.low_dens
  10.4 1.0 %collective-permute-done.up_dens = f32[2,16,128]{2,1,0:T(8,128)S(1)} collective-permute-done((f32[2,16,128]{2,1,0:T(8,128)}, f32[2,16,128]{2,1,0:T(8,128)S(1)}, u32[]{:S(2)}, u32[]{:S(2)}) %collective-permute-start) | collective-permute-done | bytes 16416 | tf_op jit(solution)/shard_map/ppermute | solution.py:327
  11.5 0.1 collective-permute-done.3.low_vel
  11.6 4.0 %collective-permute-done.1.up_vel = f32[3,2,16,128]{3,2,1,0:T(8,128)S(1)} collective-permute-done((f32[3,2,16,128]{3,2,1,0:T(8,128)}, f32[3,2,16,128]{3,2,1,0:T(8,128)S(1)}, u32[]{:S(2)}, u32[]{:S(2)}) %collective-permute-start.1) | collective-permute-done | bytes 49184 | tf_op jit(solution)/shard_map/ppermute | solution.py:327
  15.7 1.5 %collective-permute-start.5 = (f32[4,2,4,8,128]{4,3,2,1,0:T(8,128)S(1)}, f32[4,2,4,8,128]{4,3,2,1,0:T(8,128)S(1)}, u32[]{:S(2)}, u32[]{:S(2)}) collective-permute-start(f32[4,2,4,8,128]{4,3,2,1,0:T(8,128)S(1)} %shard_map.93.refs_0_), channel_id=1, source_target_pairs={{0,2},{1,3},{2,4},{3,5},{4,6},{5,7},{6,0},{7,1},{8,10},{9,11},{10,... | collective-permute-start | bytes 393224 | tf_op jit(solution)/shard_map/ppermute | solution.py:327
  17.2 1.4 %collective-permute-start.4 = (f32[4,2,4,8,128]{4,3,2,1,0:T(8,128)S(1)}, f32[4,2,4,8,128]{4,3,2,1,0:T(8,128)S(1)}, u32[]{:S(2)}, u32[]{:S(2)}) collective-permute-start(f32[4,2,4,8,128]{4,3,2,1,0:T(8,128)S(1)} %shard_map.93.refs_0_), channel_id=1, source_target_pairs={{0,6},{1,7},{2,0},{3,1},{4,2},{5,3},{6,4},{7,5},{8,14},{9,15},{10,... | collective-permute-start | bytes 393224 | tf_op jit(solution)/shard_map/ppermute | solution.py:327
  18.7 0.0 collective-permute-start.7
  18.7 1.6 %collective-permute-start.6 = (f32[4,2,4,8,128]{4,3,2,1,0:T(8,128)S(1)}, f32[4,2,4,8,128]{4,3,2,1,0:T(8,128)S(1)}, u32[]{:S(2)}, u32[]{:S(2)}) collective-permute-start(f32[4,2,4,8,128]{4,3,2,1,0:T(8,128)S(1)} %shard_map.93.refs_0_), channel_id=1, source_target_pairs={{0,5},{1,4},{2,7},{3,6},{4,1},{5,0},{6,3},{7,2},{8,13},{9,12},{10,... | collective-permute-start | bytes 393224 | tf_op jit(solution)/shard_map/ppermute | solution.py:327
  20.3 1.3 %collective-permute-done.5.refs_2_ = f32[4,2,4,8,128]{4,3,2,1,0:T(8,128)S(1)} collective-permute-done((f32[4,2,4,8,128]{4,3,2,1,0:T(8,128)S(1)}, f32[4,2,4,8,128]{4,3,2,1,0:T(8,128)S(1)}, u32[]{:S(2)}, u32[]{:S(2)}) %collective-permute-start.5) | collective-permute-done | bytes 131104 | tf_op jit(solution)/shard_map/ppermute | solution.py:327
  21.6 0.0 collective-permute-start.9
  21.6 1.5 %collective-permute-done.4.refs_1_ = f32[4,2,4,8,128]{4,3,2,1,0:T(8,128)S(1)} collective-permute-done((f32[4,2,4,8,128]{4,3,2,1,0:T(8,128)S(1)}, f32[4,2,4,8,128]{4,3,2,1,0:T(8,128)S(1)}, u32[]{:S(2)}, u32[]{:S(2)}) %collective-permute-start.4) | collective-permute-done | bytes 131104 | tf_op jit(solution)/shard_map/ppermute | solution.py:327
  23.1 0.0 collective-permute-start.8
  23.1 0.0 copy-done.3
  23.1 0.0 copy-start
  23.1 0.0 collective-permute-done.7.refs_4_
  23.1 0.7 %collective-permute-done.6.refs_3_ = f32[4,2,4,8,128]{4,3,2,1,0:T(8,128)S(1)} collective-permute-done((f32[4,2,4,8,128]{4,3,2,1,0:T(8,128)S(1)}, f32[4,2,4,8,128]{4,3,2,1,0:T(8,128)S(1)}, u32[]{:S(2)}, u32[]{:S(2)}) %collective-permute-start.6) | collective-permute-done | bytes 131104 | tf_op jit(solution)/shard_map/ppermute | solution.py:327
  23.8 0.0 collective-permute-done.9.refs_6_
  23.8 0.6 %collective-permute-done.8.refs_5_ = f32[4,2,4,8,128]{4,3,2,1,0:T(8,128)S(1)} collective-permute-done((f32[4,2,4,8,128]{4,3,2,1,0:T(8,128)S(1)}, f32[4,2,4,8,128]{4,3,2,1,0:T(8,128)S(1)}, u32[]{:S(2)}, u32[]{:S(2)}) %collective-permute-start.8) | collective-permute-done | bytes 131104 | tf_op jit(solution)/shard_map/ppermute | solution.py:327
  24.4 0.0 copy-done
  24.4 7.9 %shard_map.94 = (f32[19,2,16,128]{3,2,1,0:T(8,128)}, f32[3,8,512]{2,1,0:T(8,128)S(1)}, f32[32,8,128]{2,1,0:T(8,128)S(1)}) custom-call(s32[7]{0:T(128)S(1)} %fusion.9.place, s32[4]{0:T(128)S(1)} %copy-done, f32[4,2,4,8,128]{4,3,2,1,0:T(8,128)S(1)} %shard_map.93.refs_0_, f32[4,2,4,8,128]{4,3,2,1,0:T(8,128)S(1)} %collective-permute-done.4.refs_1_, ...), custom_call_target="tpu_custom_call" | custom-call | tf_op jit(solution)/shard_map/pallas_call | solution.py:433
  32.4 11.3 %all_to_all.5.refs_0_ = f32[32,8,128]{2,1,0:T(8,128)S(1)} all-to-all(f32[32,8,128]{2,1,0:T(8,128)S(1)} %get-tuple-element.32), channel_id=1, replica_groups=mesh['group'=4,'dev'=8] {'group','dev'}, dimensions={0} | all-to-all | bytes 262144 | tf_op jit(solution)/shard_map/all_to_all | solution.py:457
  43.6 1.2 %shard_map.95 = (f32[4,32]{1,0:T(4,128)S(1)}, f32[4,4]{1,0:T(4,128)S(1)}, f32[48,128]{1,0:T(8,128)S(1)}, s32[1,1]{1,0:T(1,128)}) custom-call(f32[32,8,128]{2,1,0:T(8,128)S(1)} %all_to_all.5.refs_0_, f32[3,8,512]{2,1,0:T(8,128)S(1)} %get-tuple-element.33.refs_1_, bf16[3,32,512]{2,1,0:T(8,128)(2,1)S(1)} %bitcast.42), custom_call_target="tpu_custom_call" | custom-call | tf_op jit(solution)/shard_map/pallas_call | solution.py:461
  44.9 0.0 copy-start.2
  45.5 0.0 copy-done.2
  45.6 0.0 copy-start.5
  45.6 0.0 copy-start.6
  45.6 0.6 %copy-done.5 = f32[4,3,1,512]{3,2,1,0:T(1,128)} copy-done((f32[4,3,1,512]{3,2,1,0:T(1,128)}, f32[4,3,1,512]{3,2,1,0:T(1,128)S(1)}, u32[]{:S(2)}) %copy-start.5) | copy-done | bytes 24600
  (9 shorter events, 0.0 us)
Async XLA Ops:
  0.6 9.8 %collective-permute-start.2 = (f32[2,16,128]{2,1,0:T(8,128)}, f32[2,16,128]{2,1,0:T(8,128)S(1)}, u32[]{:S(2)}, u32[]{:S(2)}) collective-permute-start(f32[2,16,128]{2,1,0:T(8,128)} %param.8), channel_id=1, source_target_pairs={{0,24},{8,0},{16,8},{24,16},{1,25},{9,1},{17,9},{25,17},{2,26},{10... | collective-permute-start | bytes 49160 | tf_op jit(solution)/shard_map/ppermute | solution.py:327
  5.7 5.7 %collective-permute-start = (f32[2,16,128]{2,1,0:T(8,128)}, f32[2,16,128]{2,1,0:T(8,128)S(1)}, u32[]{:S(2)}, u32[]{:S(2)}) collective-permute-start(f32[2,16,128]{2,1,0:T(8,128)} %param.8), channel_id=1, source_target_pairs={{0,8},{8,16},{16,24},{24,0},{1,9},{9,17},{17,25},{25,1},{2,10},{10... | collective-permute-start | bytes 49160 | tf_op jit(solution)/shard_map/ppermute | solution.py:327
  5.7 5.9 %collective-permute-start.3 = (f32[3,2,16,128]{3,2,1,0:T(8,128)}, f32[3,2,16,128]{3,2,1,0:T(8,128)S(1)}, u32[]{:S(2)}, u32[]{:S(2)}) collective-permute-start(f32[3,2,16,128]{3,2,1,0:T(8,128)} %param.9), channel_id=1, source_target_pairs={{0,24},{8,0},{16,8},{24,16},{1,25},{9,1},{17,9},{25,17},{2,26},{10... | collective-permute-start | bytes 147464 | tf_op jit(solution)/shard_map/ppermute | solution.py:327
  9.6 6.1 %collective-permute-start.1 = (f32[3,2,16,128]{3,2,1,0:T(8,128)}, f32[3,2,16,128]{3,2,1,0:T(8,128)S(1)}, u32[]{:S(2)}, u32[]{:S(2)}) collective-permute-start(f32[3,2,16,128]{3,2,1,0:T(8,128)} %param.9), channel_id=1, source_target_pairs={{0,8},{8,16},{16,24},{24,0},{1,9},{9,17},{17,25},{25,1},{2,10},{10... | collective-permute-start | bytes 147464 | tf_op jit(solution)/shard_map/ppermute | solution.py:327
  15.7 8.8 %copy-start.1 = (bf16[32,3,1,512]{3,0,2,1:T(8,128)(2,1)S(1)}, bf16[32,3,1,512]{3,0,2,1:T(8,128)(2,1)}, u32[]{:S(2)}) copy-start(bf16[32,3,1,512]{3,0,2,1:T(8,128)(2,1)} %param.10) | copy-start | bytes 294916
  15.7 5.9 %collective-permute-start.5 = (f32[4,2,4,8,128]{4,3,2,1,0:T(8,128)S(1)}, f32[4,2,4,8,128]{4,3,2,1,0:T(8,128)S(1)}, u32[]{:S(2)}, u32[]{:S(2)}) collective-permute-start(f32[4,2,4,8,128]{4,3,2,1,0:T(8,128)S(1)} %shard_map.93.refs_0_), channel_id=1, source_target_pairs={{0,2},{1,3},{2,4},{3,5},{4,6},{5,7},{6,0},{7,1},{8,10},{9,11},{10,... | collective-permute-start | bytes 393224 | tf_op jit(solution)/shard_map/ppermute | solution.py:327
  17.2 5.8 %collective-permute-start.4 = (f32[4,2,4,8,128]{4,3,2,1,0:T(8,128)S(1)}, f32[4,2,4,8,128]{4,3,2,1,0:T(8,128)S(1)}, u32[]{:S(2)}, u32[]{:S(2)}) collective-permute-start(f32[4,2,4,8,128]{4,3,2,1,0:T(8,128)S(1)} %shard_map.93.refs_0_), channel_id=1, source_target_pairs={{0,6},{1,7},{2,0},{3,1},{4,2},{5,3},{6,4},{7,5},{8,14},{9,15},{10,... | collective-permute-start | bytes 393224 | tf_op jit(solution)/shard_map/ppermute | solution.py:327
  18.7 4.4 %copy-start.3 = (s32[7]{0:T(128)S(1)}, s32[7]{0:T(128)}, u32[]{:S(2)}) copy-start(s32[7]{0:T(128)} %constant.71.clone) | copy-start | bytes 88
  18.7 4.4 %copy-start.4 = (s32[7]{0:T(128)S(1)}, s32[7]{0:T(128)}, u32[]{:S(2)}) copy-start(s32[7]{0:T(128)} %constant.70.clone) | copy-start | bytes 88
  18.7 4.4 %collective-permute-start.7 = (f32[4,2,4,8,128]{4,3,2,1,0:T(8,128)S(1)}, f32[4,2,4,8,128]{4,3,2,1,0:T(8,128)S(1)}, u32[]{:S(2)}, u32[]{:S(2)}) collective-permute-start(f32[4,2,4,8,128]{4,3,2,1,0:T(8,128)S(1)} %shard_map.93.refs_0_), channel_id=1, source_target_pairs={{0,1},{1,0},{2,3},{3,2},{4,5},{5,4},{6,7},{7,6},{8,9},{9,8},{10,11... | collective-permute-start | bytes 393224 | tf_op jit(solution)/shard_map/ppermute | solution.py:327
  18.7 5.2 %collective-permute-start.6 = (f32[4,2,4,8,128]{4,3,2,1,0:T(8,128)S(1)}, f32[4,2,4,8,128]{4,3,2,1,0:T(8,128)S(1)}, u32[]{:S(2)}, u32[]{:S(2)}) collective-permute-start(f32[4,2,4,8,128]{4,3,2,1,0:T(8,128)S(1)} %shard_map.93.refs_0_), channel_id=1, source_target_pairs={{0,5},{1,4},{2,7},{3,6},{4,1},{5,0},{6,3},{7,2},{8,13},{9,12},{10,... | collective-permute-start | bytes 393224 | tf_op jit(solution)/shard_map/ppermute | solution.py:327
  21.6 2.2 %collective-permute-start.9 = (f32[4,2,4,8,128]{4,3,2,1,0:T(8,128)S(1)}, f32[4,2,4,8,128]{4,3,2,1,0:T(8,128)S(1)}, u32[]{:S(2)}, u32[]{:S(2)}) collective-permute-start(f32[4,2,4,8,128]{4,3,2,1,0:T(8,128)S(1)} %collective-permute-done.5.refs_2_), channel_id=1, source_target_pairs={{0,1},{1,0},{2,3},{3,2},{4,5},{5,4},{6,7},{7,6},{8,9},{9,8},{10,11... | collective-permute-start | bytes 393224 | tf_op jit(solution)/shard_map/ppermute | solution.py:327
  23.1 1.3 %collective-permute-start.8 = (f32[4,2,4,8,128]{4,3,2,1,0:T(8,128)S(1)}, f32[4,2,4,8,128]{4,3,2,1,0:T(8,128)S(1)}, u32[]{:S(2)}, u32[]{:S(2)}) collective-permute-start(f32[4,2,4,8,128]{4,3,2,1,0:T(8,128)S(1)} %collective-permute-done.4.refs_1_), channel_id=1, source_target_pairs={{0,1},{1,0},{2,3},{3,2},{4,5},{5,4},{6,7},{7,6},{8,9},{9,8},{10,11... | collective-permute-start | bytes 393224 | tf_op jit(solution)/shard_map/ppermute | solution.py:327
  23.1 1.3 %copy-start = (s32[4]{0:T(128)S(1)}, s32[4]{0:T(128)}, u32[]{:S(2)}) copy-start(s32[4]{0:T(128)} %snap_steps.1) | copy-start | bytes 52
  44.9 0.7 %copy-start.2 = (f32[4,32]{1,0:T(4,128)}, f32[4,32]{1,0:T(4,128)S(1)}, u32[]{:S(2)}) copy-start(f32[4,32]{1,0:T(4,128)S(1)} %get-tuple-element.34) | copy-start | bytes 1540
  45.6 0.6 %copy-start.5 = (f32[4,3,1,512]{3,2,1,0:T(1,128)}, f32[4,3,1,512]{3,2,1,0:T(1,128)S(1)}, u32[]{:S(2)}) copy-start(f32[4,3,1,512]{3,2,1,0:T(1,128)S(1)} %get-tuple-element.61) | copy-start | bytes 73732
  45.6 0.6 %copy-start.6 = (f32[4,4]{1,0:T(4,128)}, f32[4,4]{1,0:T(4,128)S(1)}, u32[]{:S(2)}) copy-start(f32[4,4]{1,0:T(4,128)S(1)} %get-tuple-element.60) | copy-start | bytes 196

commit v5 on v4

--- a/solution.py
+++ b/solution.py
@@ -15,11 +15,13 @@
 DIR_Z = [0, 0, 0, 0, 0, 1, -1, 0, 0, 0, 0, 1, 1, -1, -1, 1, 1, -1, -1]
 OPPOSITE = [(1, 2), (3, 4), (5, 6), (7, 10), (8, 9), (11, 14), (12, 13), (15, 18), (16, 17)]
 OMEGA = 1.6
+KEEP = 1.0 - OMEGA
+RATE = OMEGA / KEEP
 UNIT = 10.0
 SUB = 8
 LANES = 128
 HALO = 8
-AT_ONCE = 2
+AT_ONCE = 4
 HIGHEST = lax.Precision.HIGHEST
 NT = (((1,), (1,)), ((), ()))
 VMEM_LIMIT = 48 * 1024 * 1024
@@ -38,26 +40,30 @@
 
 
 def relaxed(rate, dens, flow, speed, pops):
-    keep = 1.0 - rate
-    twice = [2.0 * f for f in flow]
-    squares = [t * s for t, s in zip(twice, speed)]
-    base = (rate / 36.0) * dens - (squares[0] + squares[1] + squares[2]) * (1.0 / 6.0)
-    base2 = 2.0 * base
+    twice = [f + f for f in flow]
+    squares = [f * s for f, s in zip(flow, speed)]
+    base = (rate / 36.0) * dens - (squares[0] + squares[1] + squares[2]) * (1.0 / 3.0)
+    based = [base + square for square in squares]
     out = [None] * DIRS
 
     def put(i, value):
-        out[i] = value if pops is None else keep * pops[i] + value
+        out[i] = value if pops is None else pops[i] + value
 
     put(0, 12.0 * base)
+    crossed = {}
     for a, b in OPPOSITE:
         direction = (DIR_X[a], DIR_Y[a], DIR_Z[a])
-        if a < 7:
-            axis = [abs(d) for d in direction].index(1)
-            even = base2 + squares[axis]
-            odd = twice[axis]
+        axes = [n for n in range(3) if direction[n]]
+        if len(axes) == 1:
+            even = based[axes[0]] + based[axes[0]]
+            odd = twice[axes[0]]
         else:
+            m, n = axes
+            if (m, n) not in crossed:
+                crossed[m, n] = based[m] + squares[n], twice[m] * speed[n]
+            both, cross = crossed[m, n]
+            even = both + cross if direction[m] * direction[n] > 0 else both - cross
             odd = along(direction, flow)
-            even = base + odd * along(direction, speed)
         put(a, even + odd)
         put(b, even - odd)
     return out
@@ -99,15 +105,17 @@
     return get
 
 
-def widen_kernel(held, up_dens, up_vel, low_dens, low_vel, wide, whole):
+def edges_kernel(held, top, bottom):
+    rows = held.shape[2]
+    top[...] = held[:, :, rows - HALO :, :]
+    bottom[...] = held[:, :, :HALO, :]
+
+
+def widen_kernel(held, upper, lower, wide, whole):
     fields, planes, rows, _ = held.shape
-    below = HALO + rows
-    whole[0, :, :HALO, :] = up_dens[:, rows - HALO :, :]
-    whole[0, :, below:, :] = low_dens[:, :HALO, :]
-    for c in range(3):
-        whole[c + 1, :, :HALO, :] = up_vel[c, :, rows - HALO :, :]
-        whole[c + 1, :, below:, :] = low_vel[c, :, :HALO, :]
-    whole[:, :, HALO:below, :] = held[...]
+    whole[:, :, :HALO, :] = upper[...]
+    whole[:, :, HALO : HALO + rows, :] = held[...]
+    whole[:, :, HALO + rows :, :] = lower[...]
     tiles = wide.shape[2]
     for f in range(fields):
         for p in range(planes):
@@ -175,8 +183,8 @@
                     dens, mom = moments(pop)
                     inverse = 1.5 * reciprocal(dens)
                     speed = [m * inverse for m in mom]
-                    flow = [m * (OMEGA * 3.0 / 36.0) for m in mom]
-                    out = relaxed(OMEGA, dens, flow, speed, pop)
+                    flow = [m * (RATE * 3.0 / 36.0) for m in mom]
+                    out = relaxed(RATE, dens, flow, speed, pop)
                     for i in range(DIRS):
                         dst[i, x, t] = out[i]
                     held.append(speed)
@@ -192,7 +200,7 @@
         get = streamed(src, reach + p, tiles)
         for i in range(DIRS):
             for t in range(tiles):
-                whole[p, i, pl.ds(t, SUB, stride=tiles), :] = get(i, t)
+                whole[p, i, pl.ds(t, SUB, stride=tiles), :] = KEEP ** (STEPS - 1) * get(i, t)
         copies.append(pltpu.make_async_copy(whole.at[p, :, pl.ds(HALO, rows), :], pops.at[:, p], sems.at[p]))
         copies[-1].start()
 
@@ -260,8 +268,43 @@
     return half // SUB * rank + half * (j - half // SUB) - half
 
 
+def residuals(proj, snaps, basis):
+    thirds = [part.astype(jnp.bfloat16) for part in split3(proj)]
+    resid = []
+    for n in range(3):
+        value = snaps[n]
+        for third in thirds:
+            value = value - jnp.dot(third, basis[n], preferred_element_type=jnp.float32)
+        resid.append(value)
+    return resid
+
+
+def solve(small, resid, scale, factor, modes):
+    count = factor.shape[0]
+    r = lax.broadcasted_iota(jnp.int32, (SUB, SUB), 0)
+    c = lax.broadcasted_iota(jnp.int32, (SUB, SUB), 1)
+    small = jnp.where((r < count) & (c < count), small, jnp.where(r == c, 1.0, 0.0))
+    below = lax.broadcasted_iota(jnp.int32, (SUB, 1), 0)
+    pivots = jnp.ones((SUB, 1), jnp.float32)
+    for j in range(count):
+        pivot = small[j : j + 1, j : j + 1]
+        pivots = jnp.where(below == j, pivot, pivots)
+        share = jnp.where(below > j, small[:, j : j + 1] / pivot, 0.0)
+        resid = [v - share * v[j : j + 1, :] for v in resid]
+        small = small - share * small[j : j + 1, :]
+    root = jnp.sqrt(pivots)
+    upper = jnp.where(c >= r, small / root, 0.0)
+    factor[...] = upper[0:count, 0:count] * (1.0 / scale)
+    gain = scale / root
+    groups = resid[0].shape[1] // LANES
+    for n in range(3):
+        value = resid[n] * gain
+        for t in range(groups):
+            modes[pl.ds(groups * n + t, count, stride=3 * groups), :] = value[0:count, LANES * t : LANES * (t + 1)]
+
+
 def finish_kernel(scale, count, rank, *refs):
-    parts, (snaps, basis, coef, factor, modes, flag, gram) = refs[:-7], refs[-7:]
+    parts, (snaps, basis, coef, factor, modes, flag, held, gram) = refs[:-8], refs[-8:]
     if len(parts) == 1 and len(parts[0].shape) == 3:
         packed = tree_sum([parts[0][n] for n in range(parts[0].shape[0])])
     else:
@@ -278,6 +321,8 @@
         gram[SUB * j : SUB * (j + 1), :] = part
     tail = pltpu.roll(packed, rank, 1)
     proj = jnp.where(row < count, tail, 0.0)[:, 0:rank]
+    held[...] = proj
+    coef[...] = proj[0:count, :]
     inner = pltpu.roll(tail, SUB - count, 0)[:, 0:SUB]
     dot = functools.partial(lax.dot_general, precision=HIGHEST, preferred_element_type=jnp.float32)
     turned = dot(proj, gram[:, 0:rank], (((1,), (0,)), ((), ())))
@@ -288,32 +333,19 @@
     c = lax.broadcasted_iota(jnp.int32, (SUB, SUB), 1)
     loss = jnp.where((r == c) & (r < count), inner + 2.0 * crossed + bent - 8.0 * small, -1.0)
     flag[0, 0] = jnp.max(jnp.where(loss < 0.0, 0.0, 1.0)).astype(jnp.int32)
-    coef[...] = proj[0:count, :]
-    resid = []
-    thirds = [part.astype(jnp.bfloat16) for part in split3(proj)]
-    for n in range(3):
-        value = snaps[n]
-        for third in thirds:
-            value = value - jnp.dot(third, basis[n], preferred_element_type=jnp.float32)
-        resid.append(value)
-    small = jnp.where((r < count) & (c < count), small, jnp.where(r == c, 1.0, 0.0))
-    below = lax.broadcasted_iota(jnp.int32, (SUB, 1), 0)
-    pivots = jnp.ones((SUB, 1), jnp.float32)
-    for j in range(count):
-        pivot = small[j : j + 1, j : j + 1]
-        pivots = jnp.where(below == j, pivot, pivots)
-        share = jnp.where(below > j, small[:, j : j + 1] / pivot, 0.0)
-        resid = [v - share * v[j : j + 1, :] for v in resid]
-        small = small - share * small[j : j + 1, :]
-    root = jnp.sqrt(pivots)
-    upper = jnp.where(c >= r, small / root, 0.0)
-    factor[...] = upper[0:count, 0:count] * (1.0 / scale)
-    gain = scale / root
-    groups = snaps.shape[2] // lanes
-    for n in range(3):
-        value = resid[n] * gain
-        for t in range(groups):
-            modes[pl.ds(groups * n + t, count, stride=3 * groups), :] = value[0:count, lanes * t : lanes * (t + 1)]
+    solve(small, residuals(proj, snaps, basis), scale, factor, modes)
+
+
+def inner_kernel(proj, snaps, basis, gram):
+    total = None
+    for resid in residuals(proj[...], snaps, basis):
+        term = lax.dot_general(resid, resid, NT, precision=HIGHEST, preferred_element_type=jnp.float32)
+        total = term if total is None else total + term
+    gram[...] = total
+
+
+def solve_kernel(scale, gram, proj, snaps, basis, factor, modes):
+    solve(gram[...], residuals(proj[...], snaps, basis), scale, factor, modes)
 
 
 def tree_sum(parts):
@@ -368,22 +400,6 @@
     return parts
 
 
-def from_residuals(coefficients, snaps, basis, scale):
-    modes = basis[:, :, 0, :].astype(jnp.float32)
-    count = coefficients.shape[1]
-    held = jnp.transpose(snaps[:, :count, :], (1, 0, 2))
-    resid = held - jnp.einsum("rk,rab->kab", coefficients, modes, precision=HIGHEST)
-    gram = lax.psum(jnp.einsum("kab,lab->kl", resid, resid, precision=HIGHEST), ("group", "dev"))
-    lower = jnp.linalg.cholesky(gram)
-    solved = []
-    for k in range(count):
-        value = resid[k]
-        for j in range(k):
-            value = value - lower[k, j] * solved[j]
-        solved.append(value / lower[k, k])
-    return lower.T / scale, (jnp.stack(solved) * scale).reshape(-1, LANES)
-
-
 def ring_blocks(own, n_dev, planes, reach):
     ahead = moved(own, "dev", lambda i: (i - 2) % n_dev)
     behind = moved(own, "dev", lambda i: (i + 2) % n_dev)
@@ -409,21 +425,23 @@
     f32 = jnp.float32
     params = pltpu.CompilerParams(vmem_limit_bytes=VMEM_LIMIT)
 
-    up = lambda i: (i + 1) % n_group
-    down = lambda i: (i - 1) % n_group
     held = jnp.concatenate([density[None], velocity])
-    upper = [moved(array, "group", up) for array in (density, velocity)]
-    lower = [moved(array, "group", down) for array in (density, velocity)]
+    edge = jax.ShapeDtypeStruct((4, planes, HALO, lanes), f32)
+    top, bottom = pl.pallas_call(
+        edges_kernel, out_shape=(edge, edge), in_specs=[vmem], out_specs=(vmem, vmem), compiler_params=params
+    )(held)
+    upper = moved(top, "group", lambda i: (i + 1) % n_group)
+    lower = moved(bottom, "group", lambda i: (i - 1) % n_group)
     wide_rows = rows + 2 * HALO
     tiles = wide_rows // SUB
     own = pl.pallas_call(
         widen_kernel,
         out_shape=jax.ShapeDtypeStruct((4, planes, tiles, SUB, lanes), f32),
-        in_specs=[vmem] * 5,
+        in_specs=[vmem] * 3,
         out_specs=vmem,
         scratch_shapes=[pltpu.VMEM((4, planes, wide_rows, lanes), f32)],
         compiler_params=params,
-    )(held, *upper, *lower)
+    )(held, upper, lower)
     blocks, place = ring_blocks(own, n_dev, planes, reach)
     modes = jnp.transpose(basis[:, :, 0, :], (1, 0, 2))
     span = planes + 2 * reach
@@ -458,25 +476,38 @@
     else:
         parts = summed(sums, n_dev, n_group)
     scale = math.sqrt(3 * width * members)
-    coef, factor, new_modes, flag = pl.pallas_call(
+    solved = (
+        jax.ShapeDtypeStruct((count, count), f32),
+        jax.ShapeDtypeStruct((count * 3 * width // lanes, lanes), f32),
+    )
+    coef, factor, new_modes, flag, proj = pl.pallas_call(
         functools.partial(finish_kernel, scale, count, rank),
         out_shape=(
             jax.ShapeDtypeStruct((count, rank), f32),
-            jax.ShapeDtypeStruct((count, count), f32),
-            jax.ShapeDtypeStruct((count * 3 * width // lanes, lanes), f32),
+            *solved,
             jax.ShapeDtypeStruct((1, 1), jnp.int32),
+            jax.ShapeDtypeStruct((SUB, rank), f32),
         ),
         in_specs=[vmem] * (len(parts) + 2),
-        out_specs=(vmem, vmem, vmem, smem),
+        out_specs=(vmem, vmem, vmem, smem, vmem),
         scratch_shapes=[pltpu.VMEM((rank, lanes), f32)],
         compiler_params=params,
     )(*parts, snaps, modes)
     coefficients = coef.T
-    factor, new_modes = lax.cond(
-        flag[0, 0] != 0,
-        lambda: from_residuals(coefficients, snaps, basis, scale),
-        lambda: (factor, new_modes),
-    )
+
+    def from_residuals(state):
+        gram = pl.pallas_call(
+            inner_kernel, out_shape=jax.ShapeDtypeStruct((SUB, SUB), f32), in_specs=[vmem] * 3, out_specs=vmem
+        )(proj, snaps, modes)
+        gram = lax.psum(gram, ("group", "dev"))
+        return (
+            jnp.int32(0),
+            *pl.pallas_call(
+                functools.partial(solve_kernel, scale), out_shape=solved, in_specs=[vmem] * 4, out_specs=(vmem, vmem)
+            )(gram, proj, snaps, modes),
+        )
+
+    _, factor, new_modes = lax.while_loop(lambda state: state[0] != 0, from_residuals, (flag[0, 0], factor, new_modes))
     return (pops, coefficients, factor, new_modes.reshape(count, 3, 1, width))
 
 

time: 46.4 us -> 41.2 us (0.89)
  starting transfers between devices: 13.5 us -> 9.79 us
  waiting for transfers between devices: 9.28 us -> 6.69 us
  blocking collectives: 11.3 us -> 13.8 us
  between operations: 1.38 us -> 0.69 us
  loops' own time: 0.01 us -> 0.63 us
  Pallas kernels: 9.17 us -> 8.56 us
  local copies, waits for them, and re-layouts: 0.62 us -> 0.02 us
    ppermute x10 -> x8, starting transfers between devices: 13.5 us -> 9.79 us  [moved(): lax.ppermute(block, axis, [(i, target(i)) for i in range(lax.axis_size(ax...]
    ppermute x10 -> x8, waiting for transfers between devices: 9.28 us -> 6.69 us  [moved(): lax.ppermute(block, axis, [(i, target(i)) for i in range(lax.axis_size(ax...]
    all_to_all x1, blocking collectives: 11.3 us -> 13.8 us  [per_device(): parts = [lax.all_to_all(sums, ('group', 'dev'), 0, 0)]]
    pallas_call x1, Pallas kernels: 7.93 us -> 7.18 us  [per_device(): pl.pallas_call(lattice_kernel, out_shape=(jax.ShapeDtypeStruct((DIRS, pla...]
    another operation x1, loops' own time: 0.01 us -> 0.63 us  [per_device(): lax.while_loop(lambda state: state[0] != 0, from_residuals, (flag[0, 0],...]
    unnamed x14 -> x8, local copies, waits for them, and re-layouts: 0.62 us -> 0.02 us
  transfers between devices with their start and end apart: 10 -> 8, of which waited for: 7 -> 6; matrix products, arithmetic and copies ran while one was open for 2% -> 0% of each run, Pallas kernels for 0% -> 0%
where the time goes in v5:
time: 41.2 us; the launch traced here: 41 us
  blocking collectives  13.8 us (33%)
  starting transfers between devices  9.79 us (24%)
  Pallas kernels  8.56 us (21%)
  waiting for transfers between devices  6.69 us (16%)
  other arithmetic  0.81 us (2%)
  between operations  0.69 us (2%)
  loops' own time  0.63 us (2%)
    all_to_all x1, blocking collectives, per_device(): parts = [lax.all_to_all(sums, ('group', 'dev'), 0, 0)]  13.8 us
    ppermute x8, starting transfers between devices, moved(): lax.ppermute(block, axis, [(i, target(i)) for i in range(lax.axis_size(ax...  9.79 us
    pallas_call x1, Pallas kernels, per_device(): pl.pallas_call(lattice_kernel, out_shape=(jax.ShapeDtypeStruct((DIRS, pla...  7.18 us
    ppermute x8, waiting for transfers between devices, moved(): lax.ppermute(block, axis, [(i, target(i)) for i in range(lax.axis_size(ax...  6.69 us
    pallas_call x1, Pallas kernels, per_device(): pl.pallas_call(functools.partial(finish_kernel, scale, count, rank), out_...  1.35 us
  transfers between devices with their start and end apart: 8, of which 6 were waited for; matrix products, arithmetic and copies ran while one was open for 0% of the time, Pallas kernels for 0%

profile of v5, /device:TPU:0, one launch (start us, length us, event | category | flops | bytes accessed | tf_op | source)
XLA Modules:
  0.0 41.0 jit_solution(9844028074686760438)
XLA Ops:
  0.6 0.8 %pad_maximum_fusion.held = f32[4,2,16,128]{3,2,1,0:T(8,128)S(1)} fusion(f32[3,2,16,128]{3,2,1,0:T(8,128)} %param.9, f32[1,2,16,128]{3,2,1,0:T(8,128)} %bitcast.10), kind=kLoop, calls=%fused_computation | loop fusion | flops 16384 | bytes 131072 | tf_op jit(solution)/shard_map/concatenate | solution.py:428
  1.4 3.1 %collective-permute-start = (f32[4,2,8,128]{3,2,1,0:T(8,128)S(1)}, f32[4,2,8,128]{3,2,1,0:T(8,128)S(1)}, u32[]{:S(2)}, u32[]{:S(2)}) collective-permute-start(f32[4,2,8,128]{3,2,1,0:T(8,128)S(1)} %get-tuple-element.46), channel_id=1, source_target_pairs={{0,8},{8,16},{16,24},{24,0},{1,9},{9,17},{17,25},{25,1},{2,10},{10... | collective-permute-start | bytes 98312 | tf_op jit(solution)/shard_map/ppermute | solution.py:359
  4.5 0.0 copy-start.1
  4.5 2.1 %collective-permute-start.1 = (f32[4,2,8,128]{3,2,1,0:T(8,128)S(1)}, f32[4,2,8,128]{3,2,1,0:T(8,128)S(1)}, u32[]{:S(2)}, u32[]{:S(2)}) collective-permute-start(f32[4,2,8,128]{3,2,1,0:T(8,128)S(1)} %get-tuple-element.47), channel_id=1, source_target_pairs={{0,24},{8,0},{16,8},{24,16},{1,25},{9,1},{17,9},{25,17},{2,26},{10... | collective-permute-start | bytes 98312 | tf_op jit(solution)/shard_map/ppermute | solution.py:359
  6.6 1.9 %collective-permute-done.upper = f32[4,2,8,128]{3,2,1,0:T(8,128)S(1)} collective-permute-done((f32[4,2,8,128]{3,2,1,0:T(8,128)S(1)}, f32[4,2,8,128]{3,2,1,0:T(8,128)S(1)}, u32[]{:S(2)}, u32[]{:S(2)}) %collective-permute-start) | collective-permute-done | bytes 32800 | tf_op jit(solution)/shard_map/ppermute | solution.py:359
  8.6 0.2 collective-permute-done.1.lower
  8.8 1.5 %collective-permute-start.3 = (f32[4,2,4,8,128]{4,3,2,1,0:T(8,128)S(1)}, f32[4,2,4,8,128]{4,3,2,1,0:T(8,128)S(1)}, u32[]{:S(2)}, u32[]{:S(2)}) collective-permute-start(f32[4,2,4,8,128]{4,3,2,1,0:T(8,128)S(1)} %shard_map.94.refs_0_), channel_id=1, source_target_pairs={{0,2},{1,3},{2,4},{3,5},{4,6},{5,7},{6,0},{7,1},{8,10},{9,11},{10,... | collective-permute-start | bytes 393224 | tf_op jit(solution)/shard_map/ppermute | solution.py:359
  10.4 1.4 %collective-permute-start.2 = (f32[4,2,4,8,128]{4,3,2,1,0:T(8,128)S(1)}, f32[4,2,4,8,128]{4,3,2,1,0:T(8,128)S(1)}, u32[]{:S(2)}, u32[]{:S(2)}) collective-permute-start(f32[4,2,4,8,128]{4,3,2,1,0:T(8,128)S(1)} %shard_map.94.refs_0_), channel_id=1, source_target_pairs={{0,6},{1,7},{2,0},{3,1},{4,2},{5,3},{6,4},{7,5},{8,14},{9,15},{10,... | collective-permute-start | bytes 393224 | tf_op jit(solution)/shard_map/ppermute | solution.py:359
  11.8 0.0 copy-start.2
  11.8 0.0 copy-start.3
  11.8 0.0 collective-permute-start.5
  11.8 1.6 %collective-permute-start.4 = (f32[4,2,4,8,128]{4,3,2,1,0:T(8,128)S(1)}, f32[4,2,4,8,128]{4,3,2,1,0:T(8,128)S(1)}, u32[]{:S(2)}, u32[]{:S(2)}) collective-permute-start(f32[4,2,4,8,128]{4,3,2,1,0:T(8,128)S(1)} %shard_map.94.refs_0_), channel_id=1, source_target_pairs={{0,5},{1,4},{2,7},{3,6},{4,1},{5,0},{6,3},{7,2},{8,13},{9,12},{10,... | collective-permute-start | bytes 393224 | tf_op jit(solution)/shard_map/ppermute | solution.py:359
  13.4 1.8 %collective-permute-done.3.refs_2_ = f32[4,2,4,8,128]{4,3,2,1,0:T(8,128)S(1)} collective-permute-done((f32[4,2,4,8,128]{4,3,2,1,0:T(8,128)S(1)}, f32[4,2,4,8,128]{4,3,2,1,0:T(8,128)S(1)}, u32[]{:S(2)}, u32[]{:S(2)}) %collective-permute-start.3) | collective-permute-done | bytes 131104 | tf_op jit(solution)/shard_map/ppermute | solution.py:359
  15.2 0.0 collective-permute-start.7
  15.2 1.4 %collective-permute-done.2.refs_1_ = f32[4,2,4,8,128]{4,3,2,1,0:T(8,128)S(1)} collective-permute-done((f32[4,2,4,8,128]{4,3,2,1,0:T(8,128)S(1)}, f32[4,2,4,8,128]{4,3,2,1,0:T(8,128)S(1)}, u32[]{:S(2)}, u32[]{:S(2)}) %collective-permute-start.2) | collective-permute-done | bytes 131104 | tf_op jit(solution)/shard_map/ppermute | solution.py:359
  16.7 0.0 collective-permute-start.6
  16.7 0.0 copy-done.2
  16.7 0.0 copy-done.3
  16.7 0.0 copy-start
  16.7 0.0 collective-permute-done.5.refs_4_
  16.7 1.0 %collective-permute-done.4.refs_3_ = f32[4,2,4,8,128]{4,3,2,1,0:T(8,128)S(1)} collective-permute-done((f32[4,2,4,8,128]{4,3,2,1,0:T(8,128)S(1)}, f32[4,2,4,8,128]{4,3,2,1,0:T(8,128)S(1)}, u32[]{:S(2)}, u32[]{:S(2)}) %collective-permute-start.4) | collective-permute-done | bytes 131104 | tf_op jit(solution)/shard_map/ppermute | solution.py:359
  17.7 0.0 collective-permute-done.7.refs_6_
  17.7 0.3 collective-permute-done.6.refs_5_
  18.0 0.0 copy-done.1
  18.0 0.0 copy-done
  18.0 7.2 %shard_map.95 = (f32[19,2,16,128]{3,2,1,0:T(8,128)}, f32[3,8,512]{2,1,0:T(8,128)S(1)}, f32[32,8,128]{2,1,0:T(8,128)S(1)}) custom-call(s32[7]{0:T(128)S(1)} %fusion.1.place, s32[4]{0:T(128)S(1)} %copy-done, f32[4,2,4,8,128]{4,3,2,1,0:T(8,128)S(1)} %shard_map.94.refs_0_, f32[4,2,4,8,128]{4,3,2,1,0:T(8,128)S(1)} %collective-permute-done.2.refs_1_, ...), custom_call_target="tpu_custom_call" | custom-call | tf_op jit(solution)/shard_map/pallas_call | solution.py:451
  25.2 13.8 %all_to_all.5.refs_0_ = f32[32,8,128]{2,1,0:T(8,128)S(1)} all-to-all(f32[32,8,128]{2,1,0:T(8,128)S(1)} %get-tuple-element.49), channel_id=1, replica_groups=mesh['group'=4,'dev'=8] {'group','dev'}, dimensions={0} | all-to-all | bytes 262144 | tf_op jit(solution)/shard_map/all_to_all | solution.py:475
  39.0 1.4 %shard_map.96 = (f32[4,32]{1,0:T(4,128)}, f32[4,4]{1,0:T(4,128)}, f32[48,128]{1,0:T(8,128)}, s32[1,1]{1,0:T(1,128)}, f32[8,32]{1,0:T(8,128)S(1)}) custom-call(f32[32,8,128]{2,1,0:T(8,128)S(1)} %all_to_all.5.refs_0_, f32[3,8,512]{2,1,0:T(8,128)S(1)} %get-tuple-element.80.refs_1_, bf16[3,32,512]{2,1,0:T(8,128)(2,1)S(1)} %bitcast.8), custom_call_target="tpu_custom_call" | custom-call | tf_op jit(solution)/shard_map/pallas_call | solution.py:483
  40.3 0.6 %while.11 = (s32[]{:T(128)}, f32[4,4]{1,0:T(4,128)}, f32[48,128]{1,0:T(8,128)}, f32[8,32]{1,0:T(8,128)S(1)}, f32[3,8,512]{2,1,0:T(8,128)S(1)}, /*index=5*/bf16[3,32,512]{2,1,0:T(8,128)(2,1)S(1)}) while((s32[]{:T(128)}, f32[4,4]{1,0:T(4,128)}, f32[48,128]{1,0:T(8,128)}, f32[8,32]{1,0:T(8,128)S(1)}, f32[3,8,512]{2,1,0:T(8,128)S(1)}, ...), condition=%region_2.3_spmd, body=%region_0.2_spmd | while | flops 65 | bytes 577 | solution.py:510
  (3 shorter events, 0.0 us)
Async XLA Ops:
  1.4 7.1 %collective-permute-start = (f32[4,2,8,128]{3,2,1,0:T(8,128)S(1)}, f32[4,2,8,128]{3,2,1,0:T(8,128)S(1)}, u32[]{:S(2)}, u32[]{:S(2)}) collective-permute-start(f32[4,2,8,128]{3,2,1,0:T(8,128)S(1)} %get-tuple-element.46), channel_id=1, source_target_pairs={{0,8},{8,16},{16,24},{24,0},{1,9},{9,17},{17,25},{25,1},{2,10},{10... | collective-permute-start | bytes 98312 | tf_op jit(solution)/shard_map/ppermute | solution.py:359
  4.5 13.5 %copy-start.1 = (bf16[32,3,1,512]{3,0,2,1:T(8,128)(2,1)S(1)}, bf16[32,3,1,512]{3,0,2,1:T(8,128)(2,1)}, u32[]{:S(2)}) copy-start(bf16[32,3,1,512]{3,0,2,1:T(8,128)(2,1)} %param.10) | copy-start | bytes 294916
  4.5 4.3 %collective-permute-start.1 = (f32[4,2,8,128]{3,2,1,0:T(8,128)S(1)}, f32[4,2,8,128]{3,2,1,0:T(8,128)S(1)}, u32[]{:S(2)}, u32[]{:S(2)}) collective-permute-start(f32[4,2,8,128]{3,2,1,0:T(8,128)S(1)} %get-tuple-element.47), channel_id=1, source_target_pairs={{0,24},{8,0},{16,8},{24,16},{1,25},{9,1},{17,9},{25,17},{2,26},{10... | collective-permute-start | bytes 98312 | tf_op jit(solution)/shard_map/ppermute | solution.py:359
  8.8 6.4 %collective-permute-start.3 = (f32[4,2,4,8,128]{4,3,2,1,0:T(8,128)S(1)}, f32[4,2,4,8,128]{4,3,2,1,0:T(8,128)S(1)}, u32[]{:S(2)}, u32[]{:S(2)}) collective-permute-start(f32[4,2,4,8,128]{4,3,2,1,0:T(8,128)S(1)} %shard_map.94.refs_0_), channel_id=1, source_target_pairs={{0,2},{1,3},{2,4},{3,5},{4,6},{5,7},{6,0},{7,1},{8,10},{9,11},{10,... | collective-permute-start | bytes 393224 | tf_op jit(solution)/shard_map/ppermute | solution.py:359
  10.4 6.3 %collective-permute-start.2 = (f32[4,2,4,8,128]{4,3,2,1,0:T(8,128)S(1)}, f32[4,2,4,8,128]{4,3,2,1,0:T(8,128)S(1)}, u32[]{:S(2)}, u32[]{:S(2)}) collective-permute-start(f32[4,2,4,8,128]{4,3,2,1,0:T(8,128)S(1)} %shard_map.94.refs_0_), channel_id=1, source_target_pairs={{0,6},{1,7},{2,0},{3,1},{4,2},{5,3},{6,4},{7,5},{8,14},{9,15},{10,... | collective-permute-start | bytes 393224 | tf_op jit(solution)/shard_map/ppermute | solution.py:359
  11.8 4.9 %copy-start.2 = (s32[7]{0:T(128)S(1)}, s32[7]{0:T(128)}, u32[]{:S(2)}) copy-start(s32[7]{0:T(128)} %constant.30.clone) | copy-start | bytes 88
  11.8 4.9 %copy-start.3 = (s32[7]{0:T(128)S(1)}, s32[7]{0:T(128)}, u32[]{:S(2)}) copy-start(s32[7]{0:T(128)} %constant.29.clone) | copy-start | bytes 88
  11.8 4.9 %collective-permute-start.5 = (f32[4,2,4,8,128]{4,3,2,1,0:T(8,128)S(1)}, f32[4,2,4,8,128]{4,3,2,1,0:T(8,128)S(1)}, u32[]{:S(2)}, u32[]{:S(2)}) collective-permute-start(f32[4,2,4,8,128]{4,3,2,1,0:T(8,128)S(1)} %shard_map.94.refs_0_), channel_id=1, source_target_pairs={{0,1},{1,0},{2,3},{3,2},{4,5},{5,4},{6,7},{7,6},{8,9},{9,8},{10,11... | collective-permute-start | bytes 393224 | tf_op jit(solution)/shard_map/ppermute | solution.py:359
  11.8 5.9 %collective-permute-start.4 = (f32[4,2,4,8,128]{4,3,2,1,0:T(8,128)S(1)}, f32[4,2,4,8,128]{4,3,2,1,0:T(8,128)S(1)}, u32[]{:S(2)}, u32[]{:S(2)}) collective-permute-start(f32[4,2,4,8,128]{4,3,2,1,0:T(8,128)S(1)} %shard_map.94.refs_0_), channel_id=1, source_target_pairs={{0,5},{1,4},{2,7},{3,6},{4,1},{5,0},{6,3},{7,2},{8,13},{9,12},{10,... | collective-permute-start | bytes 393224 | tf_op jit(solution)/shard_map/ppermute | solution.py:359
  15.2 2.5 %collective-permute-start.7 = (f32[4,2,4,8,128]{4,3,2,1,0:T(8,128)S(1)}, f32[4,2,4,8,128]{4,3,2,1,0:T(8,128)S(1)}, u32[]{:S(2)}, u32[]{:S(2)}) collective-permute-start(f32[4,2,4,8,128]{4,3,2,1,0:T(8,128)S(1)} %collective-permute-done.3.refs_2_), channel_id=1, source_target_pairs={{0,1},{1,0},{2,3},{3,2},{4,5},{5,4},{6,7},{7,6},{8,9},{9,8},{10,11... | collective-permute-start | bytes 393224 | tf_op jit(solution)/shard_map/ppermute | solution.py:359
  16.7 1.3 %collective-permute-start.6 = (f32[4,2,4,8,128]{4,3,2,1,0:T(8,128)S(1)}, f32[4,2,4,8,128]{4,3,2,1,0:T(8,128)S(1)}, u32[]{:S(2)}, u32[]{:S(2)}) collective-permute-start(f32[4,2,4,8,128]{4,3,2,1,0:T(8,128)S(1)} %collective-permute-done.2.refs_1_), channel_id=1, source_target_pairs={{0,1},{1,0},{2,3},{3,2},{4,5},{5,4},{6,7},{7,6},{8,9},{9,8},{10,11... | collective-permute-start | bytes 393224 | tf_op jit(solution)/shard_map/ppermute | solution.py:359
  16.7 1.3 %copy-start = (s32[4]{0:T(128)S(1)}, s32[4]{0:T(128)}, u32[]{:S(2)}) copy-start(s32[4]{0:T(128)} %snap_steps.1) | copy-start | bytes 52

commit v6 on v5

--- a/solution.py
+++ b/solution.py
@@ -20,8 +20,9 @@
 UNIT = 10.0
 SUB = 8
 LANES = 128
-HALO = 8
+HALO = 6
 AT_ONCE = 4
+OFFSETS = [(0, 0), (2, 2), (-2, -2), (-3, 3), (1, -1), (3, 1), (-1, -3)]
 HIGHEST = lax.Precision.HIGHEST
 NT = (((1,), (1,)), ((), ()))
 VMEM_LIMIT = 48 * 1024 * 1024
@@ -106,21 +107,21 @@
 
 
 def edges_kernel(held, top, bottom):
-    rows = held.shape[2]
-    top[...] = held[:, :, rows - HALO :, :]
-    bottom[...] = held[:, :, :HALO, :]
-
-
-def widen_kernel(held, upper, lower, wide, whole):
+    rows, edge = held.shape[2], top.shape[2]
+    top[...] = held[:, :, rows - edge :, :]
+    bottom[...] = held[:, :, :edge, :]
+
+
+def widen_kernel(held, upper, lower, wide):
     fields, planes, rows, _ = held.shape
-    whole[:, :, :HALO, :] = upper[...]
-    whole[:, :, HALO : HALO + rows, :] = held[...]
-    whole[:, :, HALO + rows :, :] = lower[...]
-    tiles = wide.shape[2]
+    high = rows + 2 * HALO
     for f in range(fields):
         for p in range(planes):
-            for t in range(tiles):
-                wide[f, p, t] = whole[f, p, pl.ds(t, SUB, stride=tiles), :]
+            at = (f * planes + p) * high
+            wide[pl.ds(at, HALO), :] = upper[f, p, upper.shape[2] - HALO :, :]
+            wide[pl.ds(at + HALO, rows), :] = held[f, p]
+            wide[pl.ds(at + HALO + rows, HALO), :] = lower[f, p, :HALO, :]
+    wide[pl.ds(fields * planes * high, SUB), :] = jnp.zeros((SUB, LANES), jnp.float32)
 
 
 def split3(value):
@@ -130,15 +131,19 @@
     return a, b, rest - b
 
 
-def lattice_kernel(place, snap_steps, *refs):
-    blocks, refs = refs[:-13], refs[-13:]
-    basis, pops, snaps, sums, ping, pong, speeds, views, coarse, rowwise, gram, whole, sems = refs
-    planes, tiles, _, lanes = blocks[0].shape[1:]
+def lattice_kernel(*refs):
+    blocks, refs = refs[:-15], refs[-15:]
+    snap_steps, basis, pops, snaps, sums, ping, pong, speeds, views, coarse, rowwise, gram, whole, at_steps, sems = refs
+    planes, rows, lanes = pops.shape[1:]
+    tiles = ping.shape[2]
     reach = STEPS
     span = planes + 2 * reach
-    rows = pops.shape[2]
-    inner = HALO // tiles
+    high = rows + 2 * HALO
     count = snap_steps.shape[0]
+    steps_copy = pltpu.make_async_copy(snap_steps, at_steps, sems.at[planes])
+    steps_copy.start()
+    odd = lax.rem(lax.axis_index("dev"), 2)
+    place = [reach + planes * (even_at + odd * (odd_at - even_at)) for even_at, odd_at in OFFSETS]
 
     def put_speed(x, held):
         for c in range(3):
@@ -158,8 +163,7 @@
             x = place[n] + p
             held = []
             for t in range(tiles):
-                dens = block[0, p, t]
-                vel = [block[c + 1, p, t] for c in range(3)]
+                dens, *vel = [block[pl.ds((f * planes + p) * high + t, SUB, stride=tiles), :] for f in range(4)]
                 part = dens * (3.0 / 36.0)
                 speed = [1.5 * v for v in vel]
                 out = relaxed(1.0, dens, [part * v for v in vel], speed, None)
@@ -200,18 +204,22 @@
         get = streamed(src, reach + p, tiles)
         for i in range(DIRS):
             for t in range(tiles):
-                whole[p, i, pl.ds(t, SUB, stride=tiles), :] = KEEP ** (STEPS - 1) * get(i, t)
-        copies.append(pltpu.make_async_copy(whole.at[p, :, pl.ds(HALO, rows), :], pops.at[:, p], sems.at[p]))
+                whole[p, i, pl.ds(SUB - HALO + t, SUB, stride=tiles), :] = KEEP ** (STEPS - 1) * get(i, t)
+        copies.append(pltpu.make_async_copy(whole.at[p, :, pl.ds(SUB, rows), :], pops.at[:, p], sems.at[p]))
         copies[-1].start()
 
-    halves = [[views[snap_steps[k], c, half] for k in range(count) for c in range(3)] for half in range(2)]
+    steps_copy.wait()
     lane = lax.broadcasted_iota(jnp.int32, (lanes, lanes), 0) // 2
     col = lax.broadcasted_iota(jnp.int32, (lanes, lanes), 1)
     flat = None
+    start_half, start_sub = HALO // 2 % 2, HALO // 2 // 2
     for half in range(2):
-        gather = jnp.where(lane + half * (lanes // 2) == col, 1.0, 0.0).astype(jnp.bfloat16)
-        stack = jnp.concatenate(halves[half], axis=0)
-        for part in split3(stack):
+        right = half != start_half
+        stack = [views[at_steps[k], c, half] for k in range(count) for c in range(3)]
+        if right and start_half == 1:
+            stack = [pltpu.roll(view, SUB - 1, 0) for view in stack]
+        gather = jnp.where(lane + (lanes // 2 if right else 0) == col, 1.0, 0.0).astype(jnp.bfloat16)
+        for part in split3(jnp.concatenate(stack, axis=0)):
             term = jnp.dot(part.astype(jnp.bfloat16), gather, preferred_element_type=jnp.float32)
             flat = term if flat is None else flat + term
     height = 3 * SUB * count
@@ -221,7 +229,7 @@
     groups = rows // tiles
     total = None
     for c in range(3):
-        parts = [coarse[pl.ds(SUB * c + inner + t, SUB, stride=3 * SUB), :] for t in range(groups)]
+        parts = [coarse[pl.ds(SUB * c + start_sub + t, SUB, stride=3 * SUB), :] for t in range(groups)]
         snap = jnp.concatenate(parts, axis=1)
         snaps[c] = snap
         a, b, d = split3(snap)
@@ -400,18 +408,14 @@
     return parts
 
 
-def ring_blocks(own, n_dev, planes, reach):
+def ring_blocks(own, n_dev):
     ahead = moved(own, "dev", lambda i: (i - 2) % n_dev)
     behind = moved(own, "dev", lambda i: (i + 2) % n_dev)
     far = moved(own, "dev", lambda i: (i + 3 if i % 2 else i - 3) % n_dev)
     other = moved(own, "dev", lambda i: i ^ 1)
     other_ahead = moved(ahead, "dev", lambda i: i ^ 1)
     other_behind = moved(behind, "dev", lambda i: i ^ 1)
-    odd = lax.axis_index("dev") % 2
-    offsets = jnp.where(
-        odd == 1, jnp.array([0, 2, -2, 3, -1, 1, -3], jnp.int32), jnp.array([0, 2, -2, -3, 1, 3, -1], jnp.int32)
-    )
-    return [own, ahead, behind, far, other, other_ahead, other_behind], reach + planes * offsets
+    return [own, ahead, behind, far, other, other_ahead, other_behind]
 
 
 def per_device(density, velocity, basis, snap_steps):
@@ -426,23 +430,22 @@
     params = pltpu.CompilerParams(vmem_limit_bytes=VMEM_LIMIT)
 
     held = jnp.concatenate([density[None], velocity])
-    edge = jax.ShapeDtypeStruct((4, planes, HALO, lanes), f32)
+    edge = jax.ShapeDtypeStruct((4, planes, SUB, lanes), f32)
     top, bottom = pl.pallas_call(
         edges_kernel, out_shape=(edge, edge), in_specs=[vmem], out_specs=(vmem, vmem), compiler_params=params
     )(held)
     upper = moved(top, "group", lambda i: (i + 1) % n_group)
     lower = moved(bottom, "group", lambda i: (i - 1) % n_group)
-    wide_rows = rows + 2 * HALO
-    tiles = wide_rows // SUB
+    high = rows + 2 * HALO
+    tiles = pl.cdiv(high, SUB)
     own = pl.pallas_call(
         widen_kernel,
-        out_shape=jax.ShapeDtypeStruct((4, planes, tiles, SUB, lanes), f32),
+        out_shape=jax.ShapeDtypeStruct((4 * planes * high + SUB, lanes), f32),
         in_specs=[vmem] * 3,
         out_specs=vmem,
-        scratch_shapes=[pltpu.VMEM((4, planes, wide_rows, lanes), f32)],
         compiler_params=params,
     )(held, upper, lower)
-    blocks, place = ring_blocks(own, n_dev, planes, reach)
+    blocks = ring_blocks(own, n_dev)
     modes = jnp.transpose(basis[:, :, 0, :], (1, 0, 2))
     span = planes + 2 * reach
     width = basis.shape[3]
@@ -455,7 +458,7 @@
             jax.ShapeDtypeStruct((3, SUB, width), f32),
             jax.ShapeDtypeStruct((members, SUB, lanes) if at_once else (SUB, lanes), f32),
         ),
-        in_specs=[smem, smem] + [vmem] * (len(blocks) + 1),
+        in_specs=[vmem] * len(blocks) + [pl.BlockSpec(memory_space=pl.ANY), vmem],
         out_specs=(pl.BlockSpec(memory_space=pltpu.HBM), vmem, vmem),
         scratch_shapes=[
             pltpu.VMEM((DIRS, span, tiles, SUB, lanes), f32),
@@ -465,11 +468,12 @@
             pltpu.VMEM((3 * SUB * SUB, lanes), f32),
             pltpu.VMEM((rank + 4 * SUB, width), jnp.bfloat16),
             pltpu.VMEM((rank + 4 * SUB, lanes), f32),
-            pltpu.VMEM((planes, DIRS, wide_rows, lanes), f32),
-            pltpu.SemaphoreType.DMA((planes,)),
+            pltpu.VMEM((planes, DIRS, SUB * tiles + SUB, lanes), f32),
+            pltpu.SMEM((count,), jnp.int32),
+            pltpu.SemaphoreType.DMA((planes + 1,)),
         ],
         compiler_params=params,
-    )(place, snap_steps, *blocks, modes)
+    )(*blocks, snap_steps, modes)
 
     if at_once:
         parts = [lax.all_to_all(sums, ("group", "dev"), 0, 0)]

time: 41.2 us -> 39.9 us (0.968)
  Pallas kernels: 8.56 us -> 7.57 us
  waiting for transfers between devices: 6.69 us -> 6.19 us
    pallas_call x1, Pallas kernels: 7.18 us -> 6.2 us  [per_device(): pl.pallas_call(lattice_kernel, out_shape=(jax.ShapeDtypeStruct((DIRS, pla...]
    ppermute x8, waiting for transfers between devices: 6.69 us -> 6.19 us  [moved(): lax.ppermute(block, axis, [(i, target(i)) for i in range(lax.axis_size(ax...]
where the time goes in v6:
time: 39.9 us; the launch traced here: 39.7 us
  blocking collectives  14.1 us (35%)
  starting transfers between devices  9.79 us (25%)
  Pallas kernels  7.57 us (19%)
  waiting for transfers between devices  6.19 us (16%)
  other arithmetic  0.81 us (2%)
  between operations  0.67 us (2%)
  loops' own time  0.57 us (1%)
    all_to_all x1, blocking collectives, per_device(): parts = [lax.all_to_all(sums, ('group', 'dev'), 0, 0)]  14.1 us
    ppermute x8, starting transfers between devices, moved(): lax.ppermute(block, axis, [(i, target(i)) for i in range(lax.axis_size(ax...  9.79 us
    pallas_call x1, Pallas kernels, per_device(): pl.pallas_call(lattice_kernel, out_shape=(jax.ShapeDtypeStruct((DIRS, pla...  6.2 us
    ppermute x8, waiting for transfers between devices, moved(): lax.ppermute(block, axis, [(i, target(i)) for i in range(lax.axis_size(ax...  6.19 us
    pallas_call x1, Pallas kernels, per_device(): pl.pallas_call(functools.partial(finish_kernel, scale, count, rank), out_...  1.35 us
    concatenate x1, other arithmetic, per_device(): held = jnp.concatenate([density[None], velocity])  0.81 us
  transfers between devices with their start and end apart: 8, of which 6 were waited for; matrix products, arithmetic and copies ran while one was open for 0% of the time, Pallas kernels for 0%

profile of v6, /device:TPU:0, one launch (start us, length us, event | category | flops | bytes accessed | tf_op | source)
XLA Modules:
  0.0 39.7 jit_solution(3952541614993240374)
XLA Ops:
  0.6 0.8 %pad_maximum_fusion.held = f32[4,2,16,128]{3,2,1,0:T(8,128)S(1)} fusion(f32[3,2,16,128]{3,2,1,0:T(8,128)} %param.7, f32[1,2,16,128]{3,2,1,0:T(8,128)} %bitcast.10), kind=kLoop, calls=%fused_computation | loop fusion | flops 16384 | bytes 131072 | tf_op jit(solution)/shard_map/concatenate | solution.py:432
  1.4 3.1 %collective-permute-start = (f32[4,2,8,128]{3,2,1,0:T(8,128)S(1)}, f32[4,2,8,128]{3,2,1,0:T(8,128)S(1)}, u32[]{:S(2)}, u32[]{:S(2)}) collective-permute-start(f32[4,2,8,128]{3,2,1,0:T(8,128)S(1)} %get-tuple-element.46), channel_id=1, source_target_pairs={{0,8},{8,16},{16,24},{24,0},{1,9},{9,17},{17,25},{25,1},{2,10},{10... | collective-permute-start | bytes 98312 | tf_op jit(solution)/shard_map/ppermute | solution.py:367
  4.5 0.0 copy-start.1
  4.5 2.1 %collective-permute-start.1 = (f32[4,2,8,128]{3,2,1,0:T(8,128)S(1)}, f32[4,2,8,128]{3,2,1,0:T(8,128)S(1)}, u32[]{:S(2)}, u32[]{:S(2)}) collective-permute-start(f32[4,2,8,128]{3,2,1,0:T(8,128)S(1)} %get-tuple-element.47), channel_id=1, source_target_pairs={{0,24},{8,0},{16,8},{24,16},{1,25},{9,1},{17,9},{25,17},{2,26},{10... | collective-permute-start | bytes 98312 | tf_op jit(solution)/shard_map/ppermute | solution.py:367
  6.6 1.9 %collective-permute-done.upper = f32[4,2,8,128]{3,2,1,0:T(8,128)S(1)} collective-permute-done((f32[4,2,8,128]{3,2,1,0:T(8,128)S(1)}, f32[4,2,8,128]{3,2,1,0:T(8,128)S(1)}, u32[]{:S(2)}, u32[]{:S(2)}) %collective-permute-start) | collective-permute-done | bytes 32800 | tf_op jit(solution)/shard_map/ppermute | solution.py:367
  8.6 0.2 collective-permute-done.1.lower
  8.8 0.0 copy-start
  8.8 1.5 %collective-permute-start.3 = (f32[232,128]{1,0:T(8,128)S(1)}, f32[232,128]{1,0:T(8,128)S(1)}, u32[]{:S(2)}, u32[]{:S(2)}) collective-permute-start(f32[232,128]{1,0:T(8,128)S(1)} %shard_map.76.refs_0_), channel_id=1, source_target_pairs={{0,2},{1,3},{2,4},{3,5},{4,6},{5,7},{6,0},{7,1},{8,10},{9,11},{10,... | collective-permute-start | bytes 356360 | tf_op jit(solution)/shard_map/ppermute | solution.py:367
  10.4 1.4 %collective-permute-start.2 = (f32[232,128]{1,0:T(8,128)S(1)}, f32[232,128]{1,0:T(8,128)S(1)}, u32[]{:S(2)}, u32[]{:S(2)}) collective-permute-start(f32[232,128]{1,0:T(8,128)S(1)} %shard_map.76.refs_0_), channel_id=1, source_target_pairs={{0,6},{1,7},{2,0},{3,1},{4,2},{5,3},{6,4},{7,5},{8,14},{9,15},{10,... | collective-permute-start | bytes 356360 | tf_op jit(solution)/shard_map/ppermute | solution.py:367
  11.8 0.0 collective-permute-start.5
  11.8 1.6 %collective-permute-start.4 = (f32[232,128]{1,0:T(8,128)S(1)}, f32[232,128]{1,0:T(8,128)S(1)}, u32[]{:S(2)}, u32[]{:S(2)}) collective-permute-start(f32[232,128]{1,0:T(8,128)S(1)} %shard_map.76.refs_0_), channel_id=1, source_target_pairs={{0,5},{1,4},{2,7},{3,6},{4,1},{5,0},{6,3},{7,2},{8,13},{9,12},{10,... | collective-permute-start | bytes 356360 | tf_op jit(solution)/shard_map/ppermute | solution.py:367
  13.4 1.4 %collective-permute-done.3.refs_2_ = f32[232,128]{1,0:T(8,128)S(1)} collective-permute-done((f32[232,128]{1,0:T(8,128)S(1)}, f32[232,128]{1,0:T(8,128)S(1)}, u32[]{:S(2)}, u32[]{:S(2)}) %collective-permute-start.3) | collective-permute-done | bytes 118816 | tf_op jit(solution)/shard_map/ppermute | solution.py:367
  14.8 0.0 collective-permute-start.7
  14.8 1.3 %collective-permute-done.2.refs_1_ = f32[232,128]{1,0:T(8,128)S(1)} collective-permute-done((f32[232,128]{1,0:T(8,128)S(1)}, f32[232,128]{1,0:T(8,128)S(1)}, u32[]{:S(2)}, u32[]{:S(2)}) %collective-permute-start.2) | collective-permute-done | bytes 118816 | tf_op jit(solution)/shard_map/ppermute | solution.py:367
  16.1 0.0 collective-permute-start.6
  16.1 0.0 collective-permute-done.5.refs_4_
  16.1 0.6 %collective-permute-done.4.refs_3_ = f32[232,128]{1,0:T(8,128)S(1)} collective-permute-done((f32[232,128]{1,0:T(8,128)S(1)}, f32[232,128]{1,0:T(8,128)S(1)}, u32[]{:S(2)}, u32[]{:S(2)}) %collective-permute-start.4) | collective-permute-done | bytes 118816 | tf_op jit(solution)/shard_map/ppermute | solution.py:367
  16.7 0.0 collective-permute-done.7.refs_6_
  16.7 0.7 %collective-permute-done.6.refs_5_ = f32[232,128]{1,0:T(8,128)S(1)} collective-permute-done((f32[232,128]{1,0:T(8,128)S(1)}, f32[232,128]{1,0:T(8,128)S(1)}, u32[]{:S(2)}, u32[]{:S(2)}) %collective-permute-start.6) | collective-permute-done | bytes 118816 | tf_op jit(solution)/shard_map/ppermute | solution.py:367
  17.5 0.0 copy-done.1
  17.5 0.0 copy-done
  17.5 6.2 %shard_map.77 = (f32[19,2,16,128]{3,2,1,0:T(8,128)}, f32[3,8,512]{2,1,0:T(8,128)S(1)}, f32[32,8,128]{2,1,0:T(8,128)S(1)}) custom-call(f32[232,128]{1,0:T(8,128)S(1)} %shard_map.76.refs_0_, f32[232,128]{1,0:T(8,128)S(1)} %collective-permute-done.2.refs_1_, f32[232,128]{1,0:T(8,128)S(1)} %collective-permute-done.3.refs_2_, ...), custom_call_target="tpu_custom_call" | custom-call | tf_op jit(solution)/shard_map/pallas_call | solution.py:454
  23.7 14.1 %all_to_all.5.refs_0_ = f32[32,8,128]{2,1,0:T(8,128)S(1)} all-to-all(f32[32,8,128]{2,1,0:T(8,128)S(1)} %get-tuple-element.49), channel_id=1, replica_groups=mesh['group'=4,'dev'=8] {'group','dev'}, dimensions={0} | all-to-all | bytes 262144 | tf_op jit(solution)/shard_map/all_to_all | solution.py:479
  37.7 1.4 %shard_map.78 = (f32[4,32]{1,0:T(4,128)}, f32[4,4]{1,0:T(4,128)}, f32[48,128]{1,0:T(8,128)}, s32[1,1]{1,0:T(1,128)}, f32[8,32]{1,0:T(8,128)S(1)}) custom-call(f32[32,8,128]{2,1,0:T(8,128)S(1)} %all_to_all.5.refs_0_, f32[3,8,512]{2,1,0:T(8,128)S(1)} %get-tuple-element.80.refs_1_, bf16[3,32,512]{2,1,0:T(8,128)(2,1)S(1)} %bitcast.8), custom_call_target="tpu_custom_call" | custom-call | tf_op jit(solution)/shard_map/pallas_call | solution.py:487
  39.1 0.6 %while.11 = (s32[]{:T(128)}, f32[4,4]{1,0:T(4,128)}, f32[48,128]{1,0:T(8,128)}, f32[8,32]{1,0:T(8,128)S(1)}, f32[3,8,512]{2,1,0:T(8,128)S(1)}, /*index=5*/bf16[3,32,512]{2,1,0:T(8,128)(2,1)S(1)}) while((s32[]{:T(128)}, f32[4,4]{1,0:T(4,128)}, f32[48,128]{1,0:T(8,128)}, f32[8,32]{1,0:T(8,128)S(1)}, f32[3,8,512]{2,1,0:T(8,128)S(1)}, ...), condition=%region_2.0_spmd, body=%region_0.0_spmd | while | flops 65 | bytes 577 | solution.py:514
  (2 shorter events, 0.0 us)
Async XLA Ops:
  1.4 7.1 %collective-permute-start = (f32[4,2,8,128]{3,2,1,0:T(8,128)S(1)}, f32[4,2,8,128]{3,2,1,0:T(8,128)S(1)}, u32[]{:S(2)}, u32[]{:S(2)}) collective-permute-start(f32[4,2,8,128]{3,2,1,0:T(8,128)S(1)} %get-tuple-element.46), channel_id=1, source_target_pairs={{0,8},{8,16},{16,24},{24,0},{1,9},{9,17},{17,25},{25,1},{2,10},{10... | collective-permute-start | bytes 98312 | tf_op jit(solution)/shard_map/ppermute | solution.py:367
  4.5 12.9 %copy-start.1 = (bf16[32,3,1,512]{3,0,2,1:T(8,128)(2,1)S(1)}, bf16[32,3,1,512]{3,0,2,1:T(8,128)(2,1)}, u32[]{:S(2)}) copy-start(bf16[32,3,1,512]{3,0,2,1:T(8,128)(2,1)} %param.8) | copy-start | bytes 294916
  4.5 4.3 %collective-permute-start.1 = (f32[4,2,8,128]{3,2,1,0:T(8,128)S(1)}, f32[4,2,8,128]{3,2,1,0:T(8,128)S(1)}, u32[]{:S(2)}, u32[]{:S(2)}) collective-permute-start(f32[4,2,8,128]{3,2,1,0:T(8,128)S(1)} %get-tuple-element.47), channel_id=1, source_target_pairs={{0,24},{8,0},{16,8},{24,16},{1,25},{9,1},{17,9},{25,17},{2,26},{10... | collective-permute-start | bytes 98312 | tf_op jit(solution)/shard_map/ppermute | solution.py:367
  8.8 8.7 %copy-start = (s32[4]{0:T(128)S(1)}, s32[4]{0:T(128)}, u32[]{:S(2)}) copy-start(s32[4]{0:T(128)} %refs_7_.1) | copy-start | bytes 52
  8.8 6.0 %collective-permute-start.3 = (f32[232,128]{1,0:T(8,128)S(1)}, f32[232,128]{1,0:T(8,128)S(1)}, u32[]{:S(2)}, u32[]{:S(2)}) collective-permute-start(f32[232,128]{1,0:T(8,128)S(1)} %shard_map.76.refs_0_), channel_id=1, source_target_pairs={{0,2},{1,3},{2,4},{3,5},{4,6},{5,7},{6,0},{7,1},{8,10},{9,11},{10,... | collective-permute-start | bytes 356360 | tf_op jit(solution)/shard_map/ppermute | solution.py:367
  10.4 5.8 %collective-permute-start.2 = (f32[232,128]{1,0:T(8,128)S(1)}, f32[232,128]{1,0:T(8,128)S(1)}, u32[]{:S(2)}, u32[]{:S(2)}) collective-permute-start(f32[232,128]{1,0:T(8,128)S(1)} %shard_map.76.refs_0_), channel_id=1, source_target_pairs={{0,6},{1,7},{2,0},{3,1},{4,2},{5,3},{6,4},{7,5},{8,14},{9,15},{10,... | collective-permute-start | bytes 356360 | tf_op jit(solution)/shard_map/ppermute | solution.py:367
  11.8 4.3 %collective-permute-start.5 = (f32[232,128]{1,0:T(8,128)S(1)}, f32[232,128]{1,0:T(8,128)S(1)}, u32[]{:S(2)}, u32[]{:S(2)}) collective-permute-start(f32[232,128]{1,0:T(8,128)S(1)} %shard_map.76.refs_0_), channel_id=1, source_target_pairs={{0,1},{1,0},{2,3},{3,2},{4,5},{5,4},{6,7},{7,6},{8,9},{9,8},{10,11... | collective-permute-start | bytes 356360 | tf_op jit(solution)/shard_map/ppermute | solution.py:367
  11.8 4.9 %collective-permute-start.4 = (f32[232,128]{1,0:T(8,128)S(1)}, f32[232,128]{1,0:T(8,128)S(1)}, u32[]{:S(2)}, u32[]{:S(2)}) collective-permute-start(f32[232,128]{1,0:T(8,128)S(1)} %shard_map.76.refs_0_), channel_id=1, source_target_pairs={{0,5},{1,4},{2,7},{3,6},{4,1},{5,0},{6,3},{7,2},{8,13},{9,12},{10,... | collective-permute-start | bytes 356360 | tf_op jit(solution)/shard_map/ppermute | solution.py:367
  14.8 1.9 %collective-permute-start.7 = (f32[232,128]{1,0:T(8,128)S(1)}, f32[232,128]{1,0:T(8,128)S(1)}, u32[]{:S(2)}, u32[]{:S(2)}) collective-permute-start(f32[232,128]{1,0:T(8,128)S(1)} %collective-permute-done.3.refs_2_), channel_id=1, source_target_pairs={{0,1},{1,0},{2,3},{3,2},{4,5},{5,4},{6,7},{7,6},{8,9},{9,8},{10,11... | collective-permute-start | bytes 356360 | tf_op jit(solution)/shard_map/ppermute | solution.py:367
  16.1 1.3 %collective-permute-start.6 = (f32[232,128]{1,0:T(8,128)S(1)}, f32[232,128]{1,0:T(8,128)S(1)}, u32[]{:S(2)}, u32[]{:S(2)}) collective-permute-start(f32[232,128]{1,0:T(8,128)S(1)} %collective-permute-done.2.refs_1_), channel_id=1, source_target_pairs={{0,1},{1,0},{2,3},{3,2},{4,5},{5,4},{6,7},{7,6},{8,9},{9,8},{10,11... | collective-permute-start | bytes 356360 | tf_op jit(solution)/shard_map/ppermute | solution.py:367

commit v7 on v6

--- a/solution.py
+++ b/solution.py
@@ -21,8 +21,8 @@
 SUB = 8
 LANES = 128
 HALO = 6
-AT_ONCE = 4
-OFFSETS = [(0, 0), (2, 2), (-2, -2), (-3, 3), (1, -1), (3, 1), (-1, -3)]
+AT_ONCE = 2
+OFFSETS = [(0, 0), (2, 2), (-2, -2), (1, -1), (-3, 3), (3, 1), (-1, -3)]
 HIGHEST = lax.Precision.HIGHEST
 NT = (((1,), (1,)), ((), ()))
 VMEM_LIMIT = 48 * 1024 * 1024
@@ -340,7 +340,8 @@
     r = lax.broadcasted_iota(jnp.int32, (SUB, SUB), 0)
     c = lax.broadcasted_iota(jnp.int32, (SUB, SUB), 1)
     loss = jnp.where((r == c) & (r < count), inner + 2.0 * crossed + bent - 8.0 * small, -1.0)
-    flag[0, 0] = jnp.max(jnp.where(loss < 0.0, 0.0, 1.0)).astype(jnp.int32)
+    lost = jnp.max(jnp.max(jnp.where(loss < 0.0, 0.0, 1.0), axis=1, keepdims=True), axis=0, keepdims=True)
+    flag[...] = lost.astype(jnp.int32)
     solve(small, residuals(proj, snaps, basis), scale, factor, modes)
 
 
@@ -411,11 +412,11 @@
 def ring_blocks(own, n_dev):
     ahead = moved(own, "dev", lambda i: (i - 2) % n_dev)
     behind = moved(own, "dev", lambda i: (i + 2) % n_dev)
+    other = moved(own, "dev", lambda i: i ^ 1)
     far = moved(own, "dev", lambda i: (i + 3 if i % 2 else i - 3) % n_dev)
-    other = moved(own, "dev", lambda i: i ^ 1)
     other_ahead = moved(ahead, "dev", lambda i: i ^ 1)
     other_behind = moved(behind, "dev", lambda i: i ^ 1)
-    return [own, ahead, behind, far, other, other_ahead, other_behind]
+    return [own, ahead, behind, other, far, other_ahead, other_behind]
 
 
 def per_device(density, velocity, basis, snap_steps):
@@ -425,7 +426,6 @@
     reach = STEPS
     n_dev, n_group = lax.axis_size("dev"), lax.axis_size("group")
     vmem = pl.BlockSpec(memory_space=pltpu.VMEM)
-    smem = pl.BlockSpec(memory_space=pltpu.SMEM)
     f32 = jnp.float32
     params = pltpu.CompilerParams(vmem_limit_bytes=VMEM_LIMIT)
 
@@ -493,7 +493,7 @@
             jax.ShapeDtypeStruct((SUB, rank), f32),
         ),
         in_specs=[vmem] * (len(parts) + 2),
-        out_specs=(vmem, vmem, vmem, smem, vmem),
+        out_specs=(vmem,) * 5,
         scratch_shapes=[pltpu.VMEM((rank, lanes), f32)],
         compiler_params=params,
     )(*parts, snaps, modes)

time: 39.9 us -> 39.7 us (level)
  blocking collectives: 14.1 us -> 13.3 us
  Pallas kernels: 7.57 us -> 8.16 us
    all_to_all x1, blocking collectives: 14.1 us -> 13.3 us  [per_device(): parts = [lax.all_to_all(sums, ('group', 'dev'), 0, 0)]]
    pallas_call x1, Pallas kernels: 6.2 us -> 6.8 us  [per_device(): pl.pallas_call(lattice_kernel, out_shape=(jax.ShapeDtypeStruct((DIRS, pla...]
where the time goes in v7:
time: 39.7 us; the launch traced here: 39.5 us
  blocking collectives  13.3 us (34%)
  starting transfers between devices  9.79 us (25%)
  Pallas kernels  8.16 us (21%)
  waiting for transfers between devices  6.19 us (16%)
  other arithmetic  0.81 us (2%)
  between operations  0.66 us (2%)
  loops' own time  0.57 us (1%)
    all_to_all x1, blocking collectives, per_device(): parts = [lax.all_to_all(sums, ('group', 'dev'), 0, 0)]  13.3 us
    ppermute x8, starting transfers between devices, moved(): lax.ppermute(block, axis, [(i, target(i)) for i in range(lax.axis_size(ax...  9.79 us
    pallas_call x1, Pallas kernels, per_device(): pl.pallas_call(lattice_kernel, out_shape=(jax.ShapeDtypeStruct((DIRS, pla...  6.8 us
    ppermute x8, waiting for transfers between devices, moved(): lax.ppermute(block, axis, [(i, target(i)) for i in range(lax.axis_size(ax...  6.19 us
    pallas_call x1, Pallas kernels, per_device(): pl.pallas_call(functools.partial(finish_kernel, scale, count, rank), out_...  1.34 us
    concatenate x1, other arithmetic, per_device(): held = jnp.concatenate([density[None], velocity])  0.81 us
  transfers between devices with their start and end apart: 8, of which 6 were waited for; matrix products, arithmetic and copies ran while one was open for 0% of the time, Pallas kernels for 0%

profile of v7, /device:TPU:0, one launch (start us, length us, event | category | flops | bytes accessed | tf_op | source)
XLA Modules:
  0.0 39.5 jit_solution(16902289003524945710)
XLA Ops:
  0.6 0.8 %pad_maximum_fusion.held = f32[4,2,16,128]{3,2,1,0:T(8,128)S(1)} fusion(f32[3,2,16,128]{3,2,1,0:T(8,128)} %param.7, f32[1,2,16,128]{3,2,1,0:T(8,128)} %bitcast.10), kind=kLoop, calls=%fused_computation | loop fusion | flops 16384 | bytes 131072 | tf_op jit(solution)/shard_map/concatenate | solution.py:432
  1.4 3.1 %collective-permute-start = (f32[4,2,8,128]{3,2,1,0:T(8,128)S(1)}, f32[4,2,8,128]{3,2,1,0:T(8,128)S(1)}, u32[]{:S(2)}, u32[]{:S(2)}) collective-permute-start(f32[4,2,8,128]{3,2,1,0:T(8,128)S(1)} %get-tuple-element.46), channel_id=1, source_target_pairs={{0,8},{8,16},{16,24},{24,0},{1,9},{9,17},{17,25},{25,1},{2,10},{10... | collective-permute-start | bytes 98312 | tf_op jit(solution)/shard_map/ppermute | solution.py:368
  4.5 0.0 copy-start.1
  4.5 2.1 %collective-permute-start.1 = (f32[4,2,8,128]{3,2,1,0:T(8,128)S(1)}, f32[4,2,8,128]{3,2,1,0:T(8,128)S(1)}, u32[]{:S(2)}, u32[]{:S(2)}) collective-permute-start(f32[4,2,8,128]{3,2,1,0:T(8,128)S(1)} %get-tuple-element.47), channel_id=1, source_target_pairs={{0,24},{8,0},{16,8},{24,16},{1,25},{9,1},{17,9},{25,17},{2,26},{10... | collective-permute-start | bytes 98312 | tf_op jit(solution)/shard_map/ppermute | solution.py:368
  6.6 1.9 %collective-permute-done.upper = f32[4,2,8,128]{3,2,1,0:T(8,128)S(1)} collective-permute-done((f32[4,2,8,128]{3,2,1,0:T(8,128)S(1)}, f32[4,2,8,128]{3,2,1,0:T(8,128)S(1)}, u32[]{:S(2)}, u32[]{:S(2)}) %collective-permute-start) | collective-permute-done | bytes 32800 | tf_op jit(solution)/shard_map/ppermute | solution.py:368
  8.6 0.2 collective-permute-done.1.lower
  8.8 0.0 copy-start
  8.8 1.5 %collective-permute-start.3 = (f32[232,128]{1,0:T(8,128)S(1)}, f32[232,128]{1,0:T(8,128)S(1)}, u32[]{:S(2)}, u32[]{:S(2)}) collective-permute-start(f32[232,128]{1,0:T(8,128)S(1)} %shard_map.76.refs_0_), channel_id=1, source_target_pairs={{0,2},{1,3},{2,4},{3,5},{4,6},{5,7},{6,0},{7,1},{8,10},{9,11},{10,... | collective-permute-start | bytes 356360 | tf_op jit(solution)/shard_map/ppermute | solution.py:368
  10.4 1.4 %collective-permute-start.2 = (f32[232,128]{1,0:T(8,128)S(1)}, f32[232,128]{1,0:T(8,128)S(1)}, u32[]{:S(2)}, u32[]{:S(2)}) collective-permute-start(f32[232,128]{1,0:T(8,128)S(1)} %shard_map.76.refs_0_), channel_id=1, source_target_pairs={{0,6},{1,7},{2,0},{3,1},{4,2},{5,3},{6,4},{7,5},{8,14},{9,15},{10,... | collective-permute-start | bytes 356360 | tf_op jit(solution)/shard_map/ppermute | solution.py:368
  11.8 0.0 collective-permute-start.5
  11.8 1.6 %collective-permute-start.4 = (f32[232,128]{1,0:T(8,128)S(1)}, f32[232,128]{1,0:T(8,128)S(1)}, u32[]{:S(2)}, u32[]{:S(2)}) collective-permute-start(f32[232,128]{1,0:T(8,128)S(1)} %shard_map.76.refs_0_), channel_id=1, source_target_pairs={{0,1},{1,0},{2,3},{3,2},{4,5},{5,4},{6,7},{7,6},{8,9},{9,8},{10,11... | collective-permute-start | bytes 356360 | tf_op jit(solution)/shard_map/ppermute | solution.py:368
  13.4 1.4 %collective-permute-done.3.refs_2_ = f32[232,128]{1,0:T(8,128)S(1)} collective-permute-done((f32[232,128]{1,0:T(8,128)S(1)}, f32[232,128]{1,0:T(8,128)S(1)}, u32[]{:S(2)}, u32[]{:S(2)}) %collective-permute-start.3) | collective-permute-done | bytes 118816 | tf_op jit(solution)/shard_map/ppermute | solution.py:368
  14.8 0.0 collective-permute-start.7
  14.8 1.3 %collective-permute-done.2.refs_1_ = f32[232,128]{1,0:T(8,128)S(1)} collective-permute-done((f32[232,128]{1,0:T(8,128)S(1)}, f32[232,128]{1,0:T(8,128)S(1)}, u32[]{:S(2)}, u32[]{:S(2)}) %collective-permute-start.2) | collective-permute-done | bytes 118816 | tf_op jit(solution)/shard_map/ppermute | solution.py:368
  16.1 0.0 collective-permute-start.6
  16.1 1.2 %collective-permute-done.5.refs_4_ = f32[232,128]{1,0:T(8,128)S(1)} collective-permute-done((f32[232,128]{1,0:T(8,128)S(1)}, f32[232,128]{1,0:T(8,128)S(1)}, u32[]{:S(2)}, u32[]{:S(2)}) %collective-permute-start.5) | collective-permute-done | bytes 118816 | tf_op jit(solution)/shard_map/ppermute | solution.py:368
  17.3 0.0 collective-permute-done.4.refs_3_
  17.3 0.0 collective-permute-done.7.refs_6_
  17.3 0.2 collective-permute-done.6.refs_5_
  17.5 0.0 copy-done.1
  17.5 0.0 copy-done
  17.5 6.8 %shard_map.77 = (f32[19,2,16,128]{3,2,1,0:T(8,128)}, f32[3,8,512]{2,1,0:T(8,128)S(1)}, f32[32,8,128]{2,1,0:T(8,128)S(1)}) custom-call(f32[232,128]{1,0:T(8,128)S(1)} %shard_map.76.refs_0_, f32[232,128]{1,0:T(8,128)S(1)} %collective-permute-done.2.refs_1_, f32[232,128]{1,0:T(8,128)S(1)} %collective-permute-done.3.refs_2_, ...), custom_call_target="tpu_custom_call" | custom-call | tf_op jit(solution)/shard_map/pallas_call | solution.py:454
  24.3 13.3 %all_to_all.5.refs_0_ = f32[32,8,128]{2,1,0:T(8,128)S(1)} all-to-all(f32[32,8,128]{2,1,0:T(8,128)S(1)} %get-tuple-element.49), channel_id=1, replica_groups=mesh['group'=4,'dev'=8] {'group','dev'}, dimensions={0} | all-to-all | bytes 262144 | tf_op jit(solution)/shard_map/all_to_all | solution.py:479
  37.6 1.3 %shard_map.78 = (f32[4,32]{1,0:T(4,128)}, f32[4,4]{1,0:T(4,128)}, f32[48,128]{1,0:T(8,128)}, s32[1,1]{1,0:T(1,128)}, f32[8,32]{1,0:T(8,128)S(1)}) custom-call(f32[32,8,128]{2,1,0:T(8,128)S(1)} %all_to_all.5.refs_0_, f32[3,8,512]{2,1,0:T(8,128)S(1)} %get-tuple-element.80.refs_1_, bf16[3,32,512]{2,1,0:T(8,128)(2,1)S(1)} %bitcast.8), custom_call_target="tpu_custom_call" | custom-call | tf_op jit(solution)/shard_map/pallas_call | solution.py:487
  38.9 0.6 %while.11 = (s32[]{:T(128)}, f32[4,4]{1,0:T(4,128)}, f32[48,128]{1,0:T(8,128)}, f32[8,32]{1,0:T(8,128)S(1)}, f32[3,8,512]{2,1,0:T(8,128)S(1)}, /*index=5*/bf16[3,32,512]{2,1,0:T(8,128)(2,1)S(1)}) while((s32[]{:T(128)}, f32[4,4]{1,0:T(4,128)}, f32[48,128]{1,0:T(8,128)}, f32[8,32]{1,0:T(8,128)S(1)}, f32[3,8,512]{2,1,0:T(8,128)S(1)}, ...), condition=%region_2.0_spmd, body=%region_0.0_spmd | while | flops 65 | bytes 577 | solution.py:514
  (2 shorter events, 0.0 us)
Async XLA Ops:
  1.4 7.1 %collective-permute-start = (f32[4,2,8,128]{3,2,1,0:T(8,128)S(1)}, f32[4,2,8,128]{3,2,1,0:T(8,128)S(1)}, u32[]{:S(2)}, u32[]{:S(2)}) collective-permute-start(f32[4,2,8,128]{3,2,1,0:T(8,128)S(1)} %get-tuple-element.46), channel_id=1, source_target_pairs={{0,8},{8,16},{16,24},{24,0},{1,9},{9,17},{17,25},{25,1},{2,10},{10... | collective-permute-start | bytes 98312 | tf_op jit(solution)/shard_map/ppermute | solution.py:368
  4.5 12.9 %copy-start.1 = (bf16[32,3,1,512]{3,0,2,1:T(8,128)(2,1)S(1)}, bf16[32,3,1,512]{3,0,2,1:T(8,128)(2,1)}, u32[]{:S(2)}) copy-start(bf16[32,3,1,512]{3,0,2,1:T(8,128)(2,1)} %param.8) | copy-start | bytes 294916
  4.5 4.3 %collective-permute-start.1 = (f32[4,2,8,128]{3,2,1,0:T(8,128)S(1)}, f32[4,2,8,128]{3,2,1,0:T(8,128)S(1)}, u32[]{:S(2)}, u32[]{:S(2)}) collective-permute-start(f32[4,2,8,128]{3,2,1,0:T(8,128)S(1)} %get-tuple-element.47), channel_id=1, source_target_pairs={{0,24},{8,0},{16,8},{24,16},{1,25},{9,1},{17,9},{25,17},{2,26},{10... | collective-permute-start | bytes 98312 | tf_op jit(solution)/shard_map/ppermute | solution.py:368
  8.8 8.7 %copy-start = (s32[4]{0:T(128)S(1)}, s32[4]{0:T(128)}, u32[]{:S(2)}) copy-start(s32[4]{0:T(128)} %refs_7_.1) | copy-start | bytes 52
  8.8 6.0 %collective-permute-start.3 = (f32[232,128]{1,0:T(8,128)S(1)}, f32[232,128]{1,0:T(8,128)S(1)}, u32[]{:S(2)}, u32[]{:S(2)}) collective-permute-start(f32[232,128]{1,0:T(8,128)S(1)} %shard_map.76.refs_0_), channel_id=1, source_target_pairs={{0,2},{1,3},{2,4},{3,5},{4,6},{5,7},{6,0},{7,1},{8,10},{9,11},{10,... | collective-permute-start | bytes 356360 | tf_op jit(solution)/shard_map/ppermute | solution.py:368
  10.4 5.8 %collective-permute-start.2 = (f32[232,128]{1,0:T(8,128)S(1)}, f32[232,128]{1,0:T(8,128)S(1)}, u32[]{:S(2)}, u32[]{:S(2)}) collective-permute-start(f32[232,128]{1,0:T(8,128)S(1)} %shard_map.76.refs_0_), channel_id=1, source_target_pairs={{0,6},{1,7},{2,0},{3,1},{4,2},{5,3},{6,4},{7,5},{8,14},{9,15},{10,... | collective-permute-start | bytes 356360 | tf_op jit(solution)/shard_map/ppermute | solution.py:368
  11.8 5.5 %collective-permute-start.5 = (f32[232,128]{1,0:T(8,128)S(1)}, f32[232,128]{1,0:T(8,128)S(1)}, u32[]{:S(2)}, u32[]{:S(2)}) collective-permute-start(f32[232,128]{1,0:T(8,128)S(1)} %shard_map.76.refs_0_), channel_id=1, source_target_pairs={{0,5},{1,4},{2,7},{3,6},{4,1},{5,0},{6,3},{7,2},{8,13},{9,12},{10,... | collective-permute-start | bytes 356360 | tf_op jit(solution)/shard_map/ppermute | solution.py:368
  11.8 5.5 %collective-permute-start.4 = (f32[232,128]{1,0:T(8,128)S(1)}, f32[232,128]{1,0:T(8,128)S(1)}, u32[]{:S(2)}, u32[]{:S(2)}) collective-permute-start(f32[232,128]{1,0:T(8,128)S(1)} %shard_map.76.refs_0_), channel_id=1, source_target_pairs={{0,1},{1,0},{2,3},{3,2},{4,5},{5,4},{6,7},{7,6},{8,9},{9,8},{10,11... | collective-permute-start | bytes 356360 | tf_op jit(solution)/shard_map/ppermute | solution.py:368
  14.8 2.5 %collective-permute-start.7 = (f32[232,128]{1,0:T(8,128)S(1)}, f32[232,128]{1,0:T(8,128)S(1)}, u32[]{:S(2)}, u32[]{:S(2)}) collective-permute-start(f32[232,128]{1,0:T(8,128)S(1)} %collective-permute-done.3.refs_2_), channel_id=1, source_target_pairs={{0,1},{1,0},{2,3},{3,2},{4,5},{5,4},{6,7},{7,6},{8,9},{9,8},{10,11... | collective-permute-start | bytes 356360 | tf_op jit(solution)/shard_map/ppermute | solution.py:368
  16.1 1.3 %collective-permute-start.6 = (f32[232,128]{1,0:T(8,128)S(1)}, f32[232,128]{1,0:T(8,128)S(1)}, u32[]{:S(2)}, u32[]{:S(2)}) collective-permute-start(f32[232,128]{1,0:T(8,128)S(1)} %collective-permute-done.2.refs_1_), channel_id=1, source_target_pairs={{0,1},{1,0},{2,3},{3,2},{4,5},{5,4},{6,7},{7,6},{8,9},{9,8},{10,11... | collective-permute-start | bytes 356360 | tf_op jit(solution)/shard_map/ppermute | solution.py:368

commit v8 on v7

--- a/solution.py
+++ b/solution.py
@@ -21,7 +21,7 @@
 SUB = 8
 LANES = 128
 HALO = 6
-AT_ONCE = 2
+AT_ONCE = 6
 OFFSETS = [(0, 0), (2, 2), (-2, -2), (1, -1), (-3, 3), (3, 1), (-1, -3)]
 HIGHEST = lax.Precision.HIGHEST
 NT = (((1,), (1,)), ((), ()))
@@ -176,7 +176,7 @@
     src, dst = ping, pong
     for step in range(1, STEPS):
         size = span - 2 * step
-        together = math.gcd(size, AT_ONCE)
+        together = max(n for n in range(1, AT_ONCE + 1) if size % n == 0)
 
         def later(n, carry, src=src, dst=dst, step=step, together=together):
             for x in [step + together * n + m for m in range(together)]:
@@ -195,7 +195,10 @@
                 put_speed(x, held)
             return carry
 
-        lax.fori_loop(0, size // together, later, 0)
+        if together == size:
+            later(0, 0)
+        else:
+            lax.fori_loop(0, size // together, later, 0)
         keep_view(step)
         src, dst = dst, src
 

time: 39.7 us -> 38.5 us (0.970)
  Pallas kernels: 8.16 us -> 6.98 us
    pallas_call x1, Pallas kernels: 6.8 us -> 5.62 us  [per_device(): pl.pallas_call(lattice_kernel, out_shape=(jax.ShapeDtypeStruct((DIRS, pla...]
where the time goes in v8:
time: 38.5 us; the launch traced here: 38.3 us
  blocking collectives  13.3 us (35%)
  starting transfers between devices  9.79 us (25%)
  Pallas kernels  6.98 us (18%)
  waiting for transfers between devices  6.19 us (16%)
  other arithmetic  0.81 us (2%)
  between operations  0.66 us (2%)
  loops' own time  0.57 us (1%)
    all_to_all x1, blocking collectives, per_device(): parts = [lax.all_to_all(sums, ('group', 'dev'), 0, 0)]  13.3 us
    ppermute x8, starting transfers between devices, moved(): lax.ppermute(block, axis, [(i, target(i)) for i in range(lax.axis_size(ax...  9.79 us
    ppermute x8, waiting for transfers between devices, moved(): lax.ppermute(block, axis, [(i, target(i)) for i in range(lax.axis_size(ax...  6.19 us
    pallas_call x1, Pallas kernels, per_device(): pl.pallas_call(lattice_kernel, out_shape=(jax.ShapeDtypeStruct((DIRS, pla...  5.62 us
    pallas_call x1, Pallas kernels, per_device(): pl.pallas_call(functools.partial(finish_kernel, scale, count, rank), out_...  1.34 us
    concatenate x1, other arithmetic, per_device(): held = jnp.concatenate([density[None], velocity])  0.81 us
  transfers between devices with their start and end apart: 8, of which 6 were waited for; matrix products, arithmetic and copies ran while one was open for 0% of the time, Pallas kernels for 0%

profile of v8, /device:TPU:0, one launch (start us, length us, event | category | flops | bytes accessed | tf_op | source)
XLA Modules:
  0.0 38.3 jit_solution(11103839957416054153)
XLA Ops:
  0.6 0.8 %pad_maximum_fusion.held = f32[4,2,16,128]{3,2,1,0:T(8,128)S(1)} fusion(f32[3,2,16,128]{3,2,1,0:T(8,128)} %param.7, f32[1,2,16,128]{3,2,1,0:T(8,128)} %bitcast.10), kind=kLoop, calls=%fused_computation | loop fusion | flops 16384 | bytes 131072 | tf_op jit(solution)/shard_map/concatenate | solution.py:435
  1.4 3.1 %collective-permute-start = (f32[4,2,8,128]{3,2,1,0:T(8,128)S(1)}, f32[4,2,8,128]{3,2,1,0:T(8,128)S(1)}, u32[]{:S(2)}, u32[]{:S(2)}) collective-permute-start(f32[4,2,8,128]{3,2,1,0:T(8,128)S(1)} %get-tuple-element.46), channel_id=1, source_target_pairs={{0,8},{8,16},{16,24},{24,0},{1,9},{9,17},{17,25},{25,1},{2,10},{10... | collective-permute-start | bytes 98312 | tf_op jit(solution)/shard_map/ppermute | solution.py:371
  4.5 0.0 copy-start.1
  4.5 2.1 %collective-permute-start.1 = (f32[4,2,8,128]{3,2,1,0:T(8,128)S(1)}, f32[4,2,8,128]{3,2,1,0:T(8,128)S(1)}, u32[]{:S(2)}, u32[]{:S(2)}) collective-permute-start(f32[4,2,8,128]{3,2,1,0:T(8,128)S(1)} %get-tuple-element.47), channel_id=1, source_target_pairs={{0,24},{8,0},{16,8},{24,16},{1,25},{9,1},{17,9},{25,17},{2,26},{10... | collective-permute-start | bytes 98312 | tf_op jit(solution)/shard_map/ppermute | solution.py:371
  6.6 1.9 %collective-permute-done.upper = f32[4,2,8,128]{3,2,1,0:T(8,128)S(1)} collective-permute-done((f32[4,2,8,128]{3,2,1,0:T(8,128)S(1)}, f32[4,2,8,128]{3,2,1,0:T(8,128)S(1)}, u32[]{:S(2)}, u32[]{:S(2)}) %collective-permute-start) | collective-permute-done | bytes 32800 | tf_op jit(solution)/shard_map/ppermute | solution.py:371
  8.6 0.2 collective-permute-done.1.lower
  8.8 0.0 copy-start
  8.8 1.5 %collective-permute-start.3 = (f32[232,128]{1,0:T(8,128)S(1)}, f32[232,128]{1,0:T(8,128)S(1)}, u32[]{:S(2)}, u32[]{:S(2)}) collective-permute-start(f32[232,128]{1,0:T(8,128)S(1)} %shard_map.76.refs_0_), channel_id=1, source_target_pairs={{0,2},{1,3},{2,4},{3,5},{4,6},{5,7},{6,0},{7,1},{8,10},{9,11},{10,... | collective-permute-start | bytes 356360 | tf_op jit(solution)/shard_map/ppermute | solution.py:371
  10.4 1.4 %collective-permute-start.2 = (f32[232,128]{1,0:T(8,128)S(1)}, f32[232,128]{1,0:T(8,128)S(1)}, u32[]{:S(2)}, u32[]{:S(2)}) collective-permute-start(f32[232,128]{1,0:T(8,128)S(1)} %shard_map.76.refs_0_), channel_id=1, source_target_pairs={{0,6},{1,7},{2,0},{3,1},{4,2},{5,3},{6,4},{7,5},{8,14},{9,15},{10,... | collective-permute-start | bytes 356360 | tf_op jit(solution)/shard_map/ppermute | solution.py:371
  11.8 0.0 collective-permute-start.5
  11.8 1.6 %collective-permute-start.4 = (f32[232,128]{1,0:T(8,128)S(1)}, f32[232,128]{1,0:T(8,128)S(1)}, u32[]{:S(2)}, u32[]{:S(2)}) collective-permute-start(f32[232,128]{1,0:T(8,128)S(1)} %shard_map.76.refs_0_), channel_id=1, source_target_pairs={{0,1},{1,0},{2,3},{3,2},{4,5},{5,4},{6,7},{7,6},{8,9},{9,8},{10,11... | collective-permute-start | bytes 356360 | tf_op jit(solution)/shard_map/ppermute | solution.py:371
  13.4 1.4 %collective-permute-done.3.refs_2_ = f32[232,128]{1,0:T(8,128)S(1)} collective-permute-done((f32[232,128]{1,0:T(8,128)S(1)}, f32[232,128]{1,0:T(8,128)S(1)}, u32[]{:S(2)}, u32[]{:S(2)}) %collective-permute-start.3) | collective-permute-done | bytes 118816 | tf_op jit(solution)/shard_map/ppermute | solution.py:371
  14.8 0.0 collective-permute-start.7
  14.8 1.3 %collective-permute-done.2.refs_1_ = f32[232,128]{1,0:T(8,128)S(1)} collective-permute-done((f32[232,128]{1,0:T(8,128)S(1)}, f32[232,128]{1,0:T(8,128)S(1)}, u32[]{:S(2)}, u32[]{:S(2)}) %collective-permute-start.2) | collective-permute-done | bytes 118816 | tf_op jit(solution)/shard_map/ppermute | solution.py:371
  16.1 0.0 collective-permute-start.6
  16.1 1.2 %collective-permute-done.5.refs_4_ = f32[232,128]{1,0:T(8,128)S(1)} collective-permute-done((f32[232,128]{1,0:T(8,128)S(1)}, f32[232,128]{1,0:T(8,128)S(1)}, u32[]{:S(2)}, u32[]{:S(2)}) %collective-permute-start.5) | collective-permute-done | bytes 118816 | tf_op jit(solution)/shard_map/ppermute | solution.py:371
  17.3 0.0 collective-permute-done.4.refs_3_
  17.3 0.0 collective-permute-done.7.refs_6_
  17.3 0.2 collective-permute-done.6.refs_5_
  17.5 0.0 copy-done.1
  17.5 0.0 copy-done
  17.5 5.6 %shard_map.77 = (f32[19,2,16,128]{3,2,1,0:T(8,128)}, f32[3,8,512]{2,1,0:T(8,128)S(1)}, f32[32,8,128]{2,1,0:T(8,128)S(1)}) custom-call(f32[232,128]{1,0:T(8,128)S(1)} %shard_map.76.refs_0_, f32[232,128]{1,0:T(8,128)S(1)} %collective-permute-done.2.refs_1_, f32[232,128]{1,0:T(8,128)S(1)} %collective-permute-done.3.refs_2_, ...), custom_call_target="tpu_custom_call" | custom-call | tf_op jit(solution)/shard_map/pallas_call | solution.py:457
  23.1 13.3 %all_to_all.5.refs_0_ = f32[32,8,128]{2,1,0:T(8,128)S(1)} all-to-all(f32[32,8,128]{2,1,0:T(8,128)S(1)} %get-tuple-element.49), channel_id=1, replica_groups=mesh['group'=4,'dev'=8] {'group','dev'}, dimensions={0} | all-to-all | bytes 262144 | tf_op jit(solution)/shard_map/all_to_all | solution.py:482
  36.4 1.3 %shard_map.78 = (f32[4,32]{1,0:T(4,128)}, f32[4,4]{1,0:T(4,128)}, f32[48,128]{1,0:T(8,128)}, s32[1,1]{1,0:T(1,128)}, f32[8,32]{1,0:T(8,128)S(1)}) custom-call(f32[32,8,128]{2,1,0:T(8,128)S(1)} %all_to_all.5.refs_0_, f32[3,8,512]{2,1,0:T(8,128)S(1)} %get-tuple-element.80.refs_1_, bf16[3,32,512]{2,1,0:T(8,128)(2,1)S(1)} %bitcast.8), custom_call_target="tpu_custom_call" | custom-call | tf_op jit(solution)/shard_map/pallas_call | solution.py:490
  37.7 0.6 %while.11 = (s32[]{:T(128)}, f32[4,4]{1,0:T(4,128)}, f32[48,128]{1,0:T(8,128)}, f32[8,32]{1,0:T(8,128)S(1)}, f32[3,8,512]{2,1,0:T(8,128)S(1)}, /*index=5*/bf16[3,32,512]{2,1,0:T(8,128)(2,1)S(1)}) while((s32[]{:T(128)}, f32[4,4]{1,0:T(4,128)}, f32[48,128]{1,0:T(8,128)}, f32[8,32]{1,0:T(8,128)S(1)}, f32[3,8,512]{2,1,0:T(8,128)S(1)}, ...), condition=%region_2.0_spmd, body=%region_0.0_spmd | while | flops 65 | bytes 577 | solution.py:517
  (2 shorter events, 0.0 us)
Async XLA Ops:
  1.4 7.1 %collective-permute-start = (f32[4,2,8,128]{3,2,1,0:T(8,128)S(1)}, f32[4,2,8,128]{3,2,1,0:T(8,128)S(1)}, u32[]{:S(2)}, u32[]{:S(2)}) collective-permute-start(f32[4,2,8,128]{3,2,1,0:T(8,128)S(1)} %get-tuple-element.46), channel_id=1, source_target_pairs={{0,8},{8,16},{16,24},{24,0},{1,9},{9,17},{17,25},{25,1},{2,10},{10... | collective-permute-start | bytes 98312 | tf_op jit(solution)/shard_map/ppermute | solution.py:371
  4.5 12.9 %copy-start.1 = (bf16[32,3,1,512]{3,0,2,1:T(8,128)(2,1)S(1)}, bf16[32,3,1,512]{3,0,2,1:T(8,128)(2,1)}, u32[]{:S(2)}) copy-start(bf16[32,3,1,512]{3,0,2,1:T(8,128)(2,1)} %param.8) | copy-start | bytes 294916
  4.5 4.3 %collective-permute-start.1 = (f32[4,2,8,128]{3,2,1,0:T(8,128)S(1)}, f32[4,2,8,128]{3,2,1,0:T(8,128)S(1)}, u32[]{:S(2)}, u32[]{:S(2)}) collective-permute-start(f32[4,2,8,128]{3,2,1,0:T(8,128)S(1)} %get-tuple-element.47), channel_id=1, source_target_pairs={{0,24},{8,0},{16,8},{24,16},{1,25},{9,1},{17,9},{25,17},{2,26},{10... | collective-permute-start | bytes 98312 | tf_op jit(solution)/shard_map/ppermute | solution.py:371
  8.8 8.7 %copy-start = (s32[4]{0:T(128)S(1)}, s32[4]{0:T(128)}, u32[]{:S(2)}) copy-start(s32[4]{0:T(128)} %refs_7_.1) | copy-start | bytes 52
  8.8 6.0 %collective-permute-start.3 = (f32[232,128]{1,0:T(8,128)S(1)}, f32[232,128]{1,0:T(8,128)S(1)}, u32[]{:S(2)}, u32[]{:S(2)}) collective-permute-start(f32[232,128]{1,0:T(8,128)S(1)} %shard_map.76.refs_0_), channel_id=1, source_target_pairs={{0,2},{1,3},{2,4},{3,5},{4,6},{5,7},{6,0},{7,1},{8,10},{9,11},{10,... | collective-permute-start | bytes 356360 | tf_op jit(solution)/shard_map/ppermute | solution.py:371
  10.4 5.8 %collective-permute-start.2 = (f32[232,128]{1,0:T(8,128)S(1)}, f32[232,128]{1,0:T(8,128)S(1)}, u32[]{:S(2)}, u32[]{:S(2)}) collective-permute-start(f32[232,128]{1,0:T(8,128)S(1)} %shard_map.76.refs_0_), channel_id=1, source_target_pairs={{0,6},{1,7},{2,0},{3,1},{4,2},{5,3},{6,4},{7,5},{8,14},{9,15},{10,... | collective-permute-start | bytes 356360 | tf_op jit(solution)/shard_map/ppermute | solution.py:371
  11.8 5.5 %collective-permute-start.5 = (f32[232,128]{1,0:T(8,128)S(1)}, f32[232,128]{1,0:T(8,128)S(1)}, u32[]{:S(2)}, u32[]{:S(2)}) collective-permute-start(f32[232,128]{1,0:T(8,128)S(1)} %shard_map.76.refs_0_), channel_id=1, source_target_pairs={{0,5},{1,4},{2,7},{3,6},{4,1},{5,0},{6,3},{7,2},{8,13},{9,12},{10,... | collective-permute-start | bytes 356360 | tf_op jit(solution)/shard_map/ppermute | solution.py:371
  11.8 5.5 %collective-permute-start.4 = (f32[232,128]{1,0:T(8,128)S(1)}, f32[232,128]{1,0:T(8,128)S(1)}, u32[]{:S(2)}, u32[]{:S(2)}) collective-permute-start(f32[232,128]{1,0:T(8,128)S(1)} %shard_map.76.refs_0_), channel_id=1, source_target_pairs={{0,1},{1,0},{2,3},{3,2},{4,5},{5,4},{6,7},{7,6},{8,9},{9,8},{10,11... | collective-permute-start | bytes 356360 | tf_op jit(solution)/shard_map/ppermute | solution.py:371
  14.8 2.5 %collective-permute-start.7 = (f32[232,128]{1,0:T(8,128)S(1)}, f32[232,128]{1,0:T(8,128)S(1)}, u32[]{:S(2)}, u32[]{:S(2)}) collective-permute-start(f32[232,128]{1,0:T(8,128)S(1)} %collective-permute-done.3.refs_2_), channel_id=1, source_target_pairs={{0,1},{1,0},{2,3},{3,2},{4,5},{5,4},{6,7},{7,6},{8,9},{9,8},{10,11... | collective-permute-start | bytes 356360 | tf_op jit(solution)/shard_map/ppermute | solution.py:371
  16.1 1.3 %collective-permute-start.6 = (f32[232,128]{1,0:T(8,128)S(1)}, f32[232,128]{1,0:T(8,128)S(1)}, u32[]{:S(2)}, u32[]{:S(2)}) collective-permute-start(f32[232,128]{1,0:T(8,128)S(1)} %collective-permute-done.2.refs_1_), channel_id=1, source_target_pairs={{0,1},{1,0},{2,3},{3,2},{4,5},{5,4},{6,7},{7,6},{8,9},{9,8},{10,11... | collective-permute-start | bytes 356360 | tf_op jit(solution)/shard_map/ppermute | solution.py:371

commit v9 on v8

--- a/solution.py
+++ b/solution.py
@@ -21,7 +21,7 @@
 SUB = 8
 LANES = 128
 HALO = 6
-AT_ONCE = 6
+AT_ONCE = 12
 OFFSETS = [(0, 0), (2, 2), (-2, -2), (1, -1), (-3, 3), (3, 1), (-1, -3)]
 HIGHEST = lax.Precision.HIGHEST
 NT = (((1,), (1,)), ((), ()))

time: 38.5 us -> 37.8 us (0.982)
  Pallas kernels: 6.98 us -> 6.23 us
    pallas_call x1, Pallas kernels: 5.62 us -> 4.87 us  [per_device(): pl.pallas_call(lattice_kernel, out_shape=(jax.ShapeDtypeStruct((DIRS, pla...]
where the time goes in v9:
time: 37.8 us; the launch traced here: 37.6 us
  blocking collectives  13.3 us (35%)
  starting transfers between devices  9.79 us (26%)
  Pallas kernels  6.23 us (16%)
  waiting for transfers between devices  6.19 us (16%)
  other arithmetic  0.81 us (2%)
  between operations  0.66 us (2%)
  loops' own time  0.57 us (2%)
    all_to_all x1, blocking collectives, per_device(): parts = [lax.all_to_all(sums, ('group', 'dev'), 0, 0)]  13.3 us
    ppermute x8, starting transfers between devices, moved(): lax.ppermute(block, axis, [(i, target(i)) for i in range(lax.axis_size(ax...  9.79 us
    ppermute x8, waiting for transfers between devices, moved(): lax.ppermute(block, axis, [(i, target(i)) for i in range(lax.axis_size(ax...  6.19 us
    pallas_call x1, Pallas kernels, per_device(): pl.pallas_call(lattice_kernel, out_shape=(jax.ShapeDtypeStruct((DIRS, pla...  4.87 us
    pallas_call x1, Pallas kernels, per_device(): pl.pallas_call(functools.partial(finish_kernel, scale, count, rank), out_...  1.34 us
    concatenate x1, other arithmetic, per_device(): held = jnp.concatenate([density[None], velocity])  0.81 us
  transfers between devices with their start and end apart: 8, of which 6 were waited for; matrix products, arithmetic and copies ran while one was open for 0% of the time, Pallas kernels for 0%

profile of v9, /device:TPU:0, one launch (start us, length us, event | category | flops | bytes accessed | tf_op | source)
XLA Modules:
  0.0 37.6 jit_solution(13424814216001908154)
XLA Ops:
  0.6 0.8 %pad_maximum_fusion.held = f32[4,2,16,128]{3,2,1,0:T(8,128)S(1)} fusion(f32[3,2,16,128]{3,2,1,0:T(8,128)} %param.7, f32[1,2,16,128]{3,2,1,0:T(8,128)} %bitcast.10), kind=kLoop, calls=%fused_computation | loop fusion | flops 16384 | bytes 131072 | tf_op jit(solution)/shard_map/concatenate | solution.py:435
  1.4 3.1 %collective-permute-start = (f32[4,2,8,128]{3,2,1,0:T(8,128)S(1)}, f32[4,2,8,128]{3,2,1,0:T(8,128)S(1)}, u32[]{:S(2)}, u32[]{:S(2)}) collective-permute-start(f32[4,2,8,128]{3,2,1,0:T(8,128)S(1)} %get-tuple-element.46), channel_id=1, source_target_pairs={{0,8},{8,16},{16,24},{24,0},{1,9},{9,17},{17,25},{25,1},{2,10},{10... | collective-permute-start | bytes 98312 | tf_op jit(solution)/shard_map/ppermute | solution.py:371
  4.5 0.0 copy-start.1
  4.5 2.1 %collective-permute-start.1 = (f32[4,2,8,128]{3,2,1,0:T(8,128)S(1)}, f32[4,2,8,128]{3,2,1,0:T(8,128)S(1)}, u32[]{:S(2)}, u32[]{:S(2)}) collective-permute-start(f32[4,2,8,128]{3,2,1,0:T(8,128)S(1)} %get-tuple-element.47), channel_id=1, source_target_pairs={{0,24},{8,0},{16,8},{24,16},{1,25},{9,1},{17,9},{25,17},{2,26},{10... | collective-permute-start | bytes 98312 | tf_op jit(solution)/shard_map/ppermute | solution.py:371
  6.6 1.9 %collective-permute-done.upper = f32[4,2,8,128]{3,2,1,0:T(8,128)S(1)} collective-permute-done((f32[4,2,8,128]{3,2,1,0:T(8,128)S(1)}, f32[4,2,8,128]{3,2,1,0:T(8,128)S(1)}, u32[]{:S(2)}, u32[]{:S(2)}) %collective-permute-start) | collective-permute-done | bytes 32800 | tf_op jit(solution)/shard_map/ppermute | solution.py:371
  8.6 0.2 collective-permute-done.1.lower
  8.8 0.0 copy-start
  8.8 1.5 %collective-permute-start.3 = (f32[232,128]{1,0:T(8,128)S(1)}, f32[232,128]{1,0:T(8,128)S(1)}, u32[]{:S(2)}, u32[]{:S(2)}) collective-permute-start(f32[232,128]{1,0:T(8,128)S(1)} %shard_map.76.refs_0_), channel_id=1, source_target_pairs={{0,2},{1,3},{2,4},{3,5},{4,6},{5,7},{6,0},{7,1},{8,10},{9,11},{10,... | collective-permute-start | bytes 356360 | tf_op jit(solution)/shard_map/ppermute | solution.py:371
  10.4 1.4 %collective-permute-start.2 = (f32[232,128]{1,0:T(8,128)S(1)}, f32[232,128]{1,0:T(8,128)S(1)}, u32[]{:S(2)}, u32[]{:S(2)}) collective-permute-start(f32[232,128]{1,0:T(8,128)S(1)} %shard_map.76.refs_0_), channel_id=1, source_target_pairs={{0,6},{1,7},{2,0},{3,1},{4,2},{5,3},{6,4},{7,5},{8,14},{9,15},{10,... | collective-permute-start | bytes 356360 | tf_op jit(solution)/shard_map/ppermute | solution.py:371
  11.8 0.0 collective-permute-start.5
  11.8 1.6 %collective-permute-start.4 = (f32[232,128]{1,0:T(8,128)S(1)}, f32[232,128]{1,0:T(8,128)S(1)}, u32[]{:S(2)}, u32[]{:S(2)}) collective-permute-start(f32[232,128]{1,0:T(8,128)S(1)} %shard_map.76.refs_0_), channel_id=1, source_target_pairs={{0,1},{1,0},{2,3},{3,2},{4,5},{5,4},{6,7},{7,6},{8,9},{9,8},{10,11... | collective-permute-start | bytes 356360 | tf_op jit(solution)/shard_map/ppermute | solution.py:371
  13.4 1.4 %collective-permute-done.3.refs_2_ = f32[232,128]{1,0:T(8,128)S(1)} collective-permute-done((f32[232,128]{1,0:T(8,128)S(1)}, f32[232,128]{1,0:T(8,128)S(1)}, u32[]{:S(2)}, u32[]{:S(2)}) %collective-permute-start.3) | collective-permute-done | bytes 118816 | tf_op jit(solution)/shard_map/ppermute | solution.py:371
  14.8 0.0 collective-permute-start.7
  14.8 1.3 %collective-permute-done.2.refs_1_ = f32[232,128]{1,0:T(8,128)S(1)} collective-permute-done((f32[232,128]{1,0:T(8,128)S(1)}, f32[232,128]{1,0:T(8,128)S(1)}, u32[]{:S(2)}, u32[]{:S(2)}) %collective-permute-start.2) | collective-permute-done | bytes 118816 | tf_op jit(solution)/shard_map/ppermute | solution.py:371
  16.1 0.0 collective-permute-start.6
  16.1 1.2 %collective-permute-done.5.refs_4_ = f32[232,128]{1,0:T(8,128)S(1)} collective-permute-done((f32[232,128]{1,0:T(8,128)S(1)}, f32[232,128]{1,0:T(8,128)S(1)}, u32[]{:S(2)}, u32[]{:S(2)}) %collective-permute-start.5) | collective-permute-done | bytes 118816 | tf_op jit(solution)/shard_map/ppermute | solution.py:371
  17.3 0.0 collective-permute-done.4.refs_3_
  17.3 0.0 collective-permute-done.7.refs_6_
  17.3 0.2 collective-permute-done.6.refs_5_
  17.5 0.0 copy-done.1
  17.5 0.0 copy-done
  17.5 4.9 %shard_map.77 = (f32[19,2,16,128]{3,2,1,0:T(8,128)}, f32[3,8,512]{2,1,0:T(8,128)S(1)}, f32[32,8,128]{2,1,0:T(8,128)S(1)}) custom-call(f32[232,128]{1,0:T(8,128)S(1)} %shard_map.76.refs_0_, f32[232,128]{1,0:T(8,128)S(1)} %collective-permute-done.2.refs_1_, f32[232,128]{1,0:T(8,128)S(1)} %collective-permute-done.3.refs_2_, ...), custom_call_target="tpu_custom_call" | custom-call | tf_op jit(solution)/shard_map/pallas_call | solution.py:457
  22.3 13.3 %all_to_all.5.refs_0_ = f32[32,8,128]{2,1,0:T(8,128)S(1)} all-to-all(f32[32,8,128]{2,1,0:T(8,128)S(1)} %get-tuple-element.49), channel_id=1, replica_groups=mesh['group'=4,'dev'=8] {'group','dev'}, dimensions={0} | all-to-all | bytes 262144 | tf_op jit(solution)/shard_map/all_to_all | solution.py:482
  35.7 1.3 %shard_map.78 = (f32[4,32]{1,0:T(4,128)}, f32[4,4]{1,0:T(4,128)}, f32[48,128]{1,0:T(8,128)}, s32[1,1]{1,0:T(1,128)}, f32[8,32]{1,0:T(8,128)S(1)}) custom-call(f32[32,8,128]{2,1,0:T(8,128)S(1)} %all_to_all.5.refs_0_, f32[3,8,512]{2,1,0:T(8,128)S(1)} %get-tuple-element.80.refs_1_, bf16[3,32,512]{2,1,0:T(8,128)(2,1)S(1)} %bitcast.8), custom_call_target="tpu_custom_call" | custom-call | tf_op jit(solution)/shard_map/pallas_call | solution.py:490
  37.0 0.6 %while.11 = (s32[]{:T(128)}, f32[4,4]{1,0:T(4,128)}, f32[48,128]{1,0:T(8,128)}, f32[8,32]{1,0:T(8,128)S(1)}, f32[3,8,512]{2,1,0:T(8,128)S(1)}, /*index=5*/bf16[3,32,512]{2,1,0:T(8,128)(2,1)S(1)}) while((s32[]{:T(128)}, f32[4,4]{1,0:T(4,128)}, f32[48,128]{1,0:T(8,128)}, f32[8,32]{1,0:T(8,128)S(1)}, f32[3,8,512]{2,1,0:T(8,128)S(1)}, ...), condition=%region_2.0_spmd, body=%region_0.0_spmd | while | flops 65 | bytes 577 | solution.py:517
  (2 shorter events, 0.0 us)
Async XLA Ops:
  1.4 7.1 %collective-permute-start = (f32[4,2,8,128]{3,2,1,0:T(8,128)S(1)}, f32[4,2,8,128]{3,2,1,0:T(8,128)S(1)}, u32[]{:S(2)}, u32[]{:S(2)}) collective-permute-start(f32[4,2,8,128]{3,2,1,0:T(8,128)S(1)} %get-tuple-element.46), channel_id=1, source_target_pairs={{0,8},{8,16},{16,24},{24,0},{1,9},{9,17},{17,25},{25,1},{2,10},{10... | collective-permute-start | bytes 98312 | tf_op jit(solution)/shard_map/ppermute | solution.py:371
  4.5 12.9 %copy-start.1 = (bf16[32,3,1,512]{3,0,2,1:T(8,128)(2,1)S(1)}, bf16[32,3,1,512]{3,0,2,1:T(8,128)(2,1)}, u32[]{:S(2)}) copy-start(bf16[32,3,1,512]{3,0,2,1:T(8,128)(2,1)} %param.8) | copy-start | bytes 294916
  4.5 4.3 %collective-permute-start.1 = (f32[4,2,8,128]{3,2,1,0:T(8,128)S(1)}, f32[4,2,8,128]{3,2,1,0:T(8,128)S(1)}, u32[]{:S(2)}, u32[]{:S(2)}) collective-permute-start(f32[4,2,8,128]{3,2,1,0:T(8,128)S(1)} %get-tuple-element.47), channel_id=1, source_target_pairs={{0,24},{8,0},{16,8},{24,16},{1,25},{9,1},{17,9},{25,17},{2,26},{10... | collective-permute-start | bytes 98312 | tf_op jit(solution)/shard_map/ppermute | solution.py:371
  8.8 8.7 %copy-start = (s32[4]{0:T(128)S(1)}, s32[4]{0:T(128)}, u32[]{:S(2)}) copy-start(s32[4]{0:T(128)} %refs_7_.1) | copy-start | bytes 52
  8.8 6.0 %collective-permute-start.3 = (f32[232,128]{1,0:T(8,128)S(1)}, f32[232,128]{1,0:T(8,128)S(1)}, u32[]{:S(2)}, u32[]{:S(2)}) collective-permute-start(f32[232,128]{1,0:T(8,128)S(1)} %shard_map.76.refs_0_), channel_id=1, source_target_pairs={{0,2},{1,3},{2,4},{3,5},{4,6},{5,7},{6,0},{7,1},{8,10},{9,11},{10,... | collective-permute-start | bytes 356360 | tf_op jit(solution)/shard_map/ppermute | solution.py:371
  10.4 5.8 %collective-permute-start.2 = (f32[232,128]{1,0:T(8,128)S(1)}, f32[232,128]{1,0:T(8,128)S(1)}, u32[]{:S(2)}, u32[]{:S(2)}) collective-permute-start(f32[232,128]{1,0:T(8,128)S(1)} %shard_map.76.refs_0_), channel_id=1, source_target_pairs={{0,6},{1,7},{2,0},{3,1},{4,2},{5,3},{6,4},{7,5},{8,14},{9,15},{10,... | collective-permute-start | bytes 356360 | tf_op jit(solution)/shard_map/ppermute | solution.py:371
  11.8 5.5 %collective-permute-start.5 = (f32[232,128]{1,0:T(8,128)S(1)}, f32[232,128]{1,0:T(8,128)S(1)}, u32[]{:S(2)}, u32[]{:S(2)}) collective-permute-start(f32[232,128]{1,0:T(8,128)S(1)} %shard_map.76.refs_0_), channel_id=1, source_target_pairs={{0,5},{1,4},{2,7},{3,6},{4,1},{5,0},{6,3},{7,2},{8,13},{9,12},{10,... | collective-permute-start | bytes 356360 | tf_op jit(solution)/shard_map/ppermute | solution.py:371
  11.8 5.5 %collective-permute-start.4 = (f32[232,128]{1,0:T(8,128)S(1)}, f32[232,128]{1,0:T(8,128)S(1)}, u32[]{:S(2)}, u32[]{:S(2)}) collective-permute-start(f32[232,128]{1,0:T(8,128)S(1)} %shard_map.76.refs_0_), channel_id=1, source_target_pairs={{0,1},{1,0},{2,3},{3,2},{4,5},{5,4},{6,7},{7,6},{8,9},{9,8},{10,11... | collective-permute-start | bytes 356360 | tf_op jit(solution)/shard_map/ppermute | solution.py:371
  14.8 2.5 %collective-permute-start.7 = (f32[232,128]{1,0:T(8,128)S(1)}, f32[232,128]{1,0:T(8,128)S(1)}, u32[]{:S(2)}, u32[]{:S(2)}) collective-permute-start(f32[232,128]{1,0:T(8,128)S(1)} %collective-permute-done.3.refs_2_), channel_id=1, source_target_pairs={{0,1},{1,0},{2,3},{3,2},{4,5},{5,4},{6,7},{7,6},{8,9},{9,8},{10,11... | collective-permute-start | bytes 356360 | tf_op jit(solution)/shard_map/ppermute | solution.py:371
  16.1 1.3 %collective-permute-start.6 = (f32[232,128]{1,0:T(8,128)S(1)}, f32[232,128]{1,0:T(8,128)S(1)}, u32[]{:S(2)}, u32[]{:S(2)}) collective-permute-start(f32[232,128]{1,0:T(8,128)S(1)} %collective-permute-done.2.refs_1_), channel_id=1, source_target_pairs={{0,1},{1,0},{2,3},{3,2},{4,5},{5,4},{6,7},{7,6},{8,9},{9,8},{10,11... | collective-permute-start | bytes 356360 | tf_op jit(solution)/shard_map/ppermute | solution.py:371

commit v10 on v7

--- a/solution.py
+++ b/solution.py
@@ -21,7 +21,6 @@
 SUB = 8
 LANES = 128
 HALO = 6
-AT_ONCE = 2
 OFFSETS = [(0, 0), (2, 2), (-2, -2), (1, -1), (-3, 3), (3, 1), (-1, -3)]
 HIGHEST = lax.Precision.HIGHEST
 NT = (((1,), (1,)), ((), ()))
@@ -87,6 +86,14 @@
     return dens, mom
 
 
+def straight(src, x, tiles, skip):
+    def get(i, t):
+        tile = src[i, x - DIR_X[i], pl.ds(skip + t - DIR_Y[i], SUB, stride=tiles), :]
+        return pltpu.roll(tile, DIR_Z[i] % LANES, 1) if DIR_Z[i] else tile
+
+    return get
+
+
 def reciprocal(value):
     near = pl.reciprocal(value, approx=True)
     near = near * (2.0 - value * near)
@@ -132,8 +139,9 @@
 
 
 def lattice_kernel(*refs):
-    blocks, refs = refs[:-15], refs[-15:]
-    snap_steps, basis, pops, snaps, sums, ping, pong, speeds, views, coarse, rowwise, gram, whole, at_steps, sems = refs
+    blocks, refs = refs[:-16], refs[-16:]
+    snap_steps, basis, pops, snaps, sums, ping, pong, ordered, speeds, views = refs[:10]
+    coarse, rowwise, gram, whole, at_steps, sems = refs[10:]
     planes, rows, lanes = pops.shape[1:]
     tiles = ping.shape[2]
     reach = STEPS
@@ -145,18 +153,18 @@
     odd = lax.rem(lax.axis_index("dev"), 2)
     place = [reach + planes * (even_at + odd * (odd_at - even_at)) for even_at, odd_at in OFFSETS]
 
-    def put_speed(x, held):
-        for c in range(3):
-            for half in range(2):
-                speeds[x, c, half] = held[2 * half][c] + held[2 * half + 1][c]
+    def put_speed(p, row, held):
+        for t, speed in enumerate(held):
+            for c in range(3):
+                speeds[p, c, pl.ds(row + t, SUB, stride=len(held)), :] = speed[c]
 
     def keep_view(step):
         for c in range(3):
             for half in range(2):
-                total = speeds[reach, c, half]
-                for p in range(1, planes):
-                    total = total + speeds[reach + p, c, half]
-                views[step, c, half] = total
+                at = HALO + 2 * half
+                views[step, c, half] = tree_sum(
+                    [speeds[p, c, pl.ds(at + m, SUB, stride=4), :] for p in range(planes) for m in range(2)]
+                )
 
     for n, block in enumerate(blocks):
         for p in range(planes):
@@ -170,41 +178,42 @@
                 for i in range(DIRS):
                     ping[i, x, t] = out[i]
                 held.append(speed)
-            put_speed(x, held)
+            if n == 0:
+                put_speed(p, 0, held)
     keep_view(0)
 
+    few, skip = tiles - 1, (high - SUB * (tiles - 1)) // 2
     src, dst = ping, pong
     for step in range(1, STEPS):
-        size = span - 2 * step
-        together = math.gcd(size, AT_ONCE)
-
-        def later(n, carry, src=src, dst=dst, step=step, together=together):
-            for x in [step + together * n + m for m in range(together)]:
-                get = streamed(src, x, tiles)
-                held = []
-                for t in range(tiles):
-                    pop = [get(i, t) for i in range(DIRS)]
-                    dens, mom = moments(pop)
-                    inverse = 1.5 * reciprocal(dens)
-                    speed = [m * inverse for m in mom]
-                    flow = [m * (RATE * 3.0 / 36.0) for m in mom]
-                    out = relaxed(RATE, dens, flow, speed, pop)
-                    for i in range(DIRS):
+        wide = step < 2
+        for x in range(step, span - step):
+            get = straight(ordered, x, few, skip) if step == 2 else streamed(src, x, tiles if wide else few)
+            held = []
+            for t in range(tiles if wide else few):
+                pop = [get(i, t) for i in range(DIRS)]
+                dens, mom = moments(pop)
+                inverse = 1.5 * reciprocal(dens)
+                speed = [m * inverse for m in mom]
+                flow = [m * (RATE * 3.0 / 36.0) for m in mom]
+                out = relaxed(RATE, dens, flow, speed, pop)
+                for i in range(DIRS):
+                    if wide:
+                        ordered[i, x, pl.ds(t, SUB, stride=tiles), :] = out[i]
+                    else:
                         dst[i, x, t] = out[i]
-                    held.append(speed)
-                put_speed(x, held)
-            return carry
-
-        lax.fori_loop(0, size // together, later, 0)
+                held.append(speed)
+            if reach <= x < reach + planes:
+                put_speed(x - reach, 0 if wide else skip, held)
         keep_view(step)
         src, dst = dst, src
 
     copies = []
     for p in range(planes):
-        get = streamed(src, reach + p, tiles)
+        get = streamed(src, reach + p, few)
         for i in range(DIRS):
-            for t in range(tiles):
-                whole[p, i, pl.ds(SUB - HALO + t, SUB, stride=tiles), :] = KEEP ** (STEPS - 1) * get(i, t)
+            for t in range(few):
+                at = pl.ds(SUB - HALO + skip + t, SUB, stride=few)
+                whole[p, i, at, :] = KEEP ** (STEPS - 1) * get(i, t)
         copies.append(pltpu.make_async_copy(whole.at[p, :, pl.ds(SUB, rows), :], pops.at[:, p], sems.at[p]))
         copies[-1].start()
 
@@ -212,13 +221,9 @@
     lane = lax.broadcasted_iota(jnp.int32, (lanes, lanes), 0) // 2
     col = lax.broadcasted_iota(jnp.int32, (lanes, lanes), 1)
     flat = None
-    start_half, start_sub = HALO // 2 % 2, HALO // 2 // 2
     for half in range(2):
-        right = half != start_half
         stack = [views[at_steps[k], c, half] for k in range(count) for c in range(3)]
-        if right and start_half == 1:
-            stack = [pltpu.roll(view, SUB - 1, 0) for view in stack]
-        gather = jnp.where(lane + (lanes // 2 if right else 0) == col, 1.0, 0.0).astype(jnp.bfloat16)
+        gather = jnp.where(lane + half * (lanes // 2) == col, 1.0, 0.0).astype(jnp.bfloat16)
         for part in split3(jnp.concatenate(stack, axis=0)):
             term = jnp.dot(part.astype(jnp.bfloat16), gather, preferred_element_type=jnp.float32)
             flat = term if flat is None else flat + term
@@ -229,7 +234,7 @@
     groups = rows // tiles
     total = None
     for c in range(3):
-        parts = [coarse[pl.ds(SUB * c + start_sub + t, SUB, stride=3 * SUB), :] for t in range(groups)]
+        parts = [coarse[pl.ds(SUB * c + t, SUB, stride=3 * SUB), :] for t in range(groups)]
         snap = jnp.concatenate(parts, axis=1)
         snaps[c] = snap
         a, b, d = split3(snap)
@@ -463,7 +468,8 @@
         scratch_shapes=[
             pltpu.VMEM((DIRS, span, tiles, SUB, lanes), f32),
             pltpu.VMEM((DIRS, span, tiles, SUB, lanes), f32),
-            pltpu.VMEM((span, 3, 2, SUB, lanes), f32),
+            pltpu.VMEM((DIRS, span, SUB * tiles, lanes), f32),
+            pltpu.VMEM((planes, 3, SUB * (tiles + 1), lanes), f32),
             pltpu.VMEM((STEPS, 3, 2, SUB, lanes), f32),
             pltpu.VMEM((3 * SUB * SUB, lanes), f32),
             pltpu.VMEM((rank + 4 * SUB, width), jnp.bfloat16),

time: 39.7 us -> 37.4 us (0.942)
  Pallas kernels: 8.16 us -> 5.82 us
    pallas_call x1, Pallas kernels: 6.8 us -> 4.46 us  [per_device(): pl.pallas_call(lattice_kernel, out_shape=(jax.ShapeDtypeStruct((DIRS, pla...]
where the time goes in v10:
time: 37.4 us; the launch traced here: 37.2 us
  blocking collectives  13.3 us (36%)
  starting transfers between devices  9.79 us (26%)
  waiting for transfers between devices  6.19 us (17%)
  Pallas kernels  5.82 us (16%)
  other arithmetic  0.81 us (2%)
  between operations  0.66 us (2%)
  loops' own time  0.57 us (2%)
    all_to_all x1, blocking collectives, per_device(): parts = [lax.all_to_all(sums, ('group', 'dev'), 0, 0)]  13.3 us
    ppermute x8, starting transfers between devices, moved(): lax.ppermute(block, axis, [(i, target(i)) for i in range(lax.axis_size(ax...  9.79 us
    ppermute x8, waiting for transfers between devices, moved(): lax.ppermute(block, axis, [(i, target(i)) for i in range(lax.axis_size(ax...  6.19 us
    pallas_call x1, Pallas kernels, per_device(): pl.pallas_call(lattice_kernel, out_shape=(jax.ShapeDtypeStruct((DIRS, pla...  4.46 us
    pallas_call x1, Pallas kernels, per_device(): pl.pallas_call(functools.partial(finish_kernel, scale, count, rank), out_...  1.34 us
    concatenate x1, other arithmetic, per_device(): held = jnp.concatenate([density[None], velocity])  0.81 us
  transfers between devices with their start and end apart: 8, of which 6 were waited for; matrix products, arithmetic and copies ran while one was open for 0% of the time, Pallas kernels for 0%

profile of v10, /device:TPU:0, one launch (start us, length us, event | category | flops | bytes accessed | tf_op | source)
XLA Modules:
  0.0 37.2 jit_solution(4841537324328311196)
XLA Ops:
  0.6 0.8 %pad_maximum_fusion.held = f32[4,2,16,128]{3,2,1,0:T(8,128)S(1)} fusion(f32[3,2,16,128]{3,2,1,0:T(8,128)} %param.7, f32[1,2,16,128]{3,2,1,0:T(8,128)} %bitcast.10), kind=kLoop, calls=%fused_computation | loop fusion | flops 16384 | bytes 131072 | tf_op jit(solution)/shard_map/concatenate | solution.py:437
  1.4 3.1 %collective-permute-start = (f32[4,2,8,128]{3,2,1,0:T(8,128)S(1)}, f32[4,2,8,128]{3,2,1,0:T(8,128)S(1)}, u32[]{:S(2)}, u32[]{:S(2)}) collective-permute-start(f32[4,2,8,128]{3,2,1,0:T(8,128)S(1)} %get-tuple-element.46), channel_id=1, source_target_pairs={{0,8},{8,16},{16,24},{24,0},{1,9},{9,17},{17,25},{25,1},{2,10},{10... | collective-permute-start | bytes 98312 | tf_op jit(solution)/shard_map/ppermute | solution.py:373
  4.5 0.0 copy-start.1
  4.5 2.1 %collective-permute-start.1 = (f32[4,2,8,128]{3,2,1,0:T(8,128)S(1)}, f32[4,2,8,128]{3,2,1,0:T(8,128)S(1)}, u32[]{:S(2)}, u32[]{:S(2)}) collective-permute-start(f32[4,2,8,128]{3,2,1,0:T(8,128)S(1)} %get-tuple-element.47), channel_id=1, source_target_pairs={{0,24},{8,0},{16,8},{24,16},{1,25},{9,1},{17,9},{25,17},{2,26},{10... | collective-permute-start | bytes 98312 | tf_op jit(solution)/shard_map/ppermute | solution.py:373
  6.6 1.9 %collective-permute-done.upper = f32[4,2,8,128]{3,2,1,0:T(8,128)S(1)} collective-permute-done((f32[4,2,8,128]{3,2,1,0:T(8,128)S(1)}, f32[4,2,8,128]{3,2,1,0:T(8,128)S(1)}, u32[]{:S(2)}, u32[]{:S(2)}) %collective-permute-start) | collective-permute-done | bytes 32800 | tf_op jit(solution)/shard_map/ppermute | solution.py:373
  8.6 0.2 collective-permute-done.1.lower
  8.8 0.0 copy-start
  8.8 1.5 %collective-permute-start.3 = (f32[232,128]{1,0:T(8,128)S(1)}, f32[232,128]{1,0:T(8,128)S(1)}, u32[]{:S(2)}, u32[]{:S(2)}) collective-permute-start(f32[232,128]{1,0:T(8,128)S(1)} %shard_map.76.refs_0_), channel_id=1, source_target_pairs={{0,2},{1,3},{2,4},{3,5},{4,6},{5,7},{6,0},{7,1},{8,10},{9,11},{10,... | collective-permute-start | bytes 356360 | tf_op jit(solution)/shard_map/ppermute | solution.py:373
  10.4 1.4 %collective-permute-start.2 = (f32[232,128]{1,0:T(8,128)S(1)}, f32[232,128]{1,0:T(8,128)S(1)}, u32[]{:S(2)}, u32[]{:S(2)}) collective-permute-start(f32[232,128]{1,0:T(8,128)S(1)} %shard_map.76.refs_0_), channel_id=1, source_target_pairs={{0,6},{1,7},{2,0},{3,1},{4,2},{5,3},{6,4},{7,5},{8,14},{9,15},{10,... | collective-permute-start | bytes 356360 | tf_op jit(solution)/shard_map/ppermute | solution.py:373
  11.8 0.0 collective-permute-start.5
  11.8 1.6 %collective-permute-start.4 = (f32[232,128]{1,0:T(8,128)S(1)}, f32[232,128]{1,0:T(8,128)S(1)}, u32[]{:S(2)}, u32[]{:S(2)}) collective-permute-start(f32[232,128]{1,0:T(8,128)S(1)} %shard_map.76.refs_0_), channel_id=1, source_target_pairs={{0,1},{1,0},{2,3},{3,2},{4,5},{5,4},{6,7},{7,6},{8,9},{9,8},{10,11... | collective-permute-start | bytes 356360 | tf_op jit(solution)/shard_map/ppermute | solution.py:373
  13.4 1.4 %collective-permute-done.3.refs_2_ = f32[232,128]{1,0:T(8,128)S(1)} collective-permute-done((f32[232,128]{1,0:T(8,128)S(1)}, f32[232,128]{1,0:T(8,128)S(1)}, u32[]{:S(2)}, u32[]{:S(2)}) %collective-permute-start.3) | collective-permute-done | bytes 118816 | tf_op jit(solution)/shard_map/ppermute | solution.py:373
  14.8 0.0 collective-permute-start.7
  14.8 1.3 %collective-permute-done.2.refs_1_ = f32[232,128]{1,0:T(8,128)S(1)} collective-permute-done((f32[232,128]{1,0:T(8,128)S(1)}, f32[232,128]{1,0:T(8,128)S(1)}, u32[]{:S(2)}, u32[]{:S(2)}) %collective-permute-start.2) | collective-permute-done | bytes 118816 | tf_op jit(solution)/shard_map/ppermute | solution.py:373
  16.1 0.0 collective-permute-start.6
  16.1 1.2 %collective-permute-done.5.refs_4_ = f32[232,128]{1,0:T(8,128)S(1)} collective-permute-done((f32[232,128]{1,0:T(8,128)S(1)}, f32[232,128]{1,0:T(8,128)S(1)}, u32[]{:S(2)}, u32[]{:S(2)}) %collective-permute-start.5) | collective-permute-done | bytes 118816 | tf_op jit(solution)/shard_map/ppermute | solution.py:373
  17.3 0.0 collective-permute-done.4.refs_3_
  17.3 0.0 collective-permute-done.7.refs_6_
  17.3 0.2 collective-permute-done.6.refs_5_
  17.5 0.0 copy-done.1
  17.5 0.0 copy-done
  17.5 4.5 %shard_map.77 = (f32[19,2,16,128]{3,2,1,0:T(8,128)}, f32[3,8,512]{2,1,0:T(8,128)S(1)}, f32[32,8,128]{2,1,0:T(8,128)S(1)}) custom-call(f32[232,128]{1,0:T(8,128)S(1)} %shard_map.76.refs_0_, f32[232,128]{1,0:T(8,128)S(1)} %collective-permute-done.2.refs_1_, f32[232,128]{1,0:T(8,128)S(1)} %collective-permute-done.3.refs_2_, ...), custom_call_target="tpu_custom_call" | custom-call | tf_op jit(solution)/shard_map/pallas_call | solution.py:459
  21.9 13.3 %all_to_all.5.refs_0_ = f32[32,8,128]{2,1,0:T(8,128)S(1)} all-to-all(f32[32,8,128]{2,1,0:T(8,128)S(1)} %get-tuple-element.49), channel_id=1, replica_groups=mesh['group'=4,'dev'=8] {'group','dev'}, dimensions={0} | all-to-all | bytes 262144 | tf_op jit(solution)/shard_map/all_to_all | solution.py:485
  35.2 1.3 %shard_map.78 = (f32[4,32]{1,0:T(4,128)}, f32[4,4]{1,0:T(4,128)}, f32[48,128]{1,0:T(8,128)}, s32[1,1]{1,0:T(1,128)}, f32[8,32]{1,0:T(8,128)S(1)}) custom-call(f32[32,8,128]{2,1,0:T(8,128)S(1)} %all_to_all.5.refs_0_, f32[3,8,512]{2,1,0:T(8,128)S(1)} %get-tuple-element.80.refs_1_, bf16[3,32,512]{2,1,0:T(8,128)(2,1)S(1)} %bitcast.8), custom_call_target="tpu_custom_call" | custom-call | tf_op jit(solution)/shard_map/pallas_call | solution.py:493
  36.6 0.6 %while.11 = (s32[]{:T(128)}, f32[4,4]{1,0:T(4,128)}, f32[48,128]{1,0:T(8,128)}, f32[8,32]{1,0:T(8,128)S(1)}, f32[3,8,512]{2,1,0:T(8,128)S(1)}, /*index=5*/bf16[3,32,512]{2,1,0:T(8,128)(2,1)S(1)}) while((s32[]{:T(128)}, f32[4,4]{1,0:T(4,128)}, f32[48,128]{1,0:T(8,128)}, f32[8,32]{1,0:T(8,128)S(1)}, f32[3,8,512]{2,1,0:T(8,128)S(1)}, ...), condition=%region_2.0_spmd, body=%region_0.0_spmd | while | flops 65 | bytes 577 | solution.py:520
  (2 shorter events, 0.0 us)
Async XLA Ops:
  1.4 7.1 %collective-permute-start = (f32[4,2,8,128]{3,2,1,0:T(8,128)S(1)}, f32[4,2,8,128]{3,2,1,0:T(8,128)S(1)}, u32[]{:S(2)}, u32[]{:S(2)}) collective-permute-start(f32[4,2,8,128]{3,2,1,0:T(8,128)S(1)} %get-tuple-element.46), channel_id=1, source_target_pairs={{0,8},{8,16},{16,24},{24,0},{1,9},{9,17},{17,25},{25,1},{2,10},{10... | collective-permute-start | bytes 98312 | tf_op jit(solution)/shard_map/ppermute | solution.py:373
  4.5 12.9 %copy-start.1 = (bf16[32,3,1,512]{3,0,2,1:T(8,128)(2,1)S(1)}, bf16[32,3,1,512]{3,0,2,1:T(8,128)(2,1)}, u32[]{:S(2)}) copy-start(bf16[32,3,1,512]{3,0,2,1:T(8,128)(2,1)} %param.8) | copy-start | bytes 294916
  4.5 4.3 %collective-permute-start.1 = (f32[4,2,8,128]{3,2,1,0:T(8,128)S(1)}, f32[4,2,8,128]{3,2,1,0:T(8,128)S(1)}, u32[]{:S(2)}, u32[]{:S(2)}) collective-permute-start(f32[4,2,8,128]{3,2,1,0:T(8,128)S(1)} %get-tuple-element.47), channel_id=1, source_target_pairs={{0,24},{8,0},{16,8},{24,16},{1,25},{9,1},{17,9},{25,17},{2,26},{10... | collective-permute-start | bytes 98312 | tf_op jit(solution)/shard_map/ppermute | solution.py:373
  8.8 8.7 %copy-start = (s32[4]{0:T(128)S(1)}, s32[4]{0:T(128)}, u32[]{:S(2)}) copy-start(s32[4]{0:T(128)} %refs_7_.1) | copy-start | bytes 52
  8.8 6.0 %collective-permute-start.3 = (f32[232,128]{1,0:T(8,128)S(1)}, f32[232,128]{1,0:T(8,128)S(1)}, u32[]{:S(2)}, u32[]{:S(2)}) collective-permute-start(f32[232,128]{1,0:T(8,128)S(1)} %shard_map.76.refs_0_), channel_id=1, source_target_pairs={{0,2},{1,3},{2,4},{3,5},{4,6},{5,7},{6,0},{7,1},{8,10},{9,11},{10,... | collective-permute-start | bytes 356360 | tf_op jit(solution)/shard_map/ppermute | solution.py:373
  10.4 5.8 %collective-permute-start.2 = (f32[232,128]{1,0:T(8,128)S(1)}, f32[232,128]{1,0:T(8,128)S(1)}, u32[]{:S(2)}, u32[]{:S(2)}) collective-permute-start(f32[232,128]{1,0:T(8,128)S(1)} %shard_map.76.refs_0_), channel_id=1, source_target_pairs={{0,6},{1,7},{2,0},{3,1},{4,2},{5,3},{6,4},{7,5},{8,14},{9,15},{10,... | collective-permute-start | bytes 356360 | tf_op jit(solution)/shard_map/ppermute | solution.py:373
  11.8 5.5 %collective-permute-start.5 = (f32[232,128]{1,0:T(8,128)S(1)}, f32[232,128]{1,0:T(8,128)S(1)}, u32[]{:S(2)}, u32[]{:S(2)}) collective-permute-start(f32[232,128]{1,0:T(8,128)S(1)} %shard_map.76.refs_0_), channel_id=1, source_target_pairs={{0,5},{1,4},{2,7},{3,6},{4,1},{5,0},{6,3},{7,2},{8,13},{9,12},{10,... | collective-permute-start | bytes 356360 | tf_op jit(solution)/shard_map/ppermute | solution.py:373
  11.8 5.5 %collective-permute-start.4 = (f32[232,128]{1,0:T(8,128)S(1)}, f32[232,128]{1,0:T(8,128)S(1)}, u32[]{:S(2)}, u32[]{:S(2)}) collective-permute-start(f32[232,128]{1,0:T(8,128)S(1)} %shard_map.76.refs_0_), channel_id=1, source_target_pairs={{0,1},{1,0},{2,3},{3,2},{4,5},{5,4},{6,7},{7,6},{8,9},{9,8},{10,11... | collective-permute-start | bytes 356360 | tf_op jit(solution)/shard_map/ppermute | solution.py:373
  14.8 2.5 %collective-permute-start.7 = (f32[232,128]{1,0:T(8,128)S(1)}, f32[232,128]{1,0:T(8,128)S(1)}, u32[]{:S(2)}, u32[]{:S(2)}) collective-permute-start(f32[232,128]{1,0:T(8,128)S(1)} %collective-permute-done.3.refs_2_), channel_id=1, source_target_pairs={{0,1},{1,0},{2,3},{3,2},{4,5},{5,4},{6,7},{7,6},{8,9},{9,8},{10,11... | collective-permute-start | bytes 356360 | tf_op jit(solution)/shard_map/ppermute | solution.py:373
  16.1 1.3 %collective-permute-start.6 = (f32[232,128]{1,0:T(8,128)S(1)}, f32[232,128]{1,0:T(8,128)S(1)}, u32[]{:S(2)}, u32[]{:S(2)}) collective-permute-start(f32[232,128]{1,0:T(8,128)S(1)} %collective-permute-done.2.refs_1_), channel_id=1, source_target_pairs={{0,1},{1,0},{2,3},{3,2},{4,5},{5,4},{6,7},{7,6},{8,9},{9,8},{10,11... | collective-permute-start | bytes 356360 | tf_op jit(solution)/shard_map/ppermute | solution.py:373

commit v11 on v10

--- a/solution.py
+++ b/solution.py
@@ -196,7 +196,10 @@
                 speed = [m * inverse for m in mom]
                 flow = [m * (RATE * 3.0 / 36.0) for m in mom]
                 out = relaxed(RATE, dens, flow, speed, pop)
+                inwards = {step: 1, span - 1 - step: -1}.get(x)
                 for i in range(DIRS):
+                    if inwards is not None and DIR_X[i] != inwards:
+                        continue
                     if wide:
                         ordered[i, x, pl.ds(t, SUB, stride=tiles), :] = out[i]
                     else:

time: 37.4 us -> 37.3 us (level)
  no operation moved by 1% of the time
where the time goes in v11:
time: 37.3 us; the launch traced here: 37.1 us
  blocking collectives  13.3 us (36%)
  starting transfers between devices  9.79 us (26%)
  waiting for transfers between devices  6.19 us (17%)
  Pallas kernels  5.72 us (15%)
  other arithmetic  0.81 us (2%)
  between operations  0.66 us (2%)
  loops' own time  0.57 us (2%)
    all_to_all x1, blocking collectives, per_device(): parts = [lax.all_to_all(sums, ('group', 'dev'), 0, 0)]  13.3 us
    ppermute x8, starting transfers between devices, moved(): lax.ppermute(block, axis, [(i, target(i)) for i in range(lax.axis_size(ax...  9.79 us
    ppermute x8, waiting for transfers between devices, moved(): lax.ppermute(block, axis, [(i, target(i)) for i in range(lax.axis_size(ax...  6.19 us
    pallas_call x1, Pallas kernels, per_device(): pl.pallas_call(lattice_kernel, out_shape=(jax.ShapeDtypeStruct((DIRS, pla...  4.36 us
    pallas_call x1, Pallas kernels, per_device(): pl.pallas_call(functools.partial(finish_kernel, scale, count, rank), out_...  1.34 us
    concatenate x1, other arithmetic, per_device(): held = jnp.concatenate([density[None], velocity])  0.81 us
  transfers between devices with their start and end apart: 8, of which 6 were waited for; matrix products, arithmetic and copies ran while one was open for 0% of the time, Pallas kernels for 0%

profile of v11, /device:TPU:0, one launch (start us, length us, event | category | flops | bytes accessed | tf_op | source)
XLA Modules:
  0.0 37.1 jit_solution(589901837783080072)
XLA Ops:
  0.6 0.8 %pad_maximum_fusion.held = f32[4,2,16,128]{3,2,1,0:T(8,128)S(1)} fusion(f32[3,2,16,128]{3,2,1,0:T(8,128)} %param.7, f32[1,2,16,128]{3,2,1,0:T(8,128)} %bitcast.10), kind=kLoop, calls=%fused_computation | loop fusion | flops 16384 | bytes 131072 | tf_op jit(solution)/shard_map/concatenate | solution.py:440
  1.4 3.1 %collective-permute-start = (f32[4,2,8,128]{3,2,1,0:T(8,128)S(1)}, f32[4,2,8,128]{3,2,1,0:T(8,128)S(1)}, u32[]{:S(2)}, u32[]{:S(2)}) collective-permute-start(f32[4,2,8,128]{3,2,1,0:T(8,128)S(1)} %get-tuple-element.46), channel_id=1, source_target_pairs={{0,8},{8,16},{16,24},{24,0},{1,9},{9,17},{17,25},{25,1},{2,10},{10... | collective-permute-start | bytes 98312 | tf_op jit(solution)/shard_map/ppermute | solution.py:376
  4.5 0.0 copy-start.1
  4.5 2.1 %collective-permute-start.1 = (f32[4,2,8,128]{3,2,1,0:T(8,128)S(1)}, f32[4,2,8,128]{3,2,1,0:T(8,128)S(1)}, u32[]{:S(2)}, u32[]{:S(2)}) collective-permute-start(f32[4,2,8,128]{3,2,1,0:T(8,128)S(1)} %get-tuple-element.47), channel_id=1, source_target_pairs={{0,24},{8,0},{16,8},{24,16},{1,25},{9,1},{17,9},{25,17},{2,26},{10... | collective-permute-start | bytes 98312 | tf_op jit(solution)/shard_map/ppermute | solution.py:376
  6.6 1.9 %collective-permute-done.upper = f32[4,2,8,128]{3,2,1,0:T(8,128)S(1)} collective-permute-done((f32[4,2,8,128]{3,2,1,0:T(8,128)S(1)}, f32[4,2,8,128]{3,2,1,0:T(8,128)S(1)}, u32[]{:S(2)}, u32[]{:S(2)}) %collective-permute-start) | collective-permute-done | bytes 32800 | tf_op jit(solution)/shard_map/ppermute | solution.py:376
  8.6 0.2 collective-permute-done.1.lower
  8.8 0.0 copy-start
  8.8 1.5 %collective-permute-start.3 = (f32[232,128]{1,0:T(8,128)S(1)}, f32[232,128]{1,0:T(8,128)S(1)}, u32[]{:S(2)}, u32[]{:S(2)}) collective-permute-start(f32[232,128]{1,0:T(8,128)S(1)} %shard_map.76.refs_0_), channel_id=1, source_target_pairs={{0,2},{1,3},{2,4},{3,5},{4,6},{5,7},{6,0},{7,1},{8,10},{9,11},{10,... | collective-permute-start | bytes 356360 | tf_op jit(solution)/shard_map/ppermute | solution.py:376
  10.4 1.4 %collective-permute-start.2 = (f32[232,128]{1,0:T(8,128)S(1)}, f32[232,128]{1,0:T(8,128)S(1)}, u32[]{:S(2)}, u32[]{:S(2)}) collective-permute-start(f32[232,128]{1,0:T(8,128)S(1)} %shard_map.76.refs_0_), channel_id=1, source_target_pairs={{0,6},{1,7},{2,0},{3,1},{4,2},{5,3},{6,4},{7,5},{8,14},{9,15},{10,... | collective-permute-start | bytes 356360 | tf_op jit(solution)/shard_map/ppermute | solution.py:376
  11.8 0.0 collective-permute-start.5
  11.8 1.6 %collective-permute-start.4 = (f32[232,128]{1,0:T(8,128)S(1)}, f32[232,128]{1,0:T(8,128)S(1)}, u32[]{:S(2)}, u32[]{:S(2)}) collective-permute-start(f32[232,128]{1,0:T(8,128)S(1)} %shard_map.76.refs_0_), channel_id=1, source_target_pairs={{0,1},{1,0},{2,3},{3,2},{4,5},{5,4},{6,7},{7,6},{8,9},{9,8},{10,11... | collective-permute-start | bytes 356360 | tf_op jit(solution)/shard_map/ppermute | solution.py:376
  13.4 1.4 %collective-permute-done.3.refs_2_ = f32[232,128]{1,0:T(8,128)S(1)} collective-permute-done((f32[232,128]{1,0:T(8,128)S(1)}, f32[232,128]{1,0:T(8,128)S(1)}, u32[]{:S(2)}, u32[]{:S(2)}) %collective-permute-start.3) | collective-permute-done | bytes 118816 | tf_op jit(solution)/shard_map/ppermute | solution.py:376
  14.8 0.0 collective-permute-start.7
  14.8 1.3 %collective-permute-done.2.refs_1_ = f32[232,128]{1,0:T(8,128)S(1)} collective-permute-done((f32[232,128]{1,0:T(8,128)S(1)}, f32[232,128]{1,0:T(8,128)S(1)}, u32[]{:S(2)}, u32[]{:S(2)}) %collective-permute-start.2) | collective-permute-done | bytes 118816 | tf_op jit(solution)/shard_map/ppermute | solution.py:376
  16.1 0.0 collective-permute-start.6
  16.1 1.2 %collective-permute-done.5.refs_4_ = f32[232,128]{1,0:T(8,128)S(1)} collective-permute-done((f32[232,128]{1,0:T(8,128)S(1)}, f32[232,128]{1,0:T(8,128)S(1)}, u32[]{:S(2)}, u32[]{:S(2)}) %collective-permute-start.5) | collective-permute-done | bytes 118816 | tf_op jit(solution)/shard_map/ppermute | solution.py:376
  17.3 0.0 collective-permute-done.4.refs_3_
  17.3 0.0 collective-permute-done.7.refs_6_
  17.3 0.2 collective-permute-done.6.refs_5_
  17.5 0.0 copy-done.1
  17.5 0.0 copy-done
  17.5 4.4 %shard_map.77 = (f32[19,2,16,128]{3,2,1,0:T(8,128)}, f32[3,8,512]{2,1,0:T(8,128)S(1)}, f32[32,8,128]{2,1,0:T(8,128)S(1)}) custom-call(f32[232,128]{1,0:T(8,128)S(1)} %shard_map.76.refs_0_, f32[232,128]{1,0:T(8,128)S(1)} %collective-permute-done.2.refs_1_, f32[232,128]{1,0:T(8,128)S(1)} %collective-permute-done.3.refs_2_, ...), custom_call_target="tpu_custom_call" | custom-call | tf_op jit(solution)/shard_map/pallas_call | solution.py:462
  21.8 13.3 %all_to_all.5.refs_0_ = f32[32,8,128]{2,1,0:T(8,128)S(1)} all-to-all(f32[32,8,128]{2,1,0:T(8,128)S(1)} %get-tuple-element.49), channel_id=1, replica_groups=mesh['group'=4,'dev'=8] {'group','dev'}, dimensions={0} | all-to-all | bytes 262144 | tf_op jit(solution)/shard_map/all_to_all | solution.py:488
  35.1 1.3 %shard_map.78 = (f32[4,32]{1,0:T(4,128)}, f32[4,4]{1,0:T(4,128)}, f32[48,128]{1,0:T(8,128)}, s32[1,1]{1,0:T(1,128)}, f32[8,32]{1,0:T(8,128)S(1)}) custom-call(f32[32,8,128]{2,1,0:T(8,128)S(1)} %all_to_all.5.refs_0_, f32[3,8,512]{2,1,0:T(8,128)S(1)} %get-tuple-element.80.refs_1_, bf16[3,32,512]{2,1,0:T(8,128)(2,1)S(1)} %bitcast.8), custom_call_target="tpu_custom_call" | custom-call | tf_op jit(solution)/shard_map/pallas_call | solution.py:496
  36.5 0.6 %while.11 = (s32[]{:T(128)}, f32[4,4]{1,0:T(4,128)}, f32[48,128]{1,0:T(8,128)}, f32[8,32]{1,0:T(8,128)S(1)}, f32[3,8,512]{2,1,0:T(8,128)S(1)}, /*index=5*/bf16[3,32,512]{2,1,0:T(8,128)(2,1)S(1)}) while((s32[]{:T(128)}, f32[4,4]{1,0:T(4,128)}, f32[48,128]{1,0:T(8,128)}, f32[8,32]{1,0:T(8,128)S(1)}, f32[3,8,512]{2,1,0:T(8,128)S(1)}, ...), condition=%region_2.0_spmd, body=%region_0.0_spmd | while | flops 65 | bytes 577 | solution.py:523
  (2 shorter events, 0.0 us)
Async XLA Ops:
  1.4 7.1 %collective-permute-start = (f32[4,2,8,128]{3,2,1,0:T(8,128)S(1)}, f32[4,2,8,128]{3,2,1,0:T(8,128)S(1)}, u32[]{:S(2)}, u32[]{:S(2)}) collective-permute-start(f32[4,2,8,128]{3,2,1,0:T(8,128)S(1)} %get-tuple-element.46), channel_id=1, source_target_pairs={{0,8},{8,16},{16,24},{24,0},{1,9},{9,17},{17,25},{25,1},{2,10},{10... | collective-permute-start | bytes 98312 | tf_op jit(solution)/shard_map/ppermute | solution.py:376
  4.5 12.9 %copy-start.1 = (bf16[32,3,1,512]{3,0,2,1:T(8,128)(2,1)S(1)}, bf16[32,3,1,512]{3,0,2,1:T(8,128)(2,1)}, u32[]{:S(2)}) copy-start(bf16[32,3,1,512]{3,0,2,1:T(8,128)(2,1)} %param.8) | copy-start | bytes 294916
  4.5 4.3 %collective-permute-start.1 = (f32[4,2,8,128]{3,2,1,0:T(8,128)S(1)}, f32[4,2,8,128]{3,2,1,0:T(8,128)S(1)}, u32[]{:S(2)}, u32[]{:S(2)}) collective-permute-start(f32[4,2,8,128]{3,2,1,0:T(8,128)S(1)} %get-tuple-element.47), channel_id=1, source_target_pairs={{0,24},{8,0},{16,8},{24,16},{1,25},{9,1},{17,9},{25,17},{2,26},{10... | collective-permute-start | bytes 98312 | tf_op jit(solution)/shard_map/ppermute | solution.py:376
  8.8 8.7 %copy-start = (s32[4]{0:T(128)S(1)}, s32[4]{0:T(128)}, u32[]{:S(2)}) copy-start(s32[4]{0:T(128)} %refs_7_.1) | copy-start | bytes 52
  8.8 6.0 %collective-permute-start.3 = (f32[232,128]{1,0:T(8,128)S(1)}, f32[232,128]{1,0:T(8,128)S(1)}, u32[]{:S(2)}, u32[]{:S(2)}) collective-permute-start(f32[232,128]{1,0:T(8,128)S(1)} %shard_map.76.refs_0_), channel_id=1, source_target_pairs={{0,2},{1,3},{2,4},{3,5},{4,6},{5,7},{6,0},{7,1},{8,10},{9,11},{10,... | collective-permute-start | bytes 356360 | tf_op jit(solution)/shard_map/ppermute | solution.py:376
  10.4 5.8 %collective-permute-start.2 = (f32[232,128]{1,0:T(8,128)S(1)}, f32[232,128]{1,0:T(8,128)S(1)}, u32[]{:S(2)}, u32[]{:S(2)}) collective-permute-start(f32[232,128]{1,0:T(8,128)S(1)} %shard_map.76.refs_0_), channel_id=1, source_target_pairs={{0,6},{1,7},{2,0},{3,1},{4,2},{5,3},{6,4},{7,5},{8,14},{9,15},{10,... | collective-permute-start | bytes 356360 | tf_op jit(solution)/shard_map/ppermute | solution.py:376
  11.8 5.5 %collective-permute-start.5 = (f32[232,128]{1,0:T(8,128)S(1)}, f32[232,128]{1,0:T(8,128)S(1)}, u32[]{:S(2)}, u32[]{:S(2)}) collective-permute-start(f32[232,128]{1,0:T(8,128)S(1)} %shard_map.76.refs_0_), channel_id=1, source_target_pairs={{0,5},{1,4},{2,7},{3,6},{4,1},{5,0},{6,3},{7,2},{8,13},{9,12},{10,... | collective-permute-start | bytes 356360 | tf_op jit(solution)/shard_map/ppermute | solution.py:376
  11.8 5.5 %collective-permute-start.4 = (f32[232,128]{1,0:T(8,128)S(1)}, f32[232,128]{1,0:T(8,128)S(1)}, u32[]{:S(2)}, u32[]{:S(2)}) collective-permute-start(f32[232,128]{1,0:T(8,128)S(1)} %shard_map.76.refs_0_), channel_id=1, source_target_pairs={{0,1},{1,0},{2,3},{3,2},{4,5},{5,4},{6,7},{7,6},{8,9},{9,8},{10,11... | collective-permute-start | bytes 356360 | tf_op jit(solution)/shard_map/ppermute | solution.py:376
  14.8 2.5 %collective-permute-start.7 = (f32[232,128]{1,0:T(8,128)S(1)}, f32[232,128]{1,0:T(8,128)S(1)}, u32[]{:S(2)}, u32[]{:S(2)}) collective-permute-start(f32[232,128]{1,0:T(8,128)S(1)} %collective-permute-done.3.refs_2_), channel_id=1, source_target_pairs={{0,1},{1,0},{2,3},{3,2},{4,5},{5,4},{6,7},{7,6},{8,9},{9,8},{10,11... | collective-permute-start | bytes 356360 | tf_op jit(solution)/shard_map/ppermute | solution.py:376
  16.1 1.3 %collective-permute-start.6 = (f32[232,128]{1,0:T(8,128)S(1)}, f32[232,128]{1,0:T(8,128)S(1)}, u32[]{:S(2)}, u32[]{:S(2)}) collective-permute-start(f32[232,128]{1,0:T(8,128)S(1)} %collective-permute-done.2.refs_1_), channel_id=1, source_target_pairs={{0,1},{1,0},{2,3},{3,2},{4,5},{5,4},{6,7},{7,6},{8,9},{9,8},{10,11... | collective-permute-start | bytes 356360 | tf_op jit(solution)/shard_map/ppermute | solution.py:376
